TPU v7x, 128 devices: a whole 4x4x4 slice. The times are simulated.
128 devices in a mesh: ctx: 64 (over z, x_hi, y, core), fsdp: 2 (over x_lo).
Axes of the slice: x: 4 (x_hi: 2, x_lo: 2; x = x_hi * 2 + x_lo), y: 4, z: 4, core: 2. Of those that a mesh axis runs over, the one named last changes fastest.
Arguments:
- tokens: bfloat16 [16384, 768], P(('ctx', 'fsdp')), may hold values from -100 to 100
- block_order: int32 [128], replicated, may hold values from 0 to 127, each once
- cotangent: bfloat16 [16384, 768], P(('ctx', 'fsdp')), may hold values from -6 to 6
- ln_gain_attn: bfloat16 [768], P('fsdp'), may hold values from 0.099609375 to 1.8984375
- ln_bias_attn: bfloat16 [768], P('fsdp'), may hold values from -1.5 to 1.5
- ln_gain_mlp: bfloat16 [768], P('fsdp'), may hold values from 0.099609375 to 1.8984375
- ln_bias_mlp: bfloat16 [768], P('fsdp'), may hold values from -1.5 to 1.5
- w_qkv: bfloat16 [768, 2304], P('fsdp'), may hold values from -0.21875 to 0.21875
- b_qkv: bfloat16 [2304], P('fsdp'), may hold values from -1.5 to 1.5
- w_out: bfloat16 [768, 768], P('fsdp'), may hold values from -2.5 to 2.5
- b_out: bfloat16 [768], P('fsdp'), may hold values from -1.5 to 1.5
- w_fc1: bfloat16 [768, 3072], P('fsdp'), may hold values from -0.21875 to 0.21875
- b_fc1: bfloat16 [3072], P('fsdp'), may hold values from -1.5 to 1.5
- w_fc2: bfloat16 [3072, 768], P('fsdp'), may hold values from -0.109375 to 0.109375
- b_fc2: bfloat16 [768], P('fsdp'), may hold values from -1.5 to 1.5
Outputs:
- layer_out: bfloat16 [16384, 768], P(('ctx', 'fsdp'))
- grad_tokens: float32 [16384, 768], P(('ctx', 'fsdp'))
- grad_ln_gain_attn: float32 [768], P('fsdp')
- grad_ln_bias_attn: float32 [768], P('fsdp')
- grad_ln_gain_mlp: float32 [768], P('fsdp')
- grad_ln_bias_mlp: float32 [768], P('fsdp')
- grad_w_qkv: float32 [768, 2304], P('fsdp')
- grad_b_qkv: float32 [2304], P('fsdp')
- grad_w_out: float32 [768, 768], P('fsdp')
- grad_b_out: float32 [768], P('fsdp')
- grad_w_fc1: float32 [768, 3072], P('fsdp')
- grad_b_fc1: float32 [3072], P('fsdp')
- grad_w_fc2: float32 [3072, 768], P('fsdp')
- grad_b_fc2: float32 [768], P('fsdp')
All inputs are finite; a program needn't handle non-finite values.
Results may differ from a plain program's by a relative error of at most 0.0095.
Values may be sent and summed in bfloat16 or wider, within the bound.
No kernel may reach another device: no remote copies, remote signals or barrier semaphores. Data moves between devices by JAX's collectives and lax.ppermute only.
A program may use at most 512 MiB of HBM per device.

v0:
```python
from functools import partial
import math

import jax
import jax.numpy as jnp
from jax import lax
from jax.sharding import PartitionSpec as P

HEADS = 12
HEAD = 64
ROT = 16


EPS = 1e-05
MASKED = -1e30


def sent_together(arrays, axis, dim, along):
    widths = [math.prod(a.shape[along:]) for a in arrays]
    both = jnp.concatenate(
        [a.reshape(*a.shape[:along], w) for a, w in zip(arrays, widths)], axis=along
    )
    out = lax.all_gather(both, axis, axis=dim, tiled=True)
    parts = jnp.split(out, [sum(widths[:k]) for k in range(1, len(widths))], axis=along)
    return tuple((b.reshape(*out.shape[:along], *a.shape[along:]) for a, b in zip(arrays, parts)))


def in_one_piece(arrays, axis, dim, along):
    ends, at = ([], 0)
    for a in arrays[:-1]:
        at += a.shape[along]
        ends.append(at)
    both = jnp.concatenate(arrays, axis=along)
    return tuple(jnp.split(lax.all_gather(both, axis, axis=dim, tiled=True), ends, axis=along))


def positions(block_order, offset, length, block_rows):
    row_index = offset + jnp.arange(length, dtype=jnp.int32)
    block_index = row_index // block_rows
    block_ids = jnp.arange(block_order.shape[0], dtype=jnp.int32)
    anchor = jnp.sum(
        jnp.where(block_index[:, None] == block_ids[None, :], block_order[None, :], 0), axis=1
    )
    return anchor * block_rows + row_index % block_rows


def rotate(vectors, places, direction):
    half_dims = ROT // 2
    frequency = jnp.exp(jnp.arange(half_dims, dtype=jnp.float32) * (-2.0 * math.log(10000.0) / ROT))
    angles = places.astype(jnp.float32)[:, None] * frequency[None, :]
    cosine = jnp.cos(angles)[:, None, :]
    sines = direction * jnp.sin(angles)[:, None, :]
    first_half = vectors[..., :half_dims]
    second_half = vectors[..., half_dims:ROT]
    return jnp.concatenate(
        [
            first_half * cosine - second_half * sines,
            second_half * cosine + first_half * sines,
            vectors[..., ROT:],
        ],
        axis=-1,
    )


def norms(inputs, gain_attn, bias_attn, gain_mlp, bias_mlp):
    row_mean = jnp.mean(inputs, axis=1, keepdims=True)
    centred = inputs - row_mean
    row_var = jnp.mean(centred * centred, axis=1, keepdims=True)
    normed = centred * lax.rsqrt(row_var + EPS)
    return (normed * gain_attn + bias_attn, normed * gain_mlp + bias_mlp)


def keep_states(states):
    return states


def local(
    tokens,
    block_order,
    cotangent,
    ln_gain_attn,
    ln_bias_attn,
    ln_gain_mlp,
    ln_bias_mlp,
    w_qkv,
    b_qkv,
    w_out,
    b_out,
    w_fc1,
    b_fc1,
    w_fc2,
    b_fc2,
):
    full_weights = (
        lax.all_gather(ln_gain_attn, "fsdp", axis=0, tiled=True),
        lax.all_gather(ln_bias_attn, "fsdp", axis=0, tiled=True),
        lax.all_gather(ln_gain_mlp, "fsdp", axis=0, tiled=True),
        *sent_together((ln_bias_mlp, w_qkv), "fsdp", 0, 1),
        lax.all_gather(b_qkv, "fsdp", axis=0, tiled=True),
        *sent_together((w_out, b_out, w_fc1), "fsdp", 0, 1),
        *sent_together((b_fc1, w_fc2), "fsdp", 0, 1),
        lax.all_gather(b_fc2, "fsdp", axis=0, tiled=True),
    )
    (
        gain_attn,
        bias_attn,
        gain_mlp,
        bias_mlp,
        full_qkv,
        bias_qkv,
        full_out,
        bias_out,
        full_one,
        bias_one,
        full_two,
        bias_two,
    ) = full_weights
    local_rows = tokens.shape[0]
    model_width = tokens.shape[1]
    score_scale = 1.0 / math.sqrt(HEAD)
    own_pos = positions(
        block_order, lax.axis_index(("ctx", "fsdp")) * local_rows, local_rows, local_rows
    )
    inputs = tokens.astype(jnp.float32)
    (h_attn, h_mlp), norms_pull = jax.vjp(
        norms,
        inputs,
        gain_attn.astype(jnp.float32),
        bias_attn.astype(jnp.float32),
        gain_mlp.astype(jnp.float32),
        bias_mlp.astype(jnp.float32),
    )
    a_attn = h_attn.astype(jnp.bfloat16)
    a_mlp = h_mlp.astype(jnp.bfloat16)
    qkv_all = jnp.dot(a_attn, full_qkv, preferred_element_type=jnp.float32) + bias_qkv.astype(
        jnp.float32
    )
    query = rotate(qkv_all[:, :model_width].reshape(local_rows, HEADS, HEAD), own_pos, 1.0).astype(
        jnp.bfloat16
    )
    key_rot = rotate(
        qkv_all[:, model_width : 2 * model_width].reshape(local_rows, HEADS, HEAD), own_pos, 1.0
    ).astype(jnp.bfloat16)
    value_flat = qkv_all[:, 2 * model_width :].astype(jnp.bfloat16)
    value_heads = value_flat.reshape(local_rows, HEADS, HEAD)
    query_flat = query.reshape(local_rows, model_width)
    key_flat = key_rot.reshape(local_rows, model_width)
    start_states = (
        jnp.full((local_rows, HEADS), MASKED, jnp.float32),
        jnp.zeros((local_rows, HEADS), jnp.float32),
        jnp.zeros((local_rows, HEADS, HEAD), jnp.float32),
    )
    pair_keys = in_one_piece((key_flat, value_flat), "fsdp", 0, 1)
    pieces = in_one_piece((pair_keys[0], pair_keys[1]), "ctx", 0, 1)
    length = pieces[0].shape[0]
    remote_keys = pieces[0].reshape(length, HEADS, HEAD)
    remote_values = pieces[1].reshape(length, HEADS, HEAD)
    key_pos = positions(block_order, jnp.int32(0), length, local_rows)
    allowed = key_pos[None, None, :] <= own_pos[:, None, None]

    def work(states):
        running_max, running_sum, weighted = states
        scores = (
            jnp.einsum("qhd,khd->qhk", query, remote_keys, preferred_element_type=jnp.float32)
            * score_scale
        )
        scores = jnp.where(allowed, scores, MASKED)
        new_max = jnp.maximum(running_max, jnp.max(scores, axis=2))
        exps = jnp.where(allowed, jnp.exp(scores - new_max[:, :, None]), 0.0)
        running_sum = jnp.sum(exps, axis=2)
        weighted = jnp.einsum(
            "qhk,khd->qhd",
            exps.astype(jnp.bfloat16),
            remote_values,
            preferred_element_type=jnp.float32,
        )
        return (new_max, running_sum, weighted)

    running_max, running_sum, weighted = lax.cond(
        jnp.min(key_pos) <= jnp.max(own_pos), work, keep_states, start_states
    )
    attended = weighted / running_sum[:, :, None]
    log_total = running_max + jnp.log(running_sum)
    mixed_low = attended.reshape(local_rows, model_width).astype(jnp.bfloat16)
    attn_out = jnp.dot(mixed_low, full_out, preferred_element_type=jnp.float32) + bias_out.astype(
        jnp.float32
    )
    hidden_pre = jnp.dot(a_mlp, full_one, preferred_element_type=jnp.float32) + bias_one.astype(
        jnp.float32
    )
    hidden_act, gelu_pull = jax.vjp(partial(jax.nn.gelu, approximate=False), hidden_pre)
    act_low = hidden_act.astype(jnp.bfloat16)
    mlp_out = jnp.dot(act_low, full_two, preferred_element_type=jnp.float32) + bias_two.astype(
        jnp.float32
    )
    layer_out = (inputs + attn_out + mlp_out).astype(jnp.bfloat16)
    grad_out = cotangent.astype(jnp.float32)
    grad_wout = jnp.einsum("nd,ne->de", mixed_low, cotangent, preferred_element_type=jnp.float32)
    grad_bout = jnp.sum(grad_out, axis=0)
    grad_mixed = jnp.einsum(
        "ne,de->nd", cotangent, full_out, preferred_element_type=jnp.float32
    ).astype(jnp.bfloat16)
    grad_wtwo = jnp.einsum("nf,ne->fe", act_low, cotangent, preferred_element_type=jnp.float32)
    grad_act = jnp.einsum("ne,fe->nf", cotangent, full_two, preferred_element_type=jnp.float32)
    grad_hidden = gelu_pull(grad_act)[0].astype(jnp.bfloat16)
    grad_wone = jnp.einsum("nd,nf->df", a_mlp, grad_hidden, preferred_element_type=jnp.float32)
    grad_bone = jnp.sum(grad_hidden.astype(jnp.float32), axis=0)
    grad_hmlp = jnp.einsum("nf,df->nd", grad_hidden, full_one, preferred_element_type=jnp.float32)
    grad_heads = grad_mixed.reshape(local_rows, HEADS, HEAD)
    delta = jnp.sum(grad_heads.astype(jnp.float32) * attended, axis=2)
    gathered_lse, gathered_delta = in_one_piece((log_total, delta), ("ctx", "fsdp"), 0, 1)

    def grad_keys(running, pieces, offset):
        length = pieces[0].shape[0]
        remote_queries = pieces[0].reshape(length, HEADS, HEAD)
        remote_grads = pieces[1].reshape(length, HEADS, HEAD)
        query_pos = positions(block_order, offset, length, local_rows)
        allowed = own_pos[None, None, :] <= query_pos[:, None, None]

        def work(states):
            scores = (
                jnp.einsum(
                    "qhd,khd->qhk", remote_queries, key_rot, preferred_element_type=jnp.float32
                )
                * score_scale
            )
            probs = jnp.exp(jnp.where(allowed, scores - gathered_lse[:, :, None], MASKED))
            grad_prob = jnp.einsum(
                "qhd,khd->qhk", remote_grads, value_heads, preferred_element_type=jnp.float32
            )
            grad_score = (probs * (grad_prob - gathered_delta[:, :, None])).astype(jnp.bfloat16)
            grad_key = jnp.einsum(
                "qhk,qhd->khd", grad_score, remote_queries, preferred_element_type=jnp.float32
            )
            grad_value = jnp.einsum(
                "qhk,qhd->khd",
                probs.astype(jnp.bfloat16),
                remote_grads,
                preferred_element_type=jnp.float32,
            )
            return (grad_key, grad_value)

        return lax.cond(jnp.max(query_pos) >= jnp.min(own_pos), work, keep_states, running)

    zero_heads = jnp.zeros((local_rows, HEADS, HEAD), jnp.float32)
    pieces = in_one_piece((pair_keys[0], pair_keys[1]), "ctx", 0, 1)
    length = pieces[0].shape[0]
    grad_remote_keys = pieces[0].reshape(length, HEADS, HEAD)
    grad_remote_values = pieces[1].reshape(length, HEADS, HEAD)
    key_pos = positions(block_order, jnp.int32(0), length, local_rows)
    grad_allowed = key_pos[None, None, :] <= own_pos[:, None, None]

    def work(states):
        scores = (
            jnp.einsum("qhd,khd->qhk", query, grad_remote_keys, preferred_element_type=jnp.float32)
            * score_scale
        )
        probs = jnp.exp(jnp.where(grad_allowed, scores - log_total[:, :, None], MASKED))
        grad_prob = jnp.einsum(
            "qhd,khd->qhk", grad_heads, grad_remote_values, preferred_element_type=jnp.float32
        )
        grad_score = (probs * (grad_prob - delta[:, :, None])).astype(jnp.bfloat16)
        return jnp.einsum(
            "qhk,khd->qhd", grad_score, grad_remote_keys, preferred_element_type=jnp.float32
        )

    grad_query = lax.cond(jnp.min(key_pos) <= jnp.max(own_pos), work, keep_states, zero_heads)
    pair_queries = in_one_piece((query_flat, grad_mixed), "fsdp", 0, 1)
    grad_key, grad_value = grad_keys(
        (zero_heads, zero_heads),
        in_one_piece((pair_queries[0], pair_queries[1]), "ctx", 0, 1),
        jnp.int32(0),
    )
    grad_query = rotate(grad_query * score_scale, own_pos, -1.0)
    grad_key = rotate(grad_key * score_scale, own_pos, -1.0)
    grad_qkv = jnp.concatenate(
        [
            grad_query.reshape(local_rows, model_width),
            grad_key.reshape(local_rows, model_width),
            grad_value.reshape(local_rows, model_width),
        ],
        axis=1,
    ).astype(jnp.bfloat16)
    grad_wqkv = jnp.einsum("nd,nc->dc", a_attn, grad_qkv, preferred_element_type=jnp.float32)
    grad_bqkv = jnp.sum(grad_qkv.astype(jnp.float32), axis=0)
    grad_hattn = jnp.einsum("nc,dc->nd", grad_qkv, full_qkv, preferred_element_type=jnp.float32)
    grad_inputs, grad_gattn, grad_battn, grad_gmlp, grad_bmlp = norms_pull((grad_hattn, grad_hmlp))
    grad_tokens = grad_out + grad_inputs
    halves = (
        lax.psum_scatter(
            grad_gattn.astype(jnp.bfloat16), "fsdp", scatter_dimension=0, tiled=True
        ).astype(jnp.float32),
        lax.psum_scatter(
            grad_battn.astype(jnp.bfloat16), "fsdp", scatter_dimension=0, tiled=True
        ).astype(jnp.float32),
        lax.psum_scatter(
            grad_gmlp.astype(jnp.bfloat16), "fsdp", scatter_dimension=0, tiled=True
        ).astype(jnp.float32),
        lax.psum_scatter(
            grad_bmlp.astype(jnp.bfloat16), "fsdp", scatter_dimension=0, tiled=True
        ).astype(jnp.float32),
        lax.psum_scatter(
            grad_wqkv.astype(jnp.bfloat16), "fsdp", scatter_dimension=0, tiled=True
        ).astype(jnp.float32),
        lax.psum_scatter(
            grad_bqkv.astype(jnp.bfloat16), "fsdp", scatter_dimension=0, tiled=True
        ).astype(jnp.float32),
        lax.psum_scatter(
            grad_wout.astype(jnp.bfloat16), "fsdp", scatter_dimension=0, tiled=True
        ).astype(jnp.float32),
        lax.psum_scatter(
            grad_bout.astype(jnp.bfloat16), "fsdp", scatter_dimension=0, tiled=True
        ).astype(jnp.float32),
        lax.psum_scatter(
            grad_wone.astype(jnp.bfloat16), "fsdp", scatter_dimension=0, tiled=True
        ).astype(jnp.float32),
        lax.psum_scatter(
            grad_bone.astype(jnp.bfloat16), "fsdp", scatter_dimension=0, tiled=True
        ).astype(jnp.float32),
        lax.psum_scatter(
            grad_wtwo.astype(jnp.bfloat16), "fsdp", scatter_dimension=0, tiled=True
        ).astype(jnp.float32),
    )
    totals = lax.psum(
        (
            halves[0],
            halves[1],
            halves[2],
            halves[3],
            halves[4],
            halves[5],
            halves[6],
            halves[7],
            halves[8],
            halves[9],
            halves[10],
        ),
        "ctx",
    )
    grad_bfc2 = totals[7]
    return (
        layer_out,
        grad_tokens,
        totals[0],
        totals[1],
        totals[2],
        totals[3],
        totals[4],
        totals[5],
        totals[6],
        totals[7],
        totals[8],
        totals[9],
        totals[10],
        grad_bfc2,
    )


def solution(mesh):
    placed = (
        P(("ctx", "fsdp"), None),
        P(),
        P(("ctx", "fsdp"), None),
        P("fsdp"),
        P("fsdp"),
        P("fsdp"),
        P("fsdp"),
        P("fsdp", None),
        P("fsdp"),
        P("fsdp", None),
        P("fsdp"),
        P("fsdp", None),
        P("fsdp"),
        P("fsdp", None),
        P("fsdp"),
    )
    return jax.shard_map(
        local,
        mesh=mesh,
        in_specs=placed,
        out_specs=(
            P(("ctx", "fsdp"), None),
            P(("ctx", "fsdp"), None),
            P("fsdp"),
            P("fsdp"),
            P("fsdp"),
            P("fsdp"),
            P("fsdp", None),
            P("fsdp"),
            P("fsdp", None),
            P("fsdp"),
            P("fsdp", None),
            P("fsdp"),
            P("fsdp", None),
            P("fsdp"),
        ),
        check_vma=False,
    )
```

profile of v0, /device:TPU:1, one launch (start us, length us, event | category | flops | bytes accessed | tf_op | source)
XLA Modules:
  0.0 1521.0 jit_solution(12114953694725768698)
XLA Ops:
  28.1 41.0 %all-gather.12.cloned.1.call-done = bf16[768,2305]{1,0:T(8,128)(2,1)} async-done(((bf16[384,2305]{1,0:T(8,128)(2,1)}), bf16[768,2305]{1,0:T(8,128)(2,1)}) %all-gather.12.cloned.1.call-update) | async-done | bytes 3540496 | tf_op jit(solution)/shard_map/all_gather | solution.py:23
  75.9 10.8 all_gather.44
  90.2 62.8 %all-gather.16.cloned.1.call-done = bf16[768,3841]{1,0:T(8,128)(2,1)} async-done(((bf16[384,3841]{1,0:T(8,128)(2,1)}), bf16[768,3841]{1,0:T(8,128)(2,1)}) %all-gather.16.cloned.1.call-update) | async-done | bytes 5899792 | tf_op jit(solution)/shard_map/all_gather | solution.py:23
  154.9 10.9 all_gather.50
  166.4 5.1 select_reduce_fusion
  173.5 7.4 broadcast_compare_fusion.1
  181.0 188.1 %all-gather.14.cloned.1.call-done = bf16[16384,1536]{1,0:T(8,128)(2,1)} async-done(((bf16[256,1536]{1,0:T(8,128)(2,1)}), bf16[16384,1536]{1,0:T(8,128)(2,1)}) %all-gather.14.cloned.1.call-update) | async-done | bytes 50331664 | tf_op jit(solution)/shard_map/all_gather | solution.py:34
  369.0 34.2 %fusion.127 = (bf16[16384,768]{1,0:T(8,128)(2,1)}, bf16[16384,768]{1,0:T(8,128)(2,1)}) fusion(bf16[16384,1536]{1,0:T(8,128)(2,1)} %all-gather.14.cloned.1.call-done), kind=kLoop, calls=%fused_computation.197 | loop fusion | bytes 100663296 | tf_op jit(solution)/shard_map/split | solution.py:34
  403.2 32.0 %copy.87 = bf16[16384,768]{0,1:T(8,128)(2,1)} copy(bf16[16384,768]{1,0:T(8,128)(2,1)} %get-tuple-element.359) | data formatting | bytes 50331648 | tf_op jit(solution)/shard_map/split | solution.py:34
  435.2 32.8 %copy.89 = bf16[16384,768]{0,1:T(8,128)(2,1)} copy(bf16[16384,768]{1,0:T(8,128)(2,1)} %get-tuple-element.358) | data formatting | bytes 50331648 | tf_op jit(solution)/shard_map/split | solution.py:34
  468.0 130.6 %conditional.3 = (f32[128,12]{0,1:T(8,128)}, f32[128,12]{0,1:T(8,128)}, f32[128,12,64]{0,2,1:T(8,128)S(1)}, f32[128,12]{0,1:T(8,128)S(1)}) conditional(s32[]{:T(128)} %convert_element_type.195, () %tuple.45, (pred[128,1,16384]{0,2,1:T(8,128)(4,1)S(1)}, bf16[16384,12,64]{0,2,1:T(8,128)(2,1)}, bf16[128,12,64]{0,2,1:T(8,128)(2,1)S(1)}, ...), branch_computations={%region_6.7_spmd, %region_7.10_spmd} | conditional | flops 6769605120 | bytes 359252000 | solution.py:179
  468.2 46.3 %fusion = (f32[128,12]{0,1:T(8,128)S(1)}, f32[12,16384,128]{2,1,0:T(8,128)}) fusion(pred[128,16384]{0,1:T(8,128)(4,1)S(1)} %bitcast.149, bf16[16384,12,64]{0,2,1:T(8,128)(2,1)} %get-tuple-element.221, bf16[128,12,64]{0,2,1:T(8,128)(2,1)S(1)} %get-tuple-element.222), kind=kOutput, calls=%fused_computation.2 | convolution fusion | flops 3296721408 | bytes 128129024 | tf_op jit(solution)/shard_map/cond/branch_1_fun/qhd,khd->qhk/dot_general | solution.py:164
  515.1 36.8 %fusion.2 = f32[128,12]{0,1:T(8,128)} fusion(f32[12,16384,128]{2,1,0:T(8,128)} %get-tuple-element.353, f32[128,12]{0,1:T(8,128)} %broadcast_maximum_fusion, pred[128,16384]{0,1:T(8,128)(4,1)S(1)} %bitcast.150), kind=kLoop, calls=%fused_computation.4 | loop fusion | flops 125827584 | bytes 102772736 | tf_op jit(solution)/shard_map/cond/branch_1_fun/reduce_sum | solution.py:170
  552.7 45.9 %fusion.6 = f32[128,12,64]{0,2,1:T(8,128)S(1)} fusion(bf16[16384,12,64]{0,2,1:T(8,128)(2,1)} %get-tuple-element.223, f32[12,16384,128]{2,1,0:T(8,128)} %get-tuple-element.353, f32[128,12]{0,1:T(8,128)} %broadcast_maximum_fusion, pred[128,16384]{0,1:T(8,128)(4,1)S(1)} %bitcast.151), kind=kOutput, calls=%fused_computation.7 | convolution fusion | flops 3347054592 | bytes 128325632 | tf_op jit(solution)/shard_map/cond/branch_1_fun/qhk,khd->qhd/dot_general | solution.py:171
  601.4 4.0 all-gather.3
  608.2 7.3 multiply_convert_fusion
  630.5 98.7 %conditional.4 = (f32[128,12,64]{0,2,1:T(8,128)}) conditional(s32[]{:T(128)} %convert_element_type.195, () %tuple.47, (pred[128,1,16384]{0,2,1:T(8,128)(4,1)S(1)}, bf16[16384,12,64]{0,2,1:T(8,128)(2,1)}, bf16[128,12,64]{0,2,1:T(8,128)(2,1)S(1)}, f32[128,12]{0,1:T(8,128)S(1)}, bf16[16384,12,64]{0,2,1:T(8,128)(2,1)}, ...), branch_computations={%region_11.12_spmd, %region_12.13_spmd} | conditional | flops 9814671360 | bytes 279719936 | solution.py:267
  630.7 43.3 %fusion.130 = f32[12,16384,128]{2,1,0:T(8,128)} fusion(bf16[16384,12,64]{0,2,1:T(8,128)(2,1)} %get-tuple-element.225, bf16[128,12,64]{0,2,1:T(8,128)(2,1)S(1)} %get-tuple-element.226), kind=kOutput, calls=%fused_computation.200 | convolution fusion | flops 3221225472 | bytes 126025728 | tf_op jit(solution)/shard_map/cond/branch_1_fun/qhd,khd->qhk/dot_general | solution.py:255
  674.0 55.2 %fusion.21 = f32[128,12,64]{0,2,1:T(8,128)} fusion(bf16[16384,12,64]{0,2,1:T(8,128)(2,1)} %get-tuple-element.225, f32[12,16384,128]{2,1,0:T(8,128)} %fusion.130, f32[128,12]{0,1:T(8,128)S(1)} %get-tuple-element.230, f32[128,12]{0,1:T(8,128)S(1)} %get-tuple-element.227, pred[128,16384]{0,1:T(8,128)(4,1)S(1)} %bitcast.152, ...), kind=kOutput, calls=%fused_computation.21 | convolution fusion | flops 6593445888 | bytes 153694208 | tf_op jit(solution)/shard_map/cond/branch_1_fun/qhk,khd->qhd/dot_general | solution.py:263
  731.7 170.4 %all-gather.22.cloned.1.call-done = f32[16384,24]{0,1:T(8,128)} async-done(((f32[128,24]{0,1:T(8,128)}), f32[16384,24]{0,1:T(8,128)}) %all-gather.22.cloned.1.call-update) | async-done | bytes 1572880 | tf_op jit(solution)/shard_map/all_gather | solution.py:34
  902.2 183.3 %conditional.5 = (f32[128,12,64]{0,2,1:T(8,128)}, bf16[128,768]{0,1:T(8,128)(2,1)}) conditional(s32[]{:T(128)} %convert_element_type.222, () %tuple.49, (s32[128]{0:T(128)S(1)}, s32[]{:T(128)}, s32[16384]{0:T(1024)S(1)}, s32[16384,1,1]{0,2,1:T(1,128)S(1)}, bf16[16384,1536]{0,1:T(8,128)(2,1)}, /*index=5*/bf16[128,12,64]{0,2,1:T(8,128)(2,1)S(1)}, ...), branch_computations={%region_15.16_spmd, %region_16.17_spmd} | conditional | flops 13138888704 | bytes 526321728 | solution.py:243
  902.2 34.4 %fusion.125 = (bf16[16384,768]{0,1:T(8,128)(2,1)}, bf16[16384,768]{0,1:T(8,128)(2,1)}) fusion(bf16[16384,1536]{0,1:T(8,128)(2,1)} %get-tuple-element.236), kind=kLoop, calls=%fused_computation.195 | loop fusion | bytes 100663296 | tf_op jit(solution)/shard_map/split | solution.py:34
  936.7 43.9 %fusion.131 = f32[12,128,16384]{2,1,0:T(8,128)} fusion(bf16[128,12,64]{0,2,1:T(8,128)(2,1)S(1)} %get-tuple-element.235, bf16[16384,12,64]{0,2,1:T(8,128)(2,1)} %bitcast.143), kind=kOutput, calls=%fused_computation.201 | convolution fusion | flops 3221225472 | bytes 126025728 | tf_op jit(solution)/shard_map/cond/branch_1_fun/qhd,khd->qhk/dot_general | solution.py:222
  983.6 58.7 %fusion.39 = f32[128,12,64]{0,2,1:T(8,128)} fusion(bf16[16384,12,64]{0,2,1:T(8,128)(2,1)} %bitcast.144, f32[12,128,16384]{2,1,0:T(8,128)} %fusion.131, f32[16384,12]{0,1:T(8,128)} %get-tuple-element.357, f32[16384,12]{0,1:T(8,128)} %get-tuple-element.356, pred[16384,128]{0,1:T(8,128)(4,1)S(1)} %broadcast_compare_fusion, ...), kind=kOutput, calls=%fused_computation.37 | convolution fusion | flops 6593445888 | bytes 155254784 | tf_op jit(solution)/shard_map/cond/branch_1_fun/qhk,qhd->khd/dot_general | solution.py:232
  1042.3 43.0 %fusion.42 = bf16[12,128,64]{1,2,0:T(8,128)(2,1)} fusion(bf16[16384,12,64]{0,2,1:T(8,128)(2,1)} %bitcast.148, f32[12,128,16384]{2,1,0:T(8,128)} %fusion.131, f32[16384,12]{0,1:T(8,128)S(1)} %copy-done.18, pred[16384,128]{0,1:T(8,128)(4,1)S(1)} %broadcast_compare_fusion), kind=kOutput, calls=%fused_computation.38 | convolution fusion | flops 3321987072 | bytes 128909312 | tf_op jit(solution)/shard_map/cond/branch_1_fun/qhk,qhd->khd/dot_general | solution.py:235
  1088.5 4.0 convolution_convert_fusion.2
  1100.0 4.2 fusion.80
  1107.9 4.0 fusion.67
  1112.0 5.9 fusion.99
  1118.0 8.0 all-reduce.8
  1129.5 10.6 reduce-scatter.5.cloned.1.call-done
  1140.1 373.1 %all-reduce.10 = (f32[384]{0:T(512)}, f32[384]{0:T(512)}, f32[384]{0:T(512)}, f32[384]{0:T(512)}, f32[384,2304]{1,0:T(8,128)}, /*index=5*/f32[1152]{0:T(1024)}, ...) all-reduce(f32[384]{0:T(512)S(1)} %dynamic-slice_convert_fusion.6, ...), channel_id=1, replica_groups=mesh['ctx'=64,'fsdp'=2] {'ctx'}, use_global_device_ids=true, to_apply=%region_21.22 | all-reduce | flops 3543552 | bytes 21270528 | tf_op jit(solution)/shard_map/psum | solution.py:324
  (239 shorter events, 76.0 us)
Async XLA Ops:
  7.2 62.0 %all-gather.12.cloned.1.call-start = ((), (), s32[]{:S(2)}) async-start(), calls=%async_computation.4 | async-start | bytes 5603328 | tf_op jit(solution)/shard_map/all_gather | solution.py:23
  11.7 141.4 %all-gather.16.cloned.1.call-start = ((), (), s32[]{:S(2)}) async-start(), calls=%async_computation.6 | async-start | bytes 9142272 | tf_op jit(solution)/shard_map/all_gather | solution.py:23
  15.9 353.1 %all-gather.14.cloned.1.call-start = ((), (), s32[]{:S(2)}) async-start(), calls=%async_computation.5 | async-start | bytes 51118080 | tf_op jit(solution)/shard_map/all_gather | solution.py:34
  19.8 52.8 %copy-start.29 = (f32[768]{0:T(1024)}, f32[768]{0:T(1024)S(1)}, u32[]{:S(2)}) copy-start(f32[768]{0:T(1024)S(1)} %reshape.483) | copy-start | bytes 9220
  23.0 49.6 %copy-start.33 = (f32[768]{0:T(1024)}, f32[768]{0:T(1024)S(1)}, u32[]{:S(2)}) copy-start(f32[768]{0:T(1024)S(1)} %reshape.484) | copy-start | bytes 9220
  26.5 46.1 %copy-start.47 = (s32[128]{0:T(128)}, s32[128]{0:T(128)S(1)}, u32[]{:S(2)}) copy-start(s32[128]{0:T(128)S(1)} %select_reduce_fusion.1) | copy-start | bytes 1540
  26.6 46.0 %copy-start.37 = (f32[128]{0:T(128)}, f32[128]{0:T(128)S(1)}, u32[]{:S(2)}) copy-start(f32[128]{0:T(128)S(1)} %broadcast_multiply_fusion.4) | copy-start | bytes 1540
  28.1 46.7 %copy-start.35 = (f32[128,8]{0,1:T(8,128)}, f32[128,8]{0,1:T(8,128)S(1)}, u32[]{:S(2)}) copy-start(f32[128,8]{0,1:T(8,128)S(1)} %get-tuple-element.378) | copy-start | bytes 12292
  86.7 519.8 %all-gather.18.cloned.1.call-start = ((), (), s32[]{:S(2)}) async-start(), calls=%async_computation.7 | async-start | bytes 8257536 | tf_op jit(solution)/shard_map/all_gather | solution.py:23
  87.1 66.0 %copy-start.3 = (bf16[128,768]{1,0:T(8,128)(2,1)S(1)}, bf16[128,768]{1,0:T(8,128)(2,1)}, u32[]{:S(2)}) copy-start(bf16[128,768]{1,0:T(8,128)(2,1)} %param.23) | copy-start | bytes 589828
  90.1 76.4 %copy-start.55 = (s32[128]{0:T(128)S(1)}, s32[128]{0:T(128)}, u32[]{:S(2)}) copy-start(s32[128]{0:T(128)} %param.22) | copy-start | bytes 1540
  90.1 641.6 %all-gather.20.cloned.1.call-start = ((), (), s32[]{:S(2)}) async-start(), calls=%async_computation.8 | async-start | bytes 51118080 | tf_op jit(solution)/shard_map/all_gather | solution.py:34
  165.7 736.3 %all-gather.22.cloned.1.call-start = ((), (), s32[]{:S(2)}) async-start(), calls=%async_computation.9 | async-start | bytes 1585152 | tf_op jit(solution)/shard_map/all_gather | solution.py:34
  468.0 131.3 %copy-start.23 = (bf16[768,128]{1,0:T(8,128)(2,1)S(1)}, bf16[768,128]{1,0:T(8,128)(2,1)}, u32[]{:S(2)}) copy-start(bf16[768,128]{1,0:T(8,128)(2,1)} %copy-done.22) | copy-start | bytes 589828
  468.0 133.4 %copy-start.52 = (bf16[384]{0:T(512)(128)(2,1)S(1)}, bf16[384]{0:T(512)(128)(2,1)}, u32[]{:S(2)}) copy-start(bf16[384]{0:T(512)(128)(2,1)} %param.26) | copy-start | bytes 2308
  468.0 140.2 %copy-start.1 = (bf16[128,768]{1,0:T(8,128)(2,1)S(1)}, bf16[128,768]{1,0:T(8,128)(2,1)}, u32[]{:S(2)}) copy-start(bf16[128,768]{1,0:T(8,128)(2,1)} %param.21) | copy-start | bytes 589828
  468.0 140.2 %copy-start.38 = (f32[128]{0:T(128)S(1)}, f32[128]{0:T(128)}, u32[]{:S(2)}) copy-start(f32[128]{0:T(128)} %copy-done.37) | copy-start | bytes 1540
  468.0 140.2 %copy-start.42 = (f32[128]{0:T(128)S(1)}, f32[128]{0:T(128)}, u32[]{:S(2)}) copy-start(f32[128]{0:T(128)} %copy-done.41) | copy-start | bytes 1540
  601.4 502.9 %reduce-scatter.9.cloned.1.call-start = ((), (), s32[]{:S(2)}) async-start(), calls=%async_computation.12 | async-start | bytes 7077888 | tf_op jit(solution)/shard_map/reduce_scatter | solution.py:314
  623.0 481.3 %reduce-scatter.11.cloned.1.call-start = ((), (), s32[]{:S(2)}) async-start(), calls=%async_computation.13 | async-start | bytes 7077888 | tf_op jit(solution)/shard_map/reduce_scatter | solution.py:320
  626.7 480.0 %reduce-scatter.7.cloned.1.call-start = ((), (), s32[]{:S(2)}) async-start(), calls=%async_computation.11 | async-start | bytes 1769472 | tf_op jit(solution)/shard_map/reduce_scatter | solution.py:308
  629.1 511.0 %reduce-scatter.5.cloned.1.call-start = ((), (), s32[]{:S(2)}) async-start(), calls=%async_computation.10 | async-start | bytes 5308416 | tf_op jit(solution)/shard_map/reduce_scatter | solution.py:302
  630.4 271.7 %copy-start.13 = (bf16[128,12,64]{0,2,1:T(8,128)(2,1)S(1)}, bf16[128,12,64]{0,2,1:T(8,128)(2,1)}, u32[]{:S(2)}) copy-start(bf16[128,12,64]{0,2,1:T(8,128)(2,1)} %copy-done.12) | copy-start | bytes 589828
  630.4 271.7 %copy-start.17 = (bf16[128,768]{1,0:T(8,128)(2,1)S(1)}, bf16[128,768]{1,0:T(8,128)(2,1)}, u32[]{:S(2)}) copy-start(bf16[128,768]{1,0:T(8,128)(2,1)} %copy-done.16) | copy-start | bytes 589828
  630.4 271.7 %copy-start.27 = (s32[16384]{0:T(1024)S(1)}, s32[16384]{0:T(1024)}, u32[]{:S(2)}) copy-start(s32[16384]{0:T(1024)} %copy-done.26) | copy-start | bytes 196612
  630.5 271.7 %copy-start.48 = (s32[128]{0:T(128)S(1)}, s32[128]{0:T(128)}, u32[]{:S(2)}) copy-start(s32[128]{0:T(128)} %copy-done.47) | copy-start | bytes 1540
  902.2 184.4 %copy-start.36 = (f32[128,8]{0,1:T(8,128)S(1)}, f32[128,8]{0,1:T(8,128)}, u32[]{:S(2)}) copy-start(f32[128,8]{0,1:T(8,128)} %copy-done.35) | copy-start | bytes 12292
  902.2 186.2 %copy-start.2 = (bf16[128,768]{1,0:T(8,128)(2,1)S(1)}, bf16[128,768]{1,0:T(8,128)(2,1)}, u32[]{:S(2)}) copy-start(bf16[128,768]{1,0:T(8,128)(2,1)} %param.21) | copy-start | bytes 589828
  902.2 186.2 %copy-start.30 = (f32[768]{0:T(1024)S(1)}, f32[768]{0:T(1024)}, u32[]{:S(2)}) copy-start(f32[768]{0:T(1024)} %copy-done.29) | copy-start | bytes 9220
  902.2 186.2 %copy-start.34 = (f32[768]{0:T(1024)S(1)}, f32[768]{0:T(1024)}, u32[]{:S(2)}) copy-start(f32[768]{0:T(1024)} %copy-done.33) | copy-start | bytes 9220
  902.2 186.2 %copy-start.39 = (f32[128]{0:T(128)S(1)}, f32[128]{0:T(128)}, u32[]{:S(2)}) copy-start(f32[128]{0:T(128)} %copy-done.37) | copy-start | bytes 1540
  983.6 58.7 %copy-start.18 = (f32[16384,12]{0,1:T(8,128)S(1)}, f32[16384,12]{0,1:T(8,128)}, u32[]{:S(2)}) copy-start(f32[16384,12]{0,1:T(8,128)} %get-tuple-element.356) | copy-start | bytes 2359300 | tf_op jit(solution)/shard_map/cond
  (38 other events, 356.6 us)
Sparse Core Ops, SparseCore 0:
  11.8 57.3 all-gather.11
  71.4 81.6 all-gather.15
  156.2 212.7 all-gather.13
  371.1 71.1 all-gather.17
  445.1 204.7 all-gather.19
  651.3 250.6 all-gather.21
  905.0 60.0 reduce-scatter.8
  968.2 63.4 reduce-scatter.10
  1034.7 25.2 reduce-scatter.6
  1092.6 47.4 reduce-scatter.4
where the time goes:
time: 1540 us; the launch traced here: 1520 us
  waiting for transfers between devices  473 us (31%)
  blocking collectives  420 us (27%)
  matrix products  381 us (25%)
  local copies, waits for them, and re-layouts  149 us (10%)
  other arithmetic  77.1 us (5%)
  between operations  20.2 us (1%)
    psum x1, blocking collectives, local(): lax.psum((halves[0], halves[1], halves[2], halves[3], halves[4], halves[5...  373 us
    all_gather x3, waiting for transfers between devices, in_one_piece(): lax.all_gather(both, axis, axis=dim, tiled=True)  358 us
    split x5, local copies, waits for them, and re-layouts, in_one_piece(): jnp.split(lax.all_gather(both, axis, axis=dim, tiled=True), ends, axis=al...  135 us
    all_gather x3, waiting for transfers between devices, sent_together(): out = lax.all_gather(both, axis, axis=dim, tiled=True)  104 us
    dot_general x1, matrix products, work(): jnp.einsum('qhk,qhd->khd', grad_score, remote_queries, preferred_element_...  58.7 us
    dot_general x1, matrix products, work(): jnp.einsum('qhk,khd->qhd', grad_score, grad_remote_keys, preferred_elemen...  55.2 us
    dot_general x1, matrix products, work(): jnp.einsum('qhd,khd->qhk', query, remote_keys, preferred_element_type=jnp...  46.3 us
    dot_general x1, matrix products, work(): jnp.einsum('qhk,khd->qhd', exps.astype(jnp.bfloat16), remote_values, pref...  45.9 us
  transfers between devices with their start and end apart: 10, of which 5 were waited for; matrix products, arithmetic and copies ran while one was open for 39% of the time, Pallas kernels for 0%

commit v1 on v0

v1 whole, which is shorter than its diff:
```python
from functools import partial
import math

import jax
import jax.numpy as jnp
from jax import lax
from jax.experimental import pallas as pl
from jax.experimental.pallas import tpu as pltpu
from jax.sharding import Mesh, PartitionSpec as P

HEADS = 12
HEAD = 64
ROT = 16
D = 768
FF = 3072
BLK = 128
EPS = 1e-05
MASKED = -1e30
FLOOR = -1e20

AXES = ("z", "xh", "y", "core", "fsdp")
SIZES = (4, 2, 4, 2, 2)
CTX = ("z", "xh", "y", "core")
TEAM = ("core", "fsdp")
KEYS = ("z", "xh")
GROUPS = ("z", "xh", "y")

NH = 3
HW = NH * HEAD
TEAM_ROWS = 512
NQ = 16
NK = 32
QT = 2
CH = 4
NT = NQ // QT
BF = jnp.bfloat16
F32 = jnp.float32
VMEM_LIMIT = 56 * 1024 * 1024


def _sort_keys(kv_ref, ksrc, kvt, kn):
    def step(r, _):
        src = ksrc[r]
        at = pl.multiple_of((src % 4) * BLK, BLK)
        to = pl.multiple_of(r * BLK, BLK)
        blk = kv_ref[src // 4, :, pl.ds(at, BLK)]
        kvt[:, pl.ds(to, BLK)] = blk
        for h in range(NH):
            kn[h, pl.ds(to, BLK), :] = blk[2 * HEAD * h : 2 * HEAD * (h + 1)].T
        return 0

    lax.fori_loop(0, NK, step, 0)


def _tile_columns(ref, qsrc, t, rows):
    parts = []
    for i in range(QT):
        src = qsrc[t * QT + i]
        at = pl.multiple_of((src % 4) * BLK, BLK)
        parts.append(ref[src // 4, rows, pl.ds(at, BLK)])
    return jnp.concatenate(parts, axis=1)


def _allowed(kpos, qpos, t, c):
    row = lax.broadcasted_iota(jnp.int32, (BLK, QT * BLK), 0)
    col = lax.broadcasted_iota(jnp.int32, (BLK, BLK), 1)
    query = jnp.concatenate([qpos[t * QT + i] * BLK + col for i in range(QT)], axis=1)
    return jnp.concatenate([kpos[c * CH + i] * BLK + row <= query for i in range(CH)], axis=0)


def _forward(qsrc, qpos, ksrc, kpos, nfull, nall, qd_ref, kv_ref, o_ref, kvt, kn):
    _sort_keys(kv_ref, ksrc, kvt, kn)
    width = QT * BLK
    rows = CH * BLK

    def tile(t, _):
        blk = _tile_columns(qd_ref, qsrc, t, slice(None))
        half = lax.broadcasted_iota(jnp.int32, (2 * HEAD, width), 0) < HEAD
        zero = jnp.zeros((2 * HEAD, width), BF)
        queries = [
            jnp.where(half, blk[2 * HEAD * h : 2 * HEAD * (h + 1)], zero) for h in range(NH)
        ]

        def chunk(masked, c, carry):
            at = pl.multiple_of(c * rows, rows)
            out = []
            if masked:
                ok = _allowed(kpos, qpos, t, c)
            for h in range(NH):
                m, l, acc = carry[h]
                s = jnp.dot(kn[h, pl.ds(at, rows), :], queries[h], preferred_element_type=F32)
                if masked:
                    s = jnp.where(ok, s, MASKED)
                new = jnp.maximum(m, jnp.max(s, axis=0, keepdims=True))
                p = jnp.exp(s - new)
                fade = jnp.exp(m - new)
                l = l * fade + jnp.sum(p, axis=0, keepdims=True)
                v = kvt[2 * HEAD * h + HEAD : 2 * HEAD * (h + 1), pl.ds(at, rows)]
                acc = acc * fade + jnp.dot(v, p.astype(BF), preferred_element_type=F32)
                out.append((new, l, acc))
            return tuple(out)

        start = tuple(
            (
                jnp.full((1, width), FLOOR, F32),
                jnp.zeros((1, width), F32),
                jnp.zeros((HEAD, width), F32),
            )
            for _ in range(NH)
        )
        state = lax.fori_loop(0, nfull[t], partial(chunk, False), start)
        state = lax.fori_loop(nfull[t], nall[t], partial(chunk, True), state)
        stats = []
        for h in range(NH):
            m, l, acc = state[h]
            some = l > 0.0
            safe = jnp.where(some, l, 1.0)
            o = (acc / safe).astype(BF)
            lse = jnp.where(some, m + jnp.log(safe), FLOOR)
            hi = lse.astype(BF)
            rest = lse - hi.astype(F32)
            mid = rest.astype(BF)
            low = (rest - mid.astype(F32)).astype(BF)
            stats += [hi.astype(F32), mid.astype(F32), low.astype(F32)]
            for i in range(QT):
                src = qsrc[t * QT + i]
                at = pl.multiple_of((src % 4) * BLK, BLK)
                o_ref[src // 4, HEAD * h : HEAD * (h + 1), pl.ds(at, BLK)] = o[:, i * BLK : (i + 1) * BLK]
        stats = jnp.concatenate(stats + [jnp.zeros((16 - 3 * NH, width), F32)], axis=0).astype(BF)
        for i in range(QT):
            src = qsrc[t * QT + i]
            at = pl.multiple_of((src % 4) * BLK, BLK)
            o_ref[src // 4, HW : HW + 16, pl.ds(at, BLK)] = stats[:, i * BLK : (i + 1) * BLK]
        return 0

    lax.fori_loop(0, NT, tile, 0)


def _backward(
    qsrc, qpos, ksrc, kpos, nfull, nall, qd_ref, kv_ref, ld_ref, dq_ref, dkv_ref, kvt, kn, acc, w1, w2, dq
):
    _sort_keys(kv_ref, ksrc, kvt, kn)
    width = QT * BLK
    rows = CH * BLK
    acc[...] = jnp.zeros_like(acc)

    def tile(t, _):
        blk = _tile_columns(qd_ref, qsrc, t, slice(None))
        stats = _tile_columns(ld_ref, qsrc, t, slice(None))
        top = lax.broadcasted_iota(jnp.int32, (2 * HEAD, width), 0) < HEAD
        left = lax.broadcasted_iota(jnp.int32, (width, 2 * HEAD), 1) < HEAD
        zero = jnp.zeros((2 * HEAD, width), BF)
        zero_t = jnp.zeros((width, 2 * HEAD), BF)
        for h in range(NH):
            both = blk[2 * HEAD * h : 2 * HEAD * (h + 1)]
            w1[h, :, :width] = jnp.where(top, both, zero)
            w1[h, :, width:] = jnp.where(top, zero, both)
            turned = both.T
            w2[h, :width, :] = jnp.where(left, turned, zero_t)
            w2[h, width:, :] = jnp.where(left, zero_t, turned)
        dq[...] = jnp.zeros_like(dq)

        def chunk(masked, c, _):
            at = pl.multiple_of(c * rows, rows)
            if masked:
                ok = _allowed(kpos, qpos, t, c)
            for h in range(NH):
                sd = jnp.dot(kn[h, pl.ds(at, rows), :], w1[h], preferred_element_type=F32)
                s = sd[:, :width]
                if masked:
                    s = jnp.where(ok, s, MASKED)
                p = jnp.exp(s - stats[h : h + 1])
                ds = (p * (sd[:, width:] - stats[NH + h : NH + h + 1])).astype(BF)
                pd = jnp.concatenate([ds, p.astype(BF)], axis=1)
                acc[h, pl.ds(at, rows), :] += jnp.dot(pd, w2[h], preferred_element_type=F32)
                k = kvt[2 * HEAD * h : 2 * HEAD * h + HEAD, pl.ds(at, rows)]
                dq[h] += jnp.dot(k, ds, preferred_element_type=F32)
            return 0

        lax.fori_loop(0, nfull[t], partial(chunk, False), 0)
        lax.fori_loop(nfull[t], nall[t], partial(chunk, True), 0)
        for h in range(NH):
            out = (dq[h] * 0.125).astype(BF)
            for i in range(QT):
                src = qsrc[t * QT + i]
                at = pl.multiple_of((src % 4) * BLK, BLK)
                dq_ref[src // 4, HEAD * h : HEAD * (h + 1), pl.ds(at, BLK)] = out[:, i * BLK : (i + 1) * BLK]
        return 0

    lax.fori_loop(0, NT, tile, 0)

    def back(r, _):
        src = ksrc[r]
        at = pl.multiple_of((src % 4) * BLK, BLK)
        for h in range(NH):
            part = acc[h, pl.ds(pl.multiple_of(r * BLK, BLK), BLK), :].T.astype(BF)
            dkv_ref[src // 4, 2 * HEAD * h : 2 * HEAD * (h + 1), pl.ds(at, BLK)] = part
        return 0

    lax.fori_loop(0, NK, back, 0)


def _specs(n):
    return [pl.BlockSpec(memory_space=pltpu.VMEM)] * n


def attend_forward(plan, qd, kv):
    return pl.pallas_call(
        _forward,
        out_shape=jax.ShapeDtypeStruct((4, HW + 16, TEAM_ROWS), BF),
        in_specs=[pl.BlockSpec(memory_space=pltpu.SMEM)] * 6 + _specs(2),
        out_specs=pl.BlockSpec(memory_space=pltpu.VMEM),
        scratch_shapes=[
            pltpu.VMEM((2 * HW, NK * BLK), BF),
            pltpu.VMEM((NH, NK * BLK, 2 * HEAD), BF),
        ],
        compiler_params=pltpu.CompilerParams(vmem_limit_bytes=VMEM_LIMIT),
        name="attend_forward",
    )(*plan, qd, kv)


def attend_backward(plan, qd, kv, ld):
    width = QT * BLK
    return pl.pallas_call(
        _backward,
        out_shape=(
            jax.ShapeDtypeStruct((4, HW, TEAM_ROWS), BF),
            jax.ShapeDtypeStruct((8, 2 * HW, TEAM_ROWS), BF),
        ),
        in_specs=[pl.BlockSpec(memory_space=pltpu.SMEM)] * 6 + _specs(3),
        out_specs=tuple(_specs(2)),
        scratch_shapes=[
            pltpu.VMEM((2 * HW, NK * BLK), BF),
            pltpu.VMEM((NH, NK * BLK, 2 * HEAD), BF),
            pltpu.VMEM((NH, NK * BLK, 2 * HEAD), F32),
            pltpu.VMEM((NH, 2 * HEAD, 2 * width), BF),
            pltpu.VMEM((NH, 2 * width, 2 * HEAD), BF),
            pltpu.VMEM((NH, HEAD, width), F32),
        ],
        compiler_params=pltpu.CompilerParams(vmem_limit_bytes=VMEM_LIMIT),
        name="attend_backward",
    )(*plan, qd, kv, ld)


def pick(table, index):
    ids = jnp.arange(table.shape[0], dtype=jnp.int32)
    return jnp.sum(jnp.where(index[:, None] == ids[None, :], table[None, :], 0), axis=1)


def in_order(pos):
    ids = jnp.arange(pos.shape[0], dtype=jnp.int32)
    rank = jnp.sum((pos[None, :] < pos[:, None]).astype(jnp.int32), axis=1)
    hit = rank[None, :] == ids[:, None]
    return (
        jnp.sum(jnp.where(hit, ids[None, :], 0), axis=1),
        jnp.sum(jnp.where(hit, pos[None, :], 0), axis=1),
    )


def make_plan(block_order, z, xh, y):
    team = jnp.arange(4, dtype=jnp.int32)
    mine = ((z * 2 + xh) * 4 + jnp.arange(4, dtype=jnp.int32))[:, None] * 4 + team[None, :]
    theirs = (jnp.arange(8, dtype=jnp.int32) * 4 + y)[:, None] * 4 + team[None, :]
    qsrc, qpos = in_order(pick(block_order, mine.reshape(-1)))
    ksrc, kpos = in_order(pick(block_order, theirs.reshape(-1)))
    ends = qpos.reshape(NT, QT)
    below = jnp.sum((kpos[None, :] < ends[:, :1]).astype(jnp.int32), axis=1)
    upto = jnp.sum((kpos[None, :] <= ends[:, -1:]).astype(jnp.int32), axis=1)
    return (qsrc, qpos, ksrc, kpos, below // CH, (upto + CH - 1) // CH)


def rotate(x, cosine, sine):
    a, b = x[:, :, : ROT // 2], x[:, :, ROT // 2 : ROT]
    return jnp.concatenate(
        [a * cosine - b * sine, b * cosine + a * sine, x[:, :, ROT:]], axis=2
    )


def dot(a, b, dims):
    return lax.dot_general(a, b, (dims, ((), ())), preferred_element_type=F32)


def local(
    tokens,
    block_order,
    cotangent,
    ln_gain_attn,
    ln_bias_attn,
    ln_gain_mlp,
    ln_bias_mlp,
    w_qkv,
    b_qkv,
    w_out,
    b_out,
    w_fc1,
    b_fc1,
    w_fc2,
    b_fc2,
):
    z, xh, y, core, fsdp = (lax.axis_index(a) for a in AXES)
    team = core * 2 + fsdp
    mine = fsdp * 2 + core
    theirs = (1 - fsdp) * 2 + core
    swap = [(0, 1), (1, 0)]

    def columns(w, which, width):
        return lax.dynamic_slice_in_dim(w, which * width, width, axis=1)

    def qkv_columns(w, which):
        return jnp.concatenate(
            [columns(w[:, i * D : (i + 1) * D], which, HW) for i in range(3)], axis=1
        )

    def whole_rows(keep, send):
        other = lax.ppermute(send, "fsdp", swap)
        return jnp.where(
            fsdp == 0, jnp.concatenate([keep, other]), jnp.concatenate([other, keep])
        )

    x4 = lax.all_gather(tokens, TEAM, axis=0, tiled=True)
    w_q = whole_rows(qkv_columns(w_qkv, mine), qkv_columns(w_qkv, theirs))
    vectors = lax.all_gather(
        jnp.concatenate(
            [ln_gain_attn, ln_bias_attn, ln_gain_mlp, ln_bias_mlp, b_out, b_fc2, b_qkv]
        ),
        "fsdp",
        axis=0,
        tiled=False,
    ).astype(F32)
    g_attn, c_attn, g_mlp, c_mlp, bias_out, bias_two = (
        vectors[:, i * 384 : (i + 1) * 384].reshape(D) for i in range(6)
    )
    bias_qkv = vectors[:, 6 * 384 :].reshape(3, 4, HW)
    bias_qkv = lax.dynamic_index_in_dim(bias_qkv, mine, 1, keepdims=False).reshape(3 * HW)
    dy4 = lax.all_gather(cotangent, TEAM, axis=0, tiled=True)
    w_one = whole_rows(columns(w_fc1, mine, D), columns(w_fc1, theirs, D))
    w_o = lax.dynamic_slice_in_dim(w_out, core * HW, HW, axis=0)
    w_two = lax.dynamic_slice_in_dim(w_fc2, core * D, D, axis=0)
    b_one = lax.dynamic_slice_in_dim(b_fc1, core * D, D, axis=0).astype(F32)

    plan = make_plan(block_order, z, xh, y)

    x = x4.astype(F32)
    centred = x - jnp.mean(x, axis=1, keepdims=True)
    scale = lax.rsqrt(jnp.mean(centred * centred, axis=1, keepdims=True) + EPS)
    n = centred * scale
    a_attn = (n * g_attn + c_attn).astype(BF)
    a_mlp = (n * g_mlp + c_mlp).astype(BF)

    qkv = dot(w_q, a_attn, ((0,), (1,))) + bias_qkv[:, None]
    qkv = qkv.reshape(3, NH, HEAD, TEAM_ROWS)
    group = (z * 2 + xh) * 4 + y
    anchors = pick(block_order, group * 4 + jnp.arange(4, dtype=jnp.int32))
    places = (anchors[:, None] * BLK + jnp.arange(BLK, dtype=jnp.int32)[None, :]).reshape(-1)
    frequency = jnp.exp(jnp.arange(ROT // 2, dtype=F32) * (-2.0 * math.log(10000.0) / ROT))
    angles = frequency[:, None] * places.astype(F32)[None, :]
    cosine, sine = jnp.cos(angles), jnp.sin(angles)
    turned = rotate(qkv[:2], cosine, sine).astype(BF)
    d_mixed = dot(w_o, dy4, ((1,), (1,))).astype(BF).reshape(NH, HEAD, TEAM_ROWS)
    qd = jnp.stack([turned[0] * jnp.asarray(0.125, BF), d_mixed], axis=1)
    kv = jnp.stack([turned[1], qkv[2].astype(BF)], axis=1)
    qd_all = lax.all_gather(qd.reshape(2 * HW, TEAM_ROWS), "y", axis=0, tiled=False)
    kv_all = lax.all_gather(kv.reshape(2 * HW, TEAM_ROWS), KEYS, axis=0, tiled=False)

    hidden_pre = dot(a_mlp, w_one, ((1,), (0,))) + b_one
    hidden_act, gelu_pull = jax.vjp(partial(jax.nn.gelu, approximate=False), hidden_pre)
    act = hidden_act.astype(BF)
    out_part = dot(act, w_two, ((1,), (0,)))
    d_act = dot(dy4, w_two, ((1,), (1,)))
    d_hidden = gelu_pull(d_act)[0].astype(BF)
    grad_one = dot(a_mlp, d_hidden, ((0,), (0,)))
    grad_two = dot(act, dy4, ((0,), (0,)))
    grad_b_one = jnp.sum(d_hidden.astype(F32), axis=0)
    dh_mlp = dot(d_hidden, w_one, ((1,), (1,)))

    def summed(parts):
        took = lax.all_to_all(parts, GROUPS, 0, 0, tiled=True)
        return jnp.sum(took.astype(F32), axis=0)

    first = summed(
        jnp.concatenate(
            [grad_one.astype(BF).reshape(32, 24, D), grad_two.astype(BF).reshape(32, 24, D)], axis=1
        )
    ).astype(BF)

    def to_owner(part):
        pairs = []
        shape = (4, 2)
        for at in range(8):
            zz, f = at // 2, at % 2
            if f == 0 and zz >= 2:
                pairs.append((at, (zz - 2) * 2 + 1))
            elif f == 1 and zz < 2:
                pairs.append((at, (zz + 2) * 2))
            else:
                pairs.append((at, at))
        return lax.ppermute(part, ("z", "fsdp"), pairs)

    first = jnp.concatenate([to_owner(first[:24]), first[24:]], axis=0)
    first_all = lax.all_gather(first, CTX, axis=0, tiled=False)

    partial_out = attend_forward(plan, qd_all, kv_all)
    parts = lax.all_to_all(partial_out, "y", 0, 0, tiled=True).astype(F32)
    o_parts = parts[:, :HW].reshape(4, NH, HEAD, TEAM_ROWS)
    lse_parts = jnp.sum(parts[:, HW : HW + 3 * NH].reshape(4, NH, 3, TEAM_ROWS), axis=2)
    peak = jnp.max(lse_parts, axis=0)
    share = jnp.exp(lse_parts - peak[None])
    total = jnp.sum(share, axis=0)
    attended = jnp.sum(o_parts * (share / total[None])[:, :, None, :], axis=0)
    lse = peak + jnp.log(total)
    delta = jnp.sum(attended * d_mixed.astype(F32), axis=1)
    mixed = attended.astype(BF).reshape(HW, TEAM_ROWS)
    ld = jnp.concatenate([lse, delta, jnp.zeros((2, TEAM_ROWS), F32)], axis=0)
    ld_all = lax.all_gather(ld, "y", axis=0, tiled=False)

    dq_parts, dkv_parts = attend_backward(plan, qd_all, kv_all, ld_all)
    dq = jnp.sum(lax.all_to_all(dq_parts, "y", 0, 0, tiled=True).astype(F32), axis=0)
    dkv = jnp.sum(lax.all_to_all(dkv_parts, KEYS, 0, 0, tiled=True).astype(F32), axis=0)
    dkv = dkv.reshape(NH, 2, HEAD, TEAM_ROWS)
    back = rotate(jnp.stack([dq.reshape(NH, HEAD, TEAM_ROWS), dkv[:, 0]]), cosine, -sine)
    d_qkv = jnp.concatenate([back, dkv[None, :, 1]], axis=0).astype(BF)
    d_qkv = d_qkv.reshape(3 * HW, TEAM_ROWS)

    out_part = out_part + dot(mixed, w_o, ((0,), (0,)))
    grad_qkv = dot(a_attn, d_qkv, ((0,), (1,)))
    grad_out_t = dot(dy4, mixed, ((0,), (1,)))
    second = summed(
        jnp.concatenate([grad_qkv.astype(BF), grad_out_t.astype(BF)], axis=1).reshape(32, 24, D)
    ).astype(BF)
    second = jnp.concatenate([to_owner(second[:, : 3 * HW]), second[:, 3 * HW :]], axis=1)
    second_all = lax.all_gather(second, CTX, axis=0, tiled=False)

    dh_attn = dot(d_qkv, w_q, ((0,), (1,)))
    dn_part = dh_attn * g_attn + dh_mlp * g_mlp
    both = jnp.concatenate([out_part.astype(BF), dn_part.astype(BF)], axis=1)
    both = lax.all_to_all(both.reshape(4, BLK, 2 * D), TEAM, 0, 0, tiled=True)
    both = jnp.sum(both.astype(F32), axis=0)
    own = tokens.astype(F32)
    layer_out = (own + both[:, :D] + bias_out + bias_two).astype(BF)
    own_centred = own - jnp.mean(own, axis=1, keepdims=True)
    own_scale = lax.rsqrt(jnp.mean(own_centred * own_centred, axis=1, keepdims=True) + EPS)
    own_n = own_centred * own_scale
    dn = both[:, D:]
    grad_tokens = cotangent.astype(F32) + own_scale * (
        dn
        - jnp.mean(dn, axis=1, keepdims=True)
        - own_n * jnp.mean(dn * own_n, axis=1, keepdims=True)
    )

    def placed(part, width):
        return jnp.where(
            jnp.arange(4, dtype=jnp.int32)[:, None] == mine, part.reshape(-1, 1, width), 0.0
        ).reshape(-1)

    small = jnp.concatenate(
        [
            jnp.sum(dh_attn * n, axis=0),
            jnp.sum(dh_attn, axis=0),
            jnp.sum(dh_mlp * n, axis=0),
            jnp.sum(dh_mlp, axis=0),
            jnp.sum(cotangent.astype(F32), axis=0),
            placed(jnp.sum(d_qkv.astype(F32), axis=1), HW),
            placed(grad_b_one, D),
        ]
    )
    small = lax.psum(small, AXES)

    def half(start, width):
        return lax.dynamic_slice_in_dim(small, start + fsdp * (width // 2), width // 2)

    first_all = first_all.reshape(2, 16, 2, 2, 24, D)
    second_all = second_all.reshape(2, 16, 2, 24, D)
    grad_w_one = (
        first_all[:, :, :, 0].transpose(1, 3, 0, 2, 4).reshape(384, FF).astype(F32)
    )
    grad_w_two = (
        first_all[:, :, :, 1].transpose(2, 0, 1, 3, 4).reshape(FF // 2, D).astype(F32)
    )
    grad_w_qkv = (
        second_all[..., : 3 * HW]
        .reshape(2, 16, 2, 24, 3, HW)
        .transpose(1, 3, 4, 0, 2, 5)
        .reshape(384, 3 * D)
        .astype(F32)
    )
    grad_w_out = (
        second_all[..., 3 * HW :].transpose(2, 4, 0, 1, 3).reshape(384, D).astype(F32)
    )
    grad_b_out = half(4 * D, D)
    return (
        layer_out,
        grad_tokens,
        half(0, D),
        half(D, D),
        half(2 * D, D),
        half(3 * D, D),
        grad_w_qkv,
        half(5 * D, 3 * D),
        grad_w_out,
        grad_b_out,
        grad_w_one,
        half(8 * D, FF),
        grad_w_two,
        grad_b_out,
    )


def solution(mesh):
    fine = Mesh(mesh.devices.reshape(SIZES), AXES)
    rows = P(AXES, None)
    vec = P("fsdp")
    mat = P("fsdp", None)
    return jax.shard_map(
        local,
        mesh=fine,
        in_specs=(
            rows, P(), rows, vec, vec, vec, vec, mat, vec, mat, vec, mat, vec, mat, vec,
        ),
        out_specs=(
            rows, rows, vec, vec, vec, vec, mat, vec, mat, vec, mat, vec, mat, vec,
        ),
        check_vma=False,
    )
```

time: 1540 us -> 617 us (0.40)
  matrix products: 381 us -> 26.8 us
  waiting for transfers between devices: 473 us -> 152 us
  blocking collectives: 420 us -> 128 us
  Pallas kernels: 0 us -> 125 us
  local copies, waits for them, and re-layouts: 149 us -> 74.4 us
  starting transfers between devices: 0.41 us -> 49.6 us
  other arithmetic: 77.1 us -> 38.7 us
    all_gather x6 -> x4, waiting for transfers between devices: 462 us -> 33.5 us  [the longest x1 33.5 us: local(): lax.all_gather(kv.reshape(2 * HW, TEAM_ROWS), KEYS, axis=0, tiled=False)]
    dot_general x19 -> x12, matrix products: 381 us -> 26.8 us  [dot(): return lax.dot_general(a, b, (dims, ((), ())), preferred_element_type=F32)]
    psum x1, blocking collectives: 373 us -> 64.5 us  [local(): small = lax.psum(small, AXES)]
    split x5 -> x0, local copies, waits for them, and re-layouts: 135 us -> none  [in_one_piece(): jnp.split(lax.all_gather(both, axis, axis=dim, tiled=True), ends, axis=al...]
    pallas_call x0 -> x2, Pallas kernels: none -> 125 us  [the longest x1 65.1 us: attend_forward(): pl.pallas_call(_forward, out_shape=jax.ShapeDtypeStruct((4, HW + 16, TEAM...]
    all_to_all x0 -> x5, waiting for transfers between devices: none -> 106 us  [the longest x2 45.6 us: summed(): took = lax.all_to_all(parts, GROUPS, 0, 0, tiled=True)]
    all_to_all x0 -> x5, starting transfers between devices: none -> 45 us  [the longest x2 18 us: summed(): took = lax.all_to_all(parts, GROUPS, 0, 0, tiled=True)]
    convert_element_type x6 -> x8, local copies, waits for them, and re-layouts: 0.2 us -> 42.5 us  [the longest x3 23.9 us: local(): grad_w_qkv = second_all[..., :3 * HW].reshape(2, 16, 2, 24, 3, HW).transp...]
  transfers between devices with their start and end apart: 10 -> 13, of which waited for: 5 -> 7; matrix products, arithmetic and copies ran while one was open for 39% -> 15% of each run, Pallas kernels for 0% -> 21%
where the time goes in v1:
time: 617 us; the launch traced here: 610 us
  waiting for transfers between devices  152 us (25%)
  blocking collectives  128 us (21%)
  Pallas kernels  125 us (20%)
  local copies, waits for them, and re-layouts  74.4 us (12%)
  starting transfers between devices  49.6 us (8%)
  other arithmetic  38.7 us (6%)
  matrix products  26.8 us (4%)
  between operations  14.9 us (2%)
    pallas_call x1, Pallas kernels, attend_forward(): pl.pallas_call(_forward, out_shape=jax.ShapeDtypeStruct((4, HW + 16, TEAM...  65.1 us
    psum x1, blocking collectives, local(): small = lax.psum(small, AXES)  64.5 us
    pallas_call x1, Pallas kernels, attend_backward(): pl.pallas_call(_backward, out_shape=(jax.ShapeDtypeStruct((4, HW, TEAM_RO...  60.3 us
    all_to_all x2, waiting for transfers between devices, summed(): took = lax.all_to_all(parts, GROUPS, 0, 0, tiled=True)  45.6 us
    all_gather x1, waiting for transfers between devices, local(): lax.all_gather(kv.reshape(2 * HW, TEAM_ROWS), KEYS, axis=0, tiled=False)  33.5 us
    all_to_all x1, waiting for transfers between devices, local(): lax.all_to_all(dkv_parts, KEYS, 0, 0, tiled=True).astype(F32)  30.3 us
    dot_general x12, matrix products, dot(): return lax.dot_general(a, b, (dims, ((), ())), preferred_element_type=F32)  26.8 us
    convert_element_type x3, local copies, waits for them, and re-layouts, local(): grad_w_qkv = second_all[..., :3 * HW].reshape(2, 16, 2, 24, 3, HW).transp...  23.9 us
  transfers between devices with their start and end apart: 13, of which 7 were waited for; matrix products, arithmetic and copies ran while one was open for 15% of the time, Pallas kernels for 21%

profile of v1, /device:TPU:1, one launch (start us, length us, event | category | flops | bytes accessed | tf_op | source)
XLA Modules:
  0.0 609.8 jit_solution(16492151151997431564)
XLA Ops:
  19.7 7.0 %all-gather.4 = bf16[2,1,3456]{2,1,0:T(2,128)(2,1)S(1)} all-gather(bf16[1,1,3456]{2,1,0:T(2,128)(2,1)S(1)} %reshape.381), channel_id=2, replica_groups=mesh['z'=4,'xh'=2,'y'=4,'core'=2,'fsdp'=2] {'fsdp'}, dimensions={0}, use_global_device_ids=true | all-gather | bytes 20736 | tf_op jit(solution)/shard_map/all_gather | solution.py:322
  30.9 17.5 %all_gather.36 = bf16[512,768]{1,0:T(8,128)(2,1)S(1)} all-gather(bf16[128,768]{1,0:T(8,128)(2,1)S(1)} %copy-done.3), channel_id=1, replica_groups=mesh['z'=4,'xh'=2,'y'=4,'core'=2,'fsdp'=2] {'core','fsdp'}, dimensions={0}, use_global_device_ids=true | all-gather | bytes 983040 | tf_op jit(solution)/shard_map/all_gather | solution.py:320
  50.1 16.4 %all_gather.39 = bf16[512,768]{1,0:T(8,128)(2,1)} all-gather(bf16[128,768]{1,0:T(8,128)(2,1)S(1)} %copy-done.12), channel_id=1, replica_groups=mesh['z'=4,'xh'=2,'y'=4,'core'=2,'fsdp'=2] {'core','fsdp'}, dimensions={0}, use_global_device_ids=true | all-gather | bytes 983040 | tf_op jit(solution)/shard_map/all_gather | solution.py:335
  70.3 2.7 convolution_add_fusion.1
  80.5 11.8 %collective-permute-done = bf16[384,768]{1,0:T(8,128)(2,1)} collective-permute-done((bf16[384,768]{1,0:T(8,128)(2,1)}, bf16[384,768]{1,0:T(8,128)(2,1)}, u32[]{:S(2)}, u32[]{:S(2)}) %collective-permute-start) | collective-permute-done | bytes 589856 | tf_op jit(solution)/shard_map/ppermute | solution.py:315
  92.3 5.9 multiply_convert_fusion
  103.5 9.9 %all-to-all-start.5 = ((bf16[32,48,768]{2,1,0:T(8,128)(2,1)}), bf16[32,48,768]{2,1,0:T(8,128)(2,1)}, u32[]{:S(2)}, u32[]{:S(2)}) async-start(bf16[32,48,768]{2,1,0:T(8,128)(2,1)} %pad_maximum_fusion), calls=%async_computation.5 | async-start | bytes 4718592 | tf_op jit(solution)/shard_map/all_to_all | solution.py:377
  113.7 33.7 %all-to-all-done.5 = bf16[32,48,768]{2,1,0:T(8,128)(2,1)} async-done(((bf16[32,48,768]{2,1,0:T(8,128)(2,1)}), bf16[32,48,768]{2,1,0:T(8,128)(2,1)}, u32[]{:S(2)}, u32[]{:S(2)}) %all-to-all-start.5) | async-done | bytes 2359328 | tf_op jit(solution)/shard_map/all_to_all | solution.py:377
  153.8 33.5 %all-gather.12.cloned.1.call-done.kv_ref = bf16[8,384,512]{2,1,0:T(8,128)(2,1)} async-done(((bf16[1,384,512]{2,1,0:T(8,128)(2,1)}), bf16[8,384,512]{2,1,0:T(8,128)(2,1)}) %all-gather.12.cloned.1.call-update) | async-done | bytes 3145744 | tf_op jit(solution)/shard_map/all_gather | solution.py:363
  187.4 65.1 %attend_forward.1 = bf16[4,208,512]{2,1,0:T(8,128)(2,1)} custom-call(s32[16]{0:T(128)} %get-tuple-element.115.qsrc, s32[16]{0:T(128)} %copy-done.33, s32[32]{0:T(128)} %get-tuple-element.113.ksrc, s32[32]{0:T(128)} %copy-done.34, s32[8]{0:T(128)} %get-tuple-element.166.nfull, s32[8]{0:T(128)} %get-tuple-element.165.nall, ...), custom_call_target="tpu_custom_call" | custom-call | tf_op jit(solution)/shard_map/attend_forward/pallas_call | solution.py:208
  252.5 4.3 all-to-all-start
  257.4 11.4 %all-to-all-done = bf16[4,208,512]{2,1,0:T(8,128)(2,1)} async-done(((bf16[4,208,512]{2,1,0:T(8,128)(2,1)}), bf16[4,208,512]{2,1,0:T(8,128)(2,1)}, u32[]{:S(2)}, u32[]{:S(2)}) %all-to-all-start) | async-done | bytes 852000 | tf_op jit(solution)/shard_map/all_to_all | solution.py:403
  276.7 10.1 %all-gather.1 = f32[32,512]{1,0:T(8,128)} all-gather(f32[8,512]{1,0:T(8,128)S(1)} %maximum_maximum_fusion), channel_id=3, replica_groups=mesh['z'=4,'xh'=2,'y'=4,'core'=2,'fsdp'=2] {'y'}, dimensions={0}, use_global_device_ids=true | all-gather | bytes 81920 | tf_op jit(solution)/shard_map/all_gather | solution.py:414
  286.8 60.3 %attend_backward.1 = (bf16[4,192,512]{2,1,0:T(8,128)(2,1)}, bf16[8,384,512]{2,1,0:T(8,128)(2,1)}) custom-call(s32[16]{0:T(128)} %get-tuple-element.115.qsrc, s32[16]{0:T(128)} %copy-done.33, s32[32]{0:T(128)} %get-tuple-element.113.ksrc, s32[32]{0:T(128)} %copy-done.34, s32[8]{0:T(128)} %get-tuple-element.166.nfull, s32[8]{0:T(128)} %get-tuple-element.165.nall, ...), custom_call_target="tpu_custom_call" | custom-call | tf_op jit(solution)/shard_map/attend_backward/pallas_call | solution.py:224
  347.1 12.6 %all_to_all.30 = bf16[4,192,512]{2,1,0:T(8,128)(2,1)} all-to-all(bf16[4,192,512]{2,1,0:T(8,128)(2,1)} %get-tuple-element.16), channel_id=1, replica_groups=mesh['z'=4,'xh'=2,'y'=4,'core'=2,'fsdp'=2] {'y'}, dimensions={0} | all-to-all | bytes 1572864 | tf_op jit(solution)/shard_map/all_to_all | solution.py:417
  359.7 10.8 %all-to-all-start.2 = ((bf16[8,384,512]{2,1,0:T(8,128)(2,1)}), bf16[8,384,512]{2,1,0:T(8,128)(2,1)}, u32[]{:S(2)}, u32[]{:S(2)}) async-start(bf16[8,384,512]{2,1,0:T(8,128)(2,1)} %get-tuple-element.17), calls=%async_computation.2 | async-start | bytes 6291456 | tf_op jit(solution)/shard_map/all_to_all | solution.py:418
  373.6 30.3 %all-to-all-done.2 = bf16[8,384,512]{2,1,0:T(8,128)(2,1)} async-done(((bf16[8,384,512]{2,1,0:T(8,128)(2,1)}), bf16[8,384,512]{2,1,0:T(8,128)(2,1)}, u32[]{:S(2)}, u32[]{:S(2)}) %all-to-all-start.2) | async-done | bytes 3145760 | tf_op jit(solution)/shard_map/all_to_all | solution.py:418
  411.9 8.1 %all-to-all-start.4 = ((bf16[32,24,768]{2,1,0:T(8,128)(2,1)}), bf16[32,24,768]{2,1,0:T(8,128)(2,1)}, u32[]{:S(2)}, u32[]{:S(2)}) async-start(bf16[32,24,768]{2,1,0:T(8,128)(2,1)} %bitcast.97), calls=%async_computation.4 | async-start | bytes 2359296 | tf_op jit(solution)/shard_map/all_to_all | solution.py:377
  423.5 11.9 %all-to-all-done.4 = bf16[32,24,768]{2,1,0:T(8,128)(2,1)} async-done(((bf16[32,24,768]{2,1,0:T(8,128)(2,1)}), bf16[32,24,768]{2,1,0:T(8,128)(2,1)}, u32[]{:S(2)}, u32[]{:S(2)}) %all-to-all-start.4) | async-done | bytes 1179680 | tf_op jit(solution)/shard_map/all_to_all | solution.py:377
  438.9 2.5 fusion.44
  443.0 2.5 add_convert_fusion.1
  451.8 11.9 %all-to-all-start.3 = ((bf16[4,128,1536]{2,1,0:T(8,128)(2,1)}), bf16[4,128,1536]{2,1,0:T(8,128)(2,1)S(1)}, u32[]{:S(2)}, u32[]{:S(2)}) async-start(bf16[4,128,1536]{2,1,0:T(8,128)(2,1)} %bitcast.94), calls=%async_computation.3 | async-start | bytes 3145728 | tf_op jit(solution)/shard_map/all_to_all | solution.py:436
  464.3 19.0 %all-to-all-done.3 = bf16[4,128,1536]{2,1,0:T(8,128)(2,1)S(1)} async-done(((bf16[4,128,1536]{2,1,0:T(8,128)(2,1)}), bf16[4,128,1536]{2,1,0:T(8,128)(2,1)S(1)}, u32[]{:S(2)}, u32[]{:S(2)}) %all-to-all-start.3) | async-done | bytes 1572896 | tf_op jit(solution)/shard_map/all_to_all | solution.py:436
  484.8 64.5 %psum.7 = f32[9216]{0:T(1024)S(1)} all-reduce(f32[9216]{0:T(1024)S(1)} %select_dynamic-update-slice_fusion), channel_id=1, replica_groups=mesh['z'=4,'xh'=2,'y'=4,'core'=2,'fsdp'=2] {'z','xh','y','core','fsdp'}, use_global_device_ids=true, to_apply=%region_32.33 | all-reduce | flops 9216 | bytes 73728 | tf_op jit(solution)/shard_map/psum | solution.py:466
  551.3 3.2 convert_bitcast_fusion
  554.5 2.6 copy.87
  557.1 4.5 copy.86
  561.6 7.0 %reshape.369 = f32[384,3072]{1,0:T(8,128)} reshape(f32[16,24,2,2,768]{4,3,2,1,0:T(2,128)} %copy.86) | data formatting | bytes 9437184 | tf_op jit(solution)/shard_map/convert_element_type | solution.py:474
  574.7 2.5 reshape.368
  578.6 8.2 %reshape.371 = f32[2,16,2,24,3,192]{5,4,3,2,1,0:T(4,128)} reshape(f32[2,16,2,24,576]{4,3,2,1,0:T(8,128)} %slice_convert_fusion) | data formatting | bytes 7077888 | tf_op jit(solution)/shard_map/convert_element_type | solution.py:484
  586.8 8.7 %copy.84 = f32[16,24,3,2,2,192]{5,4,3,2,1,0:T(2,128)} copy(f32[16,24,3,2,2,192]{5,2,1,4,0,3:T(4,128)} %bitcast.93) | data formatting | bytes 7077888 | tf_op jit(solution)/shard_map/convert_element_type | solution.py:484
  595.5 7.0 %reshape.367 = f32[384,2304]{1,0:T(8,128)} reshape(f32[16,24,3,2,2,192]{5,4,3,2,1,0:T(2,128)} %copy.84) | data formatting | bytes 7077888 | tf_op jit(solution)/shard_map/convert_element_type | solution.py:484
  (268 shorter events, 87.3 us)
Async XLA Ops:
  7.2 91.9 %copy-start = (bf16[1536,768]{1,0:T(8,128)(2,1)S(1)}, bf16[1536,768]{1,0:T(8,128)(2,1)}, u32[]{:S(2)}) copy-start(bf16[1536,768]{1,0:T(8,128)(2,1)} %param.28) | copy-start | bytes 7077892
  7.2 146.6 %all-gather.10.cloned.1.call-start = ((), (), s32[]{:S(2)}) async-start(), calls=%async_computation.6 | async-start | bytes 1966080 | tf_op jit(solution)/shard_map/all_gather | solution.py:362
  9.8 9.7 %copy-start.36 = (bf16[1152]{0:T(1024)(128)(2,1)S(1)}, bf16[1152]{0:T(1024)(128)(2,1)}, u32[]{:S(2)}) copy-start(bf16[1152]{0:T(1024)(128)(2,1)} %param.23) | copy-start | bytes 6916
  10.7 20.2 %copy-start.3 = (bf16[128,768]{1,0:T(8,128)(2,1)S(1)}, bf16[128,768]{1,0:T(8,128)(2,1)}, u32[]{:S(2)}) copy-start(bf16[128,768]{1,0:T(8,128)(2,1)} %param.15) | copy-start | bytes 589828
  13.8 36.4 %copy-start.12 = (bf16[128,768]{1,0:T(8,128)(2,1)S(1)}, bf16[128,768]{1,0:T(8,128)(2,1)}, u32[]{:S(2)}) copy-start(bf16[128,768]{1,0:T(8,128)(2,1)} %param.17) | copy-start | bytes 589828
  13.8 56.6 %collective-permute-start.1 = (bf16[384,576]{1,0:T(8,128)(2,1)}, bf16[384,576]{1,0:T(8,128)(2,1)}, u32[]{:S(2)}, u32[]{:S(2)}) collective-permute-start(bf16[384,576]{1,0:T(8,128)(2,1)} %pad_maximum_fusion.3), channel_id=1, source_target_pairs={{0,1},{1,0},{2,3},{3,2},{4,5},{5,4},{6,7},{7,6},{8,9},{9,8},{10,11... | collective-permute-start | bytes 1327112 | tf_op jit(solution)/shard_map/ppermute | solution.py:315
  48.6 21.8 %copy-start.17 = (bf16[384,192]{1,0:T(8,128)(2,1)S(1)}, bf16[384,192]{1,0:T(8,128)(2,1)}, u32[]{:S(2)}) copy-start(bf16[384,192]{1,0:T(8,128)(2,1)} %get-tuple-element.137) | copy-start | bytes 442372
  68.7 32.2 %copy-start.45 = (f32[512]{0:T(512)}, f32[512]{0:T(512)S(1)}, u32[]{:S(2)}) copy-start(f32[512]{0:T(512)S(1)} %add_rsqrt_fusion) | copy-start | bytes 6148
  74.9 112.5 %all-gather.12.cloned.1.call-start = ((), (), s32[]{:S(2)}) async-start(), calls=%async_computation.7 | async-start | bytes 3538944 | tf_op jit(solution)/shard_map/all_gather | solution.py:363
  77.3 15.0 %copy-start.30 = (f32[512]{0:T(512)S(1)}, f32[512]{0:T(512)}, u32[]{:S(2)}) copy-start(f32[512]{0:T(512)} %copy-done.29) | copy-start | bytes 6148
  77.3 15.0 %collective-permute-start = (bf16[384,768]{1,0:T(8,128)(2,1)}, bf16[384,768]{1,0:T(8,128)(2,1)}, u32[]{:S(2)}, u32[]{:S(2)}) collective-permute-start(bf16[384,768]{1,0:T(8,128)(2,1)} %get-tuple-element.126), channel_id=1, source_target_pairs={{0,1},{1,0},{2,3},{3,2},{4,5},{5,4},{6,7},{7,6},{8,9},{9,8},{10,11... | collective-permute-start | bytes 1769480 | tf_op jit(solution)/shard_map/ppermute | solution.py:315
  80.3 20.5 %copy-start.39 = (f32[768]{0:T(1024)}, f32[768]{0:T(1024)S(1)}, u32[]{:S(2)}) copy-start(f32[768]{0:T(1024)S(1)} %mul.311) | copy-start | bytes 9220
  103.5 43.9 %all-to-all-start.5 = ((bf16[32,48,768]{2,1,0:T(8,128)(2,1)}), bf16[32,48,768]{2,1,0:T(8,128)(2,1)}, u32[]{:S(2)}, u32[]{:S(2)}) async-start(bf16[32,48,768]{2,1,0:T(8,128)(2,1)} %pad_maximum_fusion), calls=%async_computation.5 | async-start | bytes 4718592 | tf_op jit(solution)/shard_map/all_to_all | solution.py:377
  113.4 36.7 %copy-start.53 = (s32[128]{0:T(128)S(1)}, s32[128]{0:T(128)}, u32[]{:S(2)}) copy-start(s32[128]{0:T(128)} %param.16) | copy-start | bytes 1540
  113.4 438.0 %all-gather.16.cloned.1.call-start = ((), (), s32[]{:S(2)}) async-start(), calls=%async_computation.9 | async-start | bytes 4792320 | tf_op jit(solution)/shard_map/all_gather | solution.py:400
  149.4 0.9 collective-permute-start.3
  151.8 35.6 %copy-start.33 = (s32[16]{0:T(128)}, s32[16]{0:T(128)S(1)}, u32[]{:S(2)}) copy-start(s32[16]{0:T(128)S(1)} %get-tuple-element.114.qpos) | copy-start | bytes 196
  153.0 34.3 %copy-start.34 = (s32[32]{0:T(128)}, s32[32]{0:T(128)S(1)}, u32[]{:S(2)}) copy-start(s32[32]{0:T(128)S(1)} %get-tuple-element.112.kpos) | copy-start | bytes 388
  252.5 16.3 %all-to-all-start = ((bf16[4,208,512]{2,1,0:T(8,128)(2,1)}), bf16[4,208,512]{2,1,0:T(8,128)(2,1)}, u32[]{:S(2)}, u32[]{:S(2)}) async-start(bf16[4,208,512]{2,1,0:T(8,128)(2,1)} %attend_forward.1), calls=%async_computation | async-start | bytes 1703936 | tf_op jit(solution)/shard_map/all_to_all | solution.py:403
  359.7 44.2 %all-to-all-start.2 = ((bf16[8,384,512]{2,1,0:T(8,128)(2,1)}), bf16[8,384,512]{2,1,0:T(8,128)(2,1)}, u32[]{:S(2)}, u32[]{:S(2)}) async-start(bf16[8,384,512]{2,1,0:T(8,128)(2,1)} %get-tuple-element.17), calls=%async_computation.2 | async-start | bytes 6291456 | tf_op jit(solution)/shard_map/all_to_all | solution.py:418
  411.9 9.3 %copy-start.25 = (f32[2,384]{1,0:T(2,128)S(1)}, f32[2,384]{1,0:T(2,128)}, u32[]{:S(2)}) copy-start(f32[2,384]{1,0:T(2,128)} %get-tuple-element.153) | copy-start | bytes 9220
  411.9 23.5 %all-to-all-start.4 = ((bf16[32,24,768]{2,1,0:T(8,128)(2,1)}), bf16[32,24,768]{2,1,0:T(8,128)(2,1)}, u32[]{:S(2)}, u32[]{:S(2)}) async-start(bf16[32,24,768]{2,1,0:T(8,128)(2,1)} %bitcast.97), calls=%async_computation.4 | async-start | bytes 2359296 | tf_op jit(solution)/shard_map/all_to_all | solution.py:377
  420.0 148.6 %all-gather.14.cloned.1.call-start = ((), (), s32[]{:S(2)}) async-start(), calls=%async_computation.8 | async-start | bytes 2396160 | tf_op jit(solution)/shard_map/all_gather | solution.py:431
  438.3 4.0 collective-permute-start.2
  451.8 12.0 %copy-start.52 = (f32[128]{0:T(128)S(1)}, f32[128]{0:T(128)}, u32[]{:S(2)}) copy-start(f32[128]{0:T(128)} %convert_reduce_fusion.6) | copy-start | bytes 1540
  451.8 12.0 %copy-start.4 = (bf16[128,768]{1,0:T(8,128)(2,1)S(1)}, bf16[128,768]{1,0:T(8,128)(2,1)}, u32[]{:S(2)}) copy-start(bf16[128,768]{1,0:T(8,128)(2,1)} %param.15) | copy-start | bytes 589828
  451.8 12.2 %copy-start.42 = (f32[768]{0:T(1024)S(1)}, f32[768]{0:T(1024)}, u32[]{:S(2)}) copy-start(f32[768]{0:T(1024)} %get-tuple-element.163) | copy-start | bytes 9220
  451.8 12.3 %copy-start.44 = (pred[4]{0:T(512)(128)(4,1)S(1)}, pred[4]{0:T(512)(128)(4,1)}, u32[]{:S(2)}) copy-start(pred[4]{0:T(512)(128)(4,1)} %copy-done.43) | copy-start | bytes 16
  451.8 12.5 %copy-start.24 = (f32[9216]{0:T(1024)S(1)}, f32[9216]{0:T(1024)}, u32[]{:S(2)}) copy-start(f32[9216]{0:T(1024)} %custom-call) | copy-start | bytes 110596
  451.8 31.5 %all-to-all-start.3 = ((bf16[4,128,1536]{2,1,0:T(8,128)(2,1)}), bf16[4,128,1536]{2,1,0:T(8,128)(2,1)S(1)}, u32[]{:S(2)}, u32[]{:S(2)}) async-start(bf16[4,128,1536]{2,1,0:T(8,128)(2,1)} %bitcast.94), calls=%async_computation.3 | async-start | bytes 3145728 | tf_op jit(solution)/shard_map/all_to_all | solution.py:436
  464.0 19.8 %copy-start.13 = (bf16[128,768]{1,0:T(8,128)(2,1)S(1)}, bf16[128,768]{1,0:T(8,128)(2,1)}, u32[]{:S(2)}) copy-start(bf16[128,768]{1,0:T(8,128)(2,1)} %param.17) | copy-start | bytes 589828
  551.3 51.2 %copy-start.35 = (f32[384]{0:T(512)}, f32[384]{0:T(512)S(1)}, u32[]{:S(2)}) copy-start(f32[384]{0:T(512)S(1)} %get-tuple-element.196) | copy-start | bytes 4612
  (38 other events, 94.4 us)
Sparse Core Ops, SparseCore 0:
  75.0 28.9 all-gather.9
  106.9 80.4 all-gather.11
  190.5 71.6 all-gather.15
  443.1 75.2 all-gather.13

commit v2 on v1

--- a/solution.py
+++ b/solution.py
@@ -257,16 +257,124 @@
     )
 
 
-def make_plan(block_order, z, xh, y):
-    team = jnp.arange(4, dtype=jnp.int32)
-    mine = ((z * 2 + xh) * 4 + jnp.arange(4, dtype=jnp.int32))[:, None] * 4 + team[None, :]
-    theirs = (jnp.arange(8, dtype=jnp.int32) * 4 + y)[:, None] * 4 + team[None, :]
+def make_plan(block_order, team, z, xh, y):
+    rows = jnp.arange(4, dtype=jnp.int32) ^ team
+    other = (y + jnp.arange(4, dtype=jnp.int32)) % 4
+    mine = ((z * 2 + xh) * 4 + other)[:, None] * 4 + rows[None, :]
+    step = jnp.arange(8, dtype=jnp.int32)
+    there = ((z + step // 2) % 4) * 2 + (xh ^ (step % 2))
+    theirs = (there * 4 + y)[:, None] * 4 + rows[None, :]
     qsrc, qpos = in_order(pick(block_order, mine.reshape(-1)))
     ksrc, kpos = in_order(pick(block_order, theirs.reshape(-1)))
     ends = qpos.reshape(NT, QT)
     below = jnp.sum((kpos[None, :] < ends[:, :1]).astype(jnp.int32), axis=1)
     upto = jnp.sum((kpos[None, :] <= ends[:, -1:]).astype(jnp.int32), axis=1)
     return (qsrc, qpos, ksrc, kpos, below // CH, (upto + CH - 1) // CH)
+
+
+def from_y(x, i):
+    return lax.ppermute(x, "y", [((d + i) % 4, d) for d in range(4)])
+
+
+def to_y(x, i):
+    return lax.ppermute(x, "y", [(d, (d + i) % 4) for d in range(4)])
+
+
+def _key_pairs(i):
+    pairs = []
+    for d in range(8):
+        there = ((d // 2 + i // 2) % 4) * 2 + ((d % 2) ^ (i % 2))
+        pairs.append((d, there))
+    return pairs
+
+
+def from_keys(x, i):
+    return lax.ppermute(x, KEYS, [(b, a) for a, b in _key_pairs(i)])
+
+
+def to_keys(x, i):
+    return lax.ppermute(x, KEYS, _key_pairs(i))
+
+
+def swapped(x, axis):
+    return lax.ppermute(x, axis, [(0, 1), (1, 0)])
+
+
+def team_rows(x):
+    pair = jnp.concatenate([x, swapped(x, "fsdp")])
+    return jnp.concatenate([pair, swapped(pair, "core")])
+
+
+def to_all_groups(x):
+    sent = jnp.broadcast_to(x[None], (32,) + x.shape)
+    took = lax.all_to_all(sent, GROUPS, 0, 0, tiled=True)
+    other = swapped(took, "core")
+    first = lax.axis_index("core") == 0
+    return jnp.where(first, took, other), jnp.where(first, other, took)
+
+
+def _format_first(a_ref, b_ref, one_ref, two_ref):
+    def put(ref):
+        for i in range(16):
+            block = ref[0, i].astype(F32)
+            one_ref[24 * i : 24 * (i + 1), :] = block[:24]
+            two_ref[24 * i : 24 * (i + 1), :] = block[24:48]
+
+    @pl.when(pl.program_id(1) == 0)
+    def _():
+        put(a_ref)
+
+    @pl.when(pl.program_id(1) == 1)
+    def _():
+        put(b_ref)
+
+
+def format_first(a, b):
+    n = a.shape[1]
+    block = pl.BlockSpec((1, 16, n, D), lambda zh, c: (zh, 0, 0, 0))
+    return pl.pallas_call(
+        _format_first,
+        grid=(2, 2),
+        out_shape=(
+            jax.ShapeDtypeStruct((384, FF), F32),
+            jax.ShapeDtypeStruct((FF // 2, D), F32),
+        ),
+        in_specs=[block, block],
+        out_specs=(
+            pl.BlockSpec((384, D), lambda zh, c: (0, zh * 2 + c)),
+            pl.BlockSpec((384, D), lambda zh, c: (c * 2 + zh, 0)),
+        ),
+        compiler_params=pltpu.CompilerParams(vmem_limit_bytes=VMEM_LIMIT),
+        name="format_first",
+    )(a.reshape(2, 16, n, D), b.reshape(2, 16, n, D))
+
+
+def _format_second(a_ref, b_ref, qkv_ref, out_ref):
+    for c, ref in enumerate((a_ref, b_ref)):
+        turned = []
+        for zh in range(2):
+            h = zh * 2 + c
+            for i in range(16):
+                block = ref[zh * 16 + i].astype(F32)[:24]
+                for p in range(3):
+                    at = p * D + h * HW
+                    qkv_ref[24 * i : 24 * (i + 1), at : at + HW] = block[:, p * HW : (p + 1) * HW]
+                turned.append(block[:, 3 * HW :])
+        out_ref[c * HW : (c + 1) * HW, :] = jnp.concatenate(turned, axis=0).T
+
+
+def format_second(a, b):
+    return pl.pallas_call(
+        _format_second,
+        out_shape=(
+            jax.ShapeDtypeStruct((384, 3 * D), F32),
+            jax.ShapeDtypeStruct((384, D), F32),
+        ),
+        in_specs=_specs(2),
+        out_specs=tuple(_specs(2)),
+        compiler_params=pltpu.CompilerParams(vmem_limit_bytes=VMEM_LIMIT),
+        name="format_second",
+    )(a, b)
 
 
 def rotate(x, cosine, sine):
@@ -301,7 +409,7 @@
     team = core * 2 + fsdp
     mine = fsdp * 2 + core
     theirs = (1 - fsdp) * 2 + core
-    swap = [(0, 1), (1, 0)]
+    group = (z * 2 + xh) * 4 + y
 
     def columns(w, which, width):
         return lax.dynamic_slice_in_dim(w, which * width, width, axis=1)
@@ -311,34 +419,30 @@
             [columns(w[:, i * D : (i + 1) * D], which, HW) for i in range(3)], axis=1
         )
 
+    def ordered(keep, other):
+        return (jnp.where(fsdp == 0, keep, other), jnp.where(fsdp == 0, other, keep))
+
     def whole_rows(keep, send):
-        other = lax.ppermute(send, "fsdp", swap)
-        return jnp.where(
-            fsdp == 0, jnp.concatenate([keep, other]), jnp.concatenate([other, keep])
-        )
-
-    x4 = lax.all_gather(tokens, TEAM, axis=0, tiled=True)
+        return jnp.concatenate(ordered(keep, swapped(send, "fsdp")))
+
+    x4 = team_rows(tokens)
     w_q = whole_rows(qkv_columns(w_qkv, mine), qkv_columns(w_qkv, theirs))
-    vectors = lax.all_gather(
-        jnp.concatenate(
-            [ln_gain_attn, ln_bias_attn, ln_gain_mlp, ln_bias_mlp, b_out, b_fc2, b_qkv]
-        ),
-        "fsdp",
-        axis=0,
-        tiled=False,
-    ).astype(F32)
+    dy4 = team_rows(cotangent)
+    vectors = jnp.concatenate(
+        [ln_gain_attn, ln_bias_attn, ln_gain_mlp, ln_bias_mlp, b_out, b_fc2, b_qkv]
+    ).reshape(27, 128)
+    vectors = jnp.stack(ordered(vectors, swapped(vectors, "fsdp"))).astype(F32).reshape(2, -1)
     g_attn, c_attn, g_mlp, c_mlp, bias_out, bias_two = (
         vectors[:, i * 384 : (i + 1) * 384].reshape(D) for i in range(6)
     )
     bias_qkv = vectors[:, 6 * 384 :].reshape(3, 4, HW)
     bias_qkv = lax.dynamic_index_in_dim(bias_qkv, mine, 1, keepdims=False).reshape(3 * HW)
-    dy4 = lax.all_gather(cotangent, TEAM, axis=0, tiled=True)
     w_one = whole_rows(columns(w_fc1, mine, D), columns(w_fc1, theirs, D))
     w_o = lax.dynamic_slice_in_dim(w_out, core * HW, HW, axis=0)
     w_two = lax.dynamic_slice_in_dim(w_fc2, core * D, D, axis=0)
     b_one = lax.dynamic_slice_in_dim(b_fc1, core * D, D, axis=0).astype(F32)
 
-    plan = make_plan(block_order, z, xh, y)
+    plan = make_plan(block_order, team, z, xh, y)
 
     x = x4.astype(F32)
     centred = x - jnp.mean(x, axis=1, keepdims=True)
@@ -349,18 +453,18 @@
 
     qkv = dot(w_q, a_attn, ((0,), (1,))) + bias_qkv[:, None]
     qkv = qkv.reshape(3, NH, HEAD, TEAM_ROWS)
-    group = (z * 2 + xh) * 4 + y
-    anchors = pick(block_order, group * 4 + jnp.arange(4, dtype=jnp.int32))
+    anchors = pick(block_order, group * 4 + (jnp.arange(4, dtype=jnp.int32) ^ team))
     places = (anchors[:, None] * BLK + jnp.arange(BLK, dtype=jnp.int32)[None, :]).reshape(-1)
     frequency = jnp.exp(jnp.arange(ROT // 2, dtype=F32) * (-2.0 * math.log(10000.0) / ROT))
     angles = frequency[:, None] * places.astype(F32)[None, :]
     cosine, sine = jnp.cos(angles), jnp.sin(angles)
     turned = rotate(qkv[:2], cosine, sine).astype(BF)
+    kv = jnp.stack([turned[1], qkv[2].astype(BF)], axis=1).reshape(2 * HW, TEAM_ROWS)
+    kv_all = jnp.stack([kv] + [from_keys(kv, i) for i in range(1, 8)])
     d_mixed = dot(w_o, dy4, ((1,), (1,))).astype(BF).reshape(NH, HEAD, TEAM_ROWS)
     qd = jnp.stack([turned[0] * jnp.asarray(0.125, BF), d_mixed], axis=1)
-    kv = jnp.stack([turned[1], qkv[2].astype(BF)], axis=1)
-    qd_all = lax.all_gather(qd.reshape(2 * HW, TEAM_ROWS), "y", axis=0, tiled=False)
-    kv_all = lax.all_gather(kv.reshape(2 * HW, TEAM_ROWS), KEYS, axis=0, tiled=False)
+    qd = qd.reshape(2 * HW, TEAM_ROWS)
+    qd_all = jnp.stack([qd] + [from_y(qd, i) for i in range(1, 4)])
 
     hidden_pre = dot(a_mlp, w_one, ((1,), (0,))) + b_one
     hidden_act, gelu_pull = jax.vjp(partial(jax.nn.gelu, approximate=False), hidden_pre)
@@ -373,19 +477,35 @@
     grad_b_one = jnp.sum(d_hidden.astype(F32), axis=0)
     dh_mlp = dot(d_hidden, w_one, ((1,), (1,)))
 
+    def row(vectors, width):
+        return jnp.pad(vectors.reshape(32, 1, width).astype(BF), ((0, 0), (0, 0), (0, D - width)))
+
     def summed(parts):
-        took = lax.all_to_all(parts, GROUPS, 0, 0, tiled=True)
-        return jnp.sum(took.astype(F32), axis=0)
-
-    first = summed(
-        jnp.concatenate(
-            [grad_one.astype(BF).reshape(32, 24, D), grad_two.astype(BF).reshape(32, 24, D)], axis=1
-        )
-    ).astype(BF)
+        return jnp.sum(lax.all_to_all(parts, GROUPS, 0, 0, tiled=True).astype(F32), axis=0)
+
+    first = jnp.concatenate(
+        [
+            grad_one.astype(BF).reshape(32, 24, D),
+            grad_two.astype(BF).reshape(32, 24, D),
+            row(
+                jnp.concatenate(
+                    [
+                        jnp.sum(dh_mlp * n, axis=0),
+                        jnp.sum(dh_mlp, axis=0),
+                        jnp.sum(cotangent.astype(F32), axis=0),
+                        grad_b_one,
+                    ]
+                ),
+                96,
+            ),
+        ],
+        axis=1,
+    )
+    first, qd_all, kv_all = lax.optimization_barrier((first, qd_all, kv_all))
+    first = lax.all_to_all(first, GROUPS, 0, 0, tiled=True)
 
     def to_owner(part):
         pairs = []
-        shape = (4, 2)
         for at in range(8):
             zz, f = at // 2, at % 2
             if f == 0 and zz >= 2:
@@ -396,11 +516,10 @@
                 pairs.append((at, at))
         return lax.ppermute(part, ("z", "fsdp"), pairs)
 
-    first = jnp.concatenate([to_owner(first[:24]), first[24:]], axis=0)
-    first_all = lax.all_gather(first, CTX, axis=0, tiled=False)
-
     partial_out = attend_forward(plan, qd_all, kv_all)
-    parts = lax.all_to_all(partial_out, "y", 0, 0, tiled=True).astype(F32)
+    first, partial_out = lax.optimization_barrier((first, partial_out))
+    parts = [partial_out[0]] + [to_y(partial_out[i], i) for i in range(1, 4)]
+    parts = jnp.stack(parts).astype(F32)
     o_parts = parts[:, :HW].reshape(4, NH, HEAD, TEAM_ROWS)
     lse_parts = jnp.sum(parts[:, HW : HW + 3 * NH].reshape(4, NH, 3, TEAM_ROWS), axis=2)
     peak = jnp.max(lse_parts, axis=0)
@@ -411,95 +530,107 @@
     delta = jnp.sum(attended * d_mixed.astype(F32), axis=1)
     mixed = attended.astype(BF).reshape(HW, TEAM_ROWS)
     ld = jnp.concatenate([lse, delta, jnp.zeros((2, TEAM_ROWS), F32)], axis=0)
-    ld_all = lax.all_gather(ld, "y", axis=0, tiled=False)
+    ld_all = jnp.stack([ld] + [from_y(ld, i) for i in range(1, 4)])
+
+    first = jnp.sum(first.astype(F32), axis=0)
+    shares = first[48:]
+    shares = shares + jnp.where(group < 24, swapped(shares, "fsdp"), 0.0)
+    first = jnp.concatenate(
+        [to_owner(first[:24].astype(BF)), first[24:48].astype(BF), shares.astype(BF)], axis=0
+    )
+    first, ld_all = lax.optimization_barrier((first, ld_all))
+    sent = jnp.broadcast_to(first[None], (32,) + first.shape)
+    first = lax.all_to_all(sent, GROUPS, 0, 0, tiled=True)
 
     dq_parts, dkv_parts = attend_backward(plan, qd_all, kv_all, ld_all)
-    dq = jnp.sum(lax.all_to_all(dq_parts, "y", 0, 0, tiled=True).astype(F32), axis=0)
-    dkv = jnp.sum(lax.all_to_all(dkv_parts, KEYS, 0, 0, tiled=True).astype(F32), axis=0)
+    first, dq_parts, dkv_parts = lax.optimization_barrier((first, dq_parts, dkv_parts))
+    dkv = [dkv_parts[0]] + [to_keys(dkv_parts[i], i) for i in range(1, 8)]
+    dq = [dq_parts[0]] + [to_y(dq_parts[i], i) for i in range(1, 4)]
+    other = swapped(first, "core")
+    first_a = jnp.where(core == 0, first, other)
+    first_b = jnp.where(core == 0, other, first)
+    dq = sum(part.astype(F32) for part in dq)
+    dkv = sum(part.astype(F32) for part in dkv)
     dkv = dkv.reshape(NH, 2, HEAD, TEAM_ROWS)
     back = rotate(jnp.stack([dq.reshape(NH, HEAD, TEAM_ROWS), dkv[:, 0]]), cosine, -sine)
     d_qkv = jnp.concatenate([back, dkv[None, :, 1]], axis=0).astype(BF)
     d_qkv = d_qkv.reshape(3 * HW, TEAM_ROWS)
 
-    out_part = out_part + dot(mixed, w_o, ((0,), (0,)))
     grad_qkv = dot(a_attn, d_qkv, ((0,), (1,)))
     grad_out_t = dot(dy4, mixed, ((0,), (1,)))
-    second = summed(
-        jnp.concatenate([grad_qkv.astype(BF), grad_out_t.astype(BF)], axis=1).reshape(32, 24, D)
-    ).astype(BF)
-    second = jnp.concatenate([to_owner(second[:, : 3 * HW]), second[:, 3 * HW :]], axis=1)
-    second_all = lax.all_gather(second, CTX, axis=0, tiled=False)
-
     dh_attn = dot(d_qkv, w_q, ((0,), (1,)))
+    grad_b_qkv = jnp.sum(d_qkv.astype(F32), axis=1).reshape(3, 1, HW)
+    grad_b_qkv = jnp.where(jnp.arange(4, dtype=jnp.int32)[:, None] == mine, grad_b_qkv, 0.0)
+    second = jnp.concatenate(
+        [
+            jnp.concatenate([grad_qkv.astype(BF), grad_out_t.astype(BF)], axis=1).reshape(32, 24, D),
+            row(
+                jnp.concatenate(
+                    [
+                        jnp.sum(dh_attn * n, axis=0),
+                        jnp.sum(dh_attn, axis=0),
+                        grad_b_qkv.reshape(-1),
+                    ]
+                ),
+                120,
+            ),
+        ],
+        axis=1,
+    )
+    second = summed(second)
+    shares = second[24:]
+    shares = shares + swapped(shares, "fsdp")
+    second = jnp.concatenate(
+        [
+            jnp.concatenate(
+                [to_owner(second[:24, : 3 * HW].astype(BF)), second[:24, 3 * HW :].astype(BF)], axis=1
+            ),
+            shares.astype(BF),
+        ],
+        axis=0,
+    )
+    second_a, second_b = to_all_groups(second)
+
+    out_part = out_part + dot(mixed, w_o, ((0,), (0,)))
     dn_part = dh_attn * g_attn + dh_mlp * g_mlp
-    both = jnp.concatenate([out_part.astype(BF), dn_part.astype(BF)], axis=1)
-    both = lax.all_to_all(both.reshape(4, BLK, 2 * D), TEAM, 0, 0, tiled=True)
-    both = jnp.sum(both.astype(F32), axis=0)
-    own = tokens.astype(F32)
+    both = jnp.concatenate([out_part, dn_part], axis=1).reshape(4, BLK, 2 * D)
+    both = both[:2] + swapped(both[2:].astype(BF), "core").astype(F32)
+    both = both[0] + swapped(both[1].astype(BF), "fsdp").astype(F32)
+    own = x[:BLK]
     layer_out = (own + both[:, :D] + bias_out + bias_two).astype(BF)
-    own_centred = own - jnp.mean(own, axis=1, keepdims=True)
-    own_scale = lax.rsqrt(jnp.mean(own_centred * own_centred, axis=1, keepdims=True) + EPS)
-    own_n = own_centred * own_scale
     dn = both[:, D:]
-    grad_tokens = cotangent.astype(F32) + own_scale * (
+    grad_tokens = cotangent.astype(F32) + scale[:BLK] * (
         dn
         - jnp.mean(dn, axis=1, keepdims=True)
-        - own_n * jnp.mean(dn * own_n, axis=1, keepdims=True)
-    )
-
-    def placed(part, width):
-        return jnp.where(
-            jnp.arange(4, dtype=jnp.int32)[:, None] == mine, part.reshape(-1, 1, width), 0.0
-        ).reshape(-1)
-
-    small = jnp.concatenate(
-        [
-            jnp.sum(dh_attn * n, axis=0),
-            jnp.sum(dh_attn, axis=0),
-            jnp.sum(dh_mlp * n, axis=0),
-            jnp.sum(dh_mlp, axis=0),
-            jnp.sum(cotangent.astype(F32), axis=0),
-            placed(jnp.sum(d_qkv.astype(F32), axis=1), HW),
-            placed(grad_b_one, D),
-        ]
-    )
-    small = lax.psum(small, AXES)
-
-    def half(start, width):
-        return lax.dynamic_slice_in_dim(small, start + fsdp * (width // 2), width // 2)
-
-    first_all = first_all.reshape(2, 16, 2, 2, 24, D)
-    second_all = second_all.reshape(2, 16, 2, 24, D)
-    grad_w_one = (
-        first_all[:, :, :, 0].transpose(1, 3, 0, 2, 4).reshape(384, FF).astype(F32)
-    )
-    grad_w_two = (
-        first_all[:, :, :, 1].transpose(2, 0, 1, 3, 4).reshape(FF // 2, D).astype(F32)
-    )
-    grad_w_qkv = (
-        second_all[..., : 3 * HW]
-        .reshape(2, 16, 2, 24, 3, HW)
-        .transpose(1, 3, 4, 0, 2, 5)
-        .reshape(384, 3 * D)
-        .astype(F32)
-    )
-    grad_w_out = (
-        second_all[..., 3 * HW :].transpose(2, 4, 0, 1, 3).reshape(384, D).astype(F32)
-    )
-    grad_b_out = half(4 * D, D)
+        - n[:BLK] * jnp.mean(dn * n[:BLK], axis=1, keepdims=True)
+    )
+
+    grad_w_one, grad_w_two = format_first(first_a, first_b)
+    grad_w_qkv, grad_w_out = format_second(second_a, second_b)
+    tail_a, tail_b = (t[:, 48, :96].astype(F32) for t in (first_a, first_b))
+    early = (tail_a[:24] + tail_b[:24]).reshape(3, D)
+    grad_b_one = jnp.concatenate([tail_a[24:].reshape(D), tail_b[24:].reshape(D)])
+    late = second_a[:, 24, :120].astype(F32) + second_b[:, 24, :120].astype(F32)
+    late = late.reshape(-1)
+
+    def half(vector):
+        width = vector.shape[0] // 2
+        return lax.dynamic_slice_in_dim(vector, fsdp * width, width)
+
+    grad_b_out = half(early[2])
     return (
         layer_out,
         grad_tokens,
-        half(0, D),
-        half(D, D),
-        half(2 * D, D),
-        half(3 * D, D),
+        half(late[:D]),
+        half(late[D : 2 * D]),
+        half(early[0]),
+        half(early[1]),
         grad_w_qkv,
-        half(5 * D, 3 * D),
+        half(late[2 * D :]),
         grad_w_out,
         grad_b_out,
         grad_w_one,
-        half(8 * D, FF),
+        grad_b_one,
         grad_w_two,
         grad_b_out,
     )

time: 617 us -> 527 us (0.85)
  blocking collectives: 128 us -> 0 us
  starting transfers between devices: 49.6 us -> 159 us
  waiting for transfers between devices: 152 us -> 87 us
  other arithmetic: 38.7 us -> 58.3 us
  Pallas kernels: 125 us -> 109 us
  between operations: 14.9 us -> 2.17 us
    ppermute x2 -> x39, starting transfers between devices: 3.18 us -> 105 us  [the longest x13 27 us: swapped(): return lax.ppermute(x, axis, [(0, 1), (1, 0)])]
    all_to_all x5 -> x4, waiting for transfers between devices: 106 us -> 32.4 us  [the longest x1 16.6 us: to_all_groups(): took = lax.all_to_all(sent, GROUPS, 0, 0, tiled=True)]
    psum x1 -> x0, blocking collectives: 64.5 us -> none  [local(): small = lax.psum(small, AXES)]
    all_gather x4 -> x0, blocking collectives: 51.1 us -> none  [the longest x1 17.5 us: local(): x4 = lax.all_gather(tokens, TEAM, axis=0, tiled=True)]
    ppermute x2 -> x39, waiting for transfers between devices: 11.8 us -> 54.7 us  [the longest x7 22.2 us: from_keys(): return lax.ppermute(x, KEYS, [(b, a) for a, b in _key_pairs(i)])]
    convert_element_type x8 -> x2, local copies, waits for them, and re-layouts: 42.5 us -> 0.14 us  [the longest x1 0.1 us: row(): vectors.reshape(32, 1, width).astype(BF)]
    all_gather x4 -> x0, waiting for transfers between devices: 33.5 us -> none  [the longest x1 33.5 us: local(): lax.all_gather(kv.reshape(2 * HW, TEAM_ROWS), KEYS, axis=0, tiled=False)]
    unnamed x130 -> x154, local copies, waits for them, and re-layouts: 9.88 us -> 29.1 us
  transfers between devices with their start and end apart: 13 -> 45, of which waited for: 7 -> 12; matrix products, arithmetic and copies ran while one was open for 15% -> 27% of each run, Pallas kernels for 21% -> 20%
where the time goes in v2:
time: 527 us; the launch traced here: 519 us
  starting transfers between devices  159 us (30%)
  Pallas kernels  109 us (21%)
  waiting for transfers between devices  87 us (17%)
  local copies, waits for them, and re-layouts  78.8 us (15%)
  other arithmetic  58.3 us (11%)
  matrix products  24.9 us (5%)
    pallas_call x1, Pallas kernels, attend_forward(): pl.pallas_call(_forward, out_shape=jax.ShapeDtypeStruct((4, HW + 16, TEAM...  49.5 us
    pallas_call x1, Pallas kernels, attend_backward(): pl.pallas_call(_backward, out_shape=(jax.ShapeDtypeStruct((4, HW, TEAM_RO...  47.4 us
    unnamed x154, local copies, waits for them, and re-layouts  29.1 us
    ppermute x13, starting transfers between devices, swapped(): return lax.ppermute(x, axis, [(0, 1), (1, 0)])  27 us
    ppermute x6, starting transfers between devices, to_y(): return lax.ppermute(x, 'y', [(d, (d + i) % 4) for d in range(4)])  25.4 us
    dot_general x12, matrix products, dot(): return lax.dot_general(a, b, (dims, ((), ())), preferred_element_type=F32)  24.9 us
    ppermute x7, starting transfers between devices, from_keys(): return lax.ppermute(x, KEYS, [(b, a) for a, b in _key_pairs(i)])  24.7 us
    ppermute x7, waiting for transfers between devices, from_keys(): return lax.ppermute(x, KEYS, [(b, a) for a, b in _key_pairs(i)])  22.2 us
  transfers between devices with their start and end apart: 45, of which 12 were waited for; matrix products, arithmetic and copies ran while one was open for 27% of the time, Pallas kernels for 20%

profile of v2, /device:TPU:1, one launch (start us, length us, event | category | flops | bytes accessed | tf_op | source)
XLA Modules:
  0.0 519.0 jit_solution(11118561374983095971)
XLA Ops:
  64.8 3.9 collective-permute-start.11
  70.2 5.0 multiply_convert_fusion
  79.2 4.2 multiply_reduce_fusion.1
  97.5 7.4 %collective-permute-done.12 = bf16[384,512]{1,0:T(8,128)(2,1)S(1)} collective-permute-done((bf16[384,512]{1,0:T(8,128)(2,1)}, bf16[384,512]{1,0:T(8,128)(2,1)S(1)}, u32[]{:S(2)}, u32[]{:S(2)}) %collective-permute-start.12) | collective-permute-done | bytes 393248 | tf_op jit(solution)/shard_map/ppermute | solution.py:292
  106.1 17.3 %collective-permute-start.15 = (bf16[384,512]{1,0:T(8,128)(2,1)}, bf16[384,512]{1,0:T(8,128)(2,1)S(1)}, u32[]{:S(2)}, u32[]{:S(2)}) collective-permute-start(bf16[384,512]{1,0:T(8,128)(2,1)} %bitcast.16), channel_id=1, source_target_pairs={{96,0},{112,16},{0,32},{16,48},{32,64},{48,80},{64,96},{80,112},{9... | collective-permute-start | bytes 1179656 | tf_op jit(solution)/shard_map/ppermute | solution.py:292
  128.0 14.8 %collective-permute-done.15 = bf16[384,512]{1,0:T(8,128)(2,1)S(1)} collective-permute-done((bf16[384,512]{1,0:T(8,128)(2,1)}, bf16[384,512]{1,0:T(8,128)(2,1)S(1)}, u32[]{:S(2)}, u32[]{:S(2)}) %collective-permute-start.15) | collective-permute-done | bytes 393248 | tf_op jit(solution)/shard_map/ppermute | solution.py:292
  144.4 5.3 %all-to-all-start = ((bf16[32,49,768]{2,1,0:T(8,128)(2,1)}), bf16[32,49,768]{2,1,0:T(8,128)(2,1)}, u32[]{:S(2)}, u32[]{:S(2)}) async-start(bf16[32,49,768]{2,1,0:T(8,128)(2,1)} %fusion.2), calls=%async_computation | async-start | bytes 5505024 | tf_op jit(solution)/shard_map/all_to_all | solution.py:505
  153.8 49.5 %attend_forward.1 = bf16[4,208,512]{2,1,0:T(8,128)(2,1)} custom-call(s32[16]{0:T(128)} %get-tuple-element.62.qsrc, s32[16]{0:T(128)} %copy-done.47, s32[32]{0:T(128)} %get-tuple-element.60.ksrc, s32[32]{0:T(128)} %copy-done.48, s32[8]{0:T(128)} %get-tuple-element.131.nfull, s32[8]{0:T(128)} %get-tuple-element.130.nall, ...), custom_call_target="tpu_custom_call" | custom-call | tf_op jit(solution)/shard_map/attend_forward/pallas_call | solution.py:208
  209.7 11.7 %collective-permute-start.19 = (bf16[208,512]{1,0:T(8,128)(2,1)S(1)}, bf16[208,512]{1,0:T(8,128)(2,1)S(1)}, u32[]{:S(2)}, u32[]{:S(2)}) collective-permute-start(bf16[208,512]{1,0:T(8,128)(2,1)S(1)} %get-tuple-element.90), channel_id=1, source_target_pairs={{0,12},{4,0},{8,4},{12,8},{1,13},{5,1},{9,5},{13,9},{2,14},{6,2},{... | collective-permute-start | bytes 638984 | tf_op jit(solution)/shard_map/ppermute | solution.py:280
  222.7 7.1 %collective-permute-done.19 = bf16[208,512]{1,0:T(8,128)(2,1)S(1)} collective-permute-done((bf16[208,512]{1,0:T(8,128)(2,1)S(1)}, bf16[208,512]{1,0:T(8,128)(2,1)S(1)}, u32[]{:S(2)}, u32[]{:S(2)}) %collective-permute-start.19) | collective-permute-done | bytes 213024 | tf_op jit(solution)/shard_map/ppermute | solution.py:280
  229.8 4.2 collective-permute-done.17
  249.2 20.2 %all-to-all-start.1 = ((bf16[32,49,768]{2,1,0:T(8,128)(2,1)}), bf16[32,49,768]{2,1,0:T(8,128)(2,1)}, u32[]{:S(2)}, u32[]{:S(2)}) async-start(bf16[32,49,768]{2,1,0:T(8,128)(2,1)} %broadcast_in_dim.167), calls=%async_computation.1 | async-start | bytes 5505024 | tf_op jit(solution)/shard_map/all_to_all | solution.py:543
  275.2 47.4 %attend_backward.1 = (bf16[4,192,512]{2,1,0:T(8,128)(2,1)}, bf16[8,384,512]{2,1,0:T(8,128)(2,1)}) custom-call(s32[16]{0:T(128)} %get-tuple-element.62.qsrc, s32[16]{0:T(128)} %copy-done.47, s32[32]{0:T(128)} %get-tuple-element.60.ksrc, s32[32]{0:T(128)} %copy-done.48, s32[8]{0:T(128)} %get-tuple-element.131.nfull, s32[8]{0:T(128)} %get-tuple-element.130.nall, ...), custom_call_target="tpu_custom_call" | custom-call | tf_op jit(solution)/shard_map/attend_backward/pallas_call | solution.py:224
  328.0 12.2 %collective-permute-start.27 = (bf16[192,512]{1,0:T(8,128)(2,1)S(1)}, bf16[192,512]{1,0:T(8,128)(2,1)S(1)}, u32[]{:S(2)}, u32[]{:S(2)}) collective-permute-start(bf16[192,512]{1,0:T(8,128)(2,1)S(1)} %get-tuple-element.99), channel_id=1, source_target_pairs={{0,12},{4,0},{8,4},{12,8},{1,13},{5,1},{9,5},{13,9},{2,14},{6,2},{... | collective-permute-start | bytes 589832 | tf_op jit(solution)/shard_map/ppermute | solution.py:280
  341.8 3.1 collective-permute-done.27
  344.9 6.5 %collective-permute-start.32 = (bf16[384,512]{1,0:T(8,128)(2,1)S(1)}, bf16[384,512]{1,0:T(8,128)(2,1)S(1)}, u32[]{:S(2)}, u32[]{:S(2)}) collective-permute-start(bf16[384,512]{1,0:T(8,128)(2,1)S(1)} %get-tuple-element.75), channel_id=1, source_target_pairs={{0,80},{16,64},{32,112},{48,96},{64,16},{80,0},{96,48},{112,32},{1... | collective-permute-start | bytes 1179656 | tf_op jit(solution)/shard_map/ppermute | solution.py:296
  351.4 7.6 %collective-permute-start.31 = (bf16[384,512]{1,0:T(8,128)(2,1)S(1)}, bf16[384,512]{1,0:T(8,128)(2,1)S(1)}, u32[]{:S(2)}, u32[]{:S(2)}) collective-permute-start(bf16[384,512]{1,0:T(8,128)(2,1)S(1)} %get-tuple-element.76), channel_id=1, source_target_pairs={{0,64},{16,80},{32,96},{48,112},{64,0},{80,16},{96,32},{112,48},{1... | collective-permute-start | bytes 1179656 | tf_op jit(solution)/shard_map/ppermute | solution.py:296
  362.5 3.7 copy.87
  366.4 7.2 %collective-permute-start.40 = (bf16[32,49,768]{2,0,1:T(8,128)(2,1)}, bf16[32,49,768]{2,0,1:T(8,128)(2,1)}, u32[]{:S(2)}, u32[]{:S(2)}) collective-permute-start(bf16[32,49,768]{2,0,1:T(8,128)(2,1)} %copy.87), channel_id=1, source_target_pairs={{0,2},{2,0},{1,3},{3,1},{4,6},{6,4},{5,7},{7,5},{8,10},{10,8},{9,1... | collective-permute-start | bytes 7225352 | tf_op jit(solution)/shard_map/ppermute | solution.py:300
  373.5 8.2 %collective-permute-done.31 = bf16[384,512]{1,0:T(8,128)(2,1)S(1)} collective-permute-done((bf16[384,512]{1,0:T(8,128)(2,1)S(1)}, bf16[384,512]{1,0:T(8,128)(2,1)S(1)}, u32[]{:S(2)}, u32[]{:S(2)}) %collective-permute-start.31) | collective-permute-done | bytes 393248 | tf_op jit(solution)/shard_map/ppermute | solution.py:296
  381.7 8.4 %collective-permute-done.29 = bf16[384,512]{1,0:T(8,128)(2,1)S(1)} collective-permute-done((bf16[384,512]{1,0:T(8,128)(2,1)S(1)}, bf16[384,512]{1,0:T(8,128)(2,1)S(1)}, u32[]{:S(2)}, u32[]{:S(2)}) %collective-permute-start.29) | collective-permute-done | bytes 393248 | tf_op jit(solution)/shard_map/ppermute | solution.py:296
  404.5 12.1 %all-to-all-start.2 = ((bf16[32,25,768]{2,1,0:T(8,128)(2,1)}), bf16[32,25,768]{2,1,0:T(8,128)(2,1)}, u32[]{:S(2)}, u32[]{:S(2)}) async-start(bf16[32,25,768]{2,1,0:T(8,128)(2,1)} %fusion.4), calls=%async_computation.2 | async-start | bytes 3145728 | tf_op jit(solution)/shard_map/all_to_all | solution.py:484
  420.7 3.1 collective-permute-start.36
  423.9 15.8 %all-to-all-done.2 = bf16[32,25,768]{2,1,0:T(8,128)(2,1)} async-done(((bf16[32,25,768]{2,1,0:T(8,128)(2,1)}), bf16[32,25,768]{2,1,0:T(8,128)(2,1)}, u32[]{:S(2)}, u32[]{:S(2)}) %all-to-all-start.2) | async-done | bytes 1228832 | tf_op jit(solution)/shard_map/all_to_all | solution.py:484
  441.3 3.1 collective-permute-start.38
  448.0 13.6 %all-to-all-start.3 = ((bf16[32,25,768]{2,1,0:T(8,128)(2,1)}), bf16[32,25,768]{2,1,0:T(8,128)(2,1)}, u32[]{:S(2)}, u32[]{:S(2)}) async-start(bf16[32,25,768]{2,1,0:T(8,128)(2,1)} %broadcast_in_dim.172), calls=%async_computation.3 | async-start | bytes 3145728 | tf_op jit(solution)/shard_map/all_to_all | solution.py:310
  465.6 16.6 %all-to-all-done.3 = bf16[32,25,768]{2,1,0:T(8,128)(2,1)} async-done(((bf16[32,25,768]{2,1,0:T(8,128)(2,1)}), bf16[32,25,768]{2,1,0:T(8,128)(2,1)}, u32[]{:S(2)}, u32[]{:S(2)}) %all-to-all-start.3) | async-done | bytes 1228832 | tf_op jit(solution)/shard_map/all_to_all | solution.py:310
  482.2 3.2 copy.84
  485.4 4.1 collective-permute-start.39
  489.6 5.2 %broadcast_select_fusion.1 = (bf16[32,49,768]{2,1,0:T(8,128)(2,1)S(1)}, bf16[32,49,768]{2,1,0:T(8,128)(2,1)S(1)}) fusion(bf16[32,49,768]{2,1,0:T(8,128)(2,1)} %all-to-all-done.1, pred[]{:T(512)S(6)} %eq.111, bf16[32,49,768]{2,0,1:T(8,128)(2,1)} %collective-permute-done.40), kind=kLoop, calls=%fused_computation.10 | loop fusion | flops 2408448 | bytes 9633793 | tf_op jit(solution)/shard_map/jit(_where)/select_n | solution.py:550
  499.1 7.7 %format_first.1 = (f32[384,3072]{1,0:T(8,128)}, f32[1536,768]{1,0:T(8,128)}) custom-call(bf16[2,16,49,768]{3,2,1,0:T(8,128)(2,1)} %bitcast.122, bf16[2,16,49,768]{3,2,1,0:T(8,128)(2,1)} %bitcast.123), custom_call_target="tpu_custom_call" | custom-call | tf_op jit(solution)/shard_map/format_first/pallas_call | solution.py:335
  511.6 4.5 format_second.1
  (388 shorter events, 172.6 us)
Async XLA Ops:
  0.7 44.1 %collective-permute-start = (bf16[128,768]{1,0:T(8,128)(2,1)}, bf16[128,768]{1,0:T(8,128)(2,1)S(1)}, u32[]{:S(2)}, u32[]{:S(2)}) collective-permute-start(bf16[128,768]{1,0:T(8,128)(2,1)} %param.15), channel_id=1, source_target_pairs={{0,1},{1,0},{2,3},{3,2},{4,5},{5,4},{6,7},{7,6},{8,9},{9,8},{10,11... | collective-permute-start | bytes 589832 | tf_op jit(solution)/shard_map/ppermute | solution.py:300
  4.7 60.1 %collective-permute-start.3 = (bf16[384,768]{1,0:T(8,128)(2,1)}, bf16[384,768]{1,0:T(8,128)(2,1)}, u32[]{:S(2)}, u32[]{:S(2)}) collective-permute-start(bf16[384,768]{1,0:T(8,128)(2,1)} %constant_dynamic-slice_fusion.6), channel_id=1, source_target_pairs={{0,1},{1,0},{2,3},{3,2},{4,5},{5,4},{6,7},{7,6},{8,9},{9,8},{10,11... | collective-permute-start | bytes 1769480 | tf_op jit(solution)/shard_map/ppermute | solution.py:300
  14.9 17.4 %collective-permute-start.2 = (bf16[27,128]{1,0:T(8,128)(2,1)}, bf16[27,128]{1,0:T(8,128)(2,1)}, u32[]{:S(2)}, u32[]{:S(2)}) collective-permute-start(bf16[27,128]{1,0:T(8,128)(2,1)} %bitcast), channel_id=1, source_target_pairs={{0,1},{1,0},{2,3},{3,2},{4,5},{5,4},{6,7},{7,6},{8,9},{9,8},{10,11... | collective-permute-start | bytes 20744 | tf_op jit(solution)/shard_map/ppermute | solution.py:300
  16.2 31.4 %collective-permute-start.4 = (bf16[128,768]{1,0:T(8,128)(2,1)}, bf16[128,768]{1,0:T(8,128)(2,1)}, u32[]{:S(2)}, u32[]{:S(2)}) collective-permute-start(bf16[128,768]{1,0:T(8,128)(2,1)} %param.17), channel_id=1, source_target_pairs={{0,1},{1,0},{2,3},{3,2},{4,5},{5,4},{6,7},{7,6},{8,9},{9,8},{10,11... | collective-permute-start | bytes 589832 | tf_op jit(solution)/shard_map/ppermute | solution.py:300
  23.9 25.8 %collective-permute-start.6 = (bf16[384,576]{1,0:T(8,128)(2,1)}, bf16[384,576]{1,0:T(8,128)(2,1)}, u32[]{:S(2)}, u32[]{:S(2)}) collective-permute-start(bf16[384,576]{1,0:T(8,128)(2,1)} %pad_maximum_fusion.11), channel_id=1, source_target_pairs={{0,1},{1,0},{2,3},{3,2},{4,5},{5,4},{6,7},{7,6},{8,9},{9,8},{10,11... | collective-permute-start | bytes 1327112 | tf_op jit(solution)/shard_map/ppermute | solution.py:300
  56.5 68.8 %collective-permute-start.9 = (bf16[384,512]{1,0:T(8,128)(2,1)}, bf16[384,512]{1,0:T(8,128)(2,1)}, u32[]{:S(2)}, u32[]{:S(2)}) collective-permute-start(bf16[384,512]{1,0:T(8,128)(2,1)} %bitcast.8), channel_id=1, source_target_pairs={{12,0},{0,4},{4,8},{8,12},{13,1},{1,5},{5,9},{9,13},{14,2},{2,6},{... | collective-permute-start | bytes 1179656 | tf_op jit(solution)/shard_map/ppermute | solution.py:276
  57.8 67.5 %collective-permute-start.8 = (bf16[384,512]{1,0:T(8,128)(2,1)}, bf16[384,512]{1,0:T(8,128)(2,1)}, u32[]{:S(2)}, u32[]{:S(2)}) collective-permute-start(bf16[384,512]{1,0:T(8,128)(2,1)} %bitcast.8), channel_id=1, source_target_pairs={{8,0},{12,4},{0,8},{4,12},{9,1},{13,5},{1,9},{5,13},{10,2},{14,6},... | collective-permute-start | bytes 1179656 | tf_op jit(solution)/shard_map/ppermute | solution.py:276
  60.4 64.9 %collective-permute-start.7 = (bf16[384,512]{1,0:T(8,128)(2,1)}, bf16[384,512]{1,0:T(8,128)(2,1)}, u32[]{:S(2)}, u32[]{:S(2)}) collective-permute-start(bf16[384,512]{1,0:T(8,128)(2,1)} %bitcast.8), channel_id=1, source_target_pairs={{4,0},{8,4},{12,8},{0,12},{5,1},{9,5},{13,9},{1,13},{6,2},{10,6},{... | collective-permute-start | bytes 1179656 | tf_op jit(solution)/shard_map/ppermute | solution.py:276
  62.3 31.3 %collective-permute-start.10 = (bf16[384,512]{1,0:T(8,128)(2,1)}, bf16[384,512]{1,0:T(8,128)(2,1)}, u32[]{:S(2)}, u32[]{:S(2)}) collective-permute-start(bf16[384,512]{1,0:T(8,128)(2,1)} %bitcast.16), channel_id=1, source_target_pairs={{16,0},{0,16},{48,32},{32,48},{80,64},{64,80},{112,96},{96,112},{1... | collective-permute-start | bytes 1179656 | tf_op jit(solution)/shard_map/ppermute | solution.py:292
  64.8 31.0 %collective-permute-start.11 = (bf16[384,512]{1,0:T(8,128)(2,1)}, bf16[384,512]{1,0:T(8,128)(2,1)}, u32[]{:S(2)}, u32[]{:S(2)}) collective-permute-start(bf16[384,512]{1,0:T(8,128)(2,1)} %bitcast.16), channel_id=1, source_target_pairs={{32,0},{48,16},{64,32},{80,48},{96,64},{112,80},{0,96},{16,112},{3... | collective-permute-start | bytes 1179656 | tf_op jit(solution)/shard_map/ppermute | solution.py:292
  105.0 19.2 %collective-permute-start.14 = (bf16[384,512]{1,0:T(8,128)(2,1)}, bf16[384,512]{1,0:T(8,128)(2,1)S(1)}, u32[]{:S(2)}, u32[]{:S(2)}) collective-permute-start(bf16[384,512]{1,0:T(8,128)(2,1)} %bitcast.16), channel_id=1, source_target_pairs={{80,0},{64,16},{112,32},{96,48},{16,64},{0,80},{48,96},{32,112},{8... | collective-permute-start | bytes 1179656 | tf_op jit(solution)/shard_map/ppermute | solution.py:292
  106.1 36.8 %collective-permute-start.15 = (bf16[384,512]{1,0:T(8,128)(2,1)}, bf16[384,512]{1,0:T(8,128)(2,1)S(1)}, u32[]{:S(2)}, u32[]{:S(2)}) collective-permute-start(bf16[384,512]{1,0:T(8,128)(2,1)} %bitcast.16), channel_id=1, source_target_pairs={{96,0},{112,16},{0,32},{16,48},{32,64},{48,80},{64,96},{80,112},{9... | collective-permute-start | bytes 1179656 | tf_op jit(solution)/shard_map/ppermute | solution.py:292
  124.2 19.4 %collective-permute-start.16 = (bf16[384,512]{1,0:T(8,128)(2,1)}, bf16[384,512]{1,0:T(8,128)(2,1)S(1)}, u32[]{:S(2)}, u32[]{:S(2)}) collective-permute-start(bf16[384,512]{1,0:T(8,128)(2,1)} %bitcast.16), channel_id=1, source_target_pairs={{112,0},{96,16},{16,32},{0,48},{48,64},{32,80},{80,96},{64,112},{1... | collective-permute-start | bytes 1179656 | tf_op jit(solution)/shard_map/ppermute | solution.py:292
  144.4 58.9 %all-to-all-start = ((bf16[32,49,768]{2,1,0:T(8,128)(2,1)}), bf16[32,49,768]{2,1,0:T(8,128)(2,1)}, u32[]{:S(2)}, u32[]{:S(2)}) async-start(bf16[32,49,768]{2,1,0:T(8,128)(2,1)} %fusion.2), calls=%async_computation | async-start | bytes 5505024 | tf_op jit(solution)/shard_map/all_to_all | solution.py:505
  207.6 37.0 %collective-permute-start.20 = (bf16[24,768]{1,0:T(8,128)(2,1)}, bf16[24,768]{1,0:T(8,128)(2,1)}, u32[]{:S(2)}, u32[]{:S(2)}) collective-permute-start(bf16[24,768]{1,0:T(8,128)(2,1)} %get-tuple-element.111), channel_id=1, source_target_pairs={{0,0},{1,64},{32,32},{33,96},{64,1},{65,65},{96,33},{97,97},{2,2},... | collective-permute-start | bytes 110600 | tf_op jit(solution)/shard_map/ppermute | solution.py:517
  209.7 20.0 %collective-permute-start.19 = (bf16[208,512]{1,0:T(8,128)(2,1)S(1)}, bf16[208,512]{1,0:T(8,128)(2,1)S(1)}, u32[]{:S(2)}, u32[]{:S(2)}) collective-permute-start(bf16[208,512]{1,0:T(8,128)(2,1)S(1)} %get-tuple-element.90), channel_id=1, source_target_pairs={{0,12},{4,0},{8,4},{12,8},{1,13},{5,1},{9,5},{13,9},{2,14},{6,2},{... | collective-permute-start | bytes 638984 | tf_op jit(solution)/shard_map/ppermute | solution.py:280
  249.2 73.4 %all-to-all-start.1 = ((bf16[32,49,768]{2,1,0:T(8,128)(2,1)}), bf16[32,49,768]{2,1,0:T(8,128)(2,1)}, u32[]{:S(2)}, u32[]{:S(2)}) async-start(bf16[32,49,768]{2,1,0:T(8,128)(2,1)} %broadcast_in_dim.167), calls=%async_computation.1 | async-start | bytes 5505024 | tf_op jit(solution)/shard_map/all_to_all | solution.py:543
  324.7 34.3 %collective-permute-start.34 = (bf16[384,512]{1,0:T(8,128)(2,1)S(1)}, bf16[384,512]{1,0:T(8,128)(2,1)S(1)}, u32[]{:S(2)}, u32[]{:S(2)}) collective-permute-start(bf16[384,512]{1,0:T(8,128)(2,1)S(1)} %get-tuple-element.73), channel_id=1, source_target_pairs={{0,112},{16,96},{32,16},{48,0},{64,48},{80,32},{96,80},{112,64},{1... | collective-permute-start | bytes 1179656 | tf_op jit(solution)/shard_map/ppermute | solution.py:296
  325.2 35.4 %collective-permute-start.33 = (bf16[384,512]{1,0:T(8,128)(2,1)S(1)}, bf16[384,512]{1,0:T(8,128)(2,1)S(1)}, u32[]{:S(2)}, u32[]{:S(2)}) collective-permute-start(bf16[384,512]{1,0:T(8,128)(2,1)S(1)} %get-tuple-element.74), channel_id=1, source_target_pairs={{0,96},{16,112},{32,0},{48,16},{64,32},{80,48},{96,64},{112,80},{1... | collective-permute-start | bytes 1179656 | tf_op jit(solution)/shard_map/ppermute | solution.py:296
  328.0 16.9 %collective-permute-start.27 = (bf16[192,512]{1,0:T(8,128)(2,1)S(1)}, bf16[192,512]{1,0:T(8,128)(2,1)S(1)}, u32[]{:S(2)}, u32[]{:S(2)}) collective-permute-start(bf16[192,512]{1,0:T(8,128)(2,1)S(1)} %get-tuple-element.99), channel_id=1, source_target_pairs={{0,12},{4,0},{8,4},{12,8},{1,13},{5,1},{9,5},{13,9},{2,14},{6,2},{... | collective-permute-start | bytes 589832 | tf_op jit(solution)/shard_map/ppermute | solution.py:280
  340.7 18.3 %collective-permute-start.25 = (bf16[192,512]{1,0:T(8,128)(2,1)S(1)}, bf16[192,512]{1,0:T(8,128)(2,1)S(1)}, u32[]{:S(2)}, u32[]{:S(2)}) collective-permute-start(bf16[192,512]{1,0:T(8,128)(2,1)S(1)} %get-tuple-element.98), channel_id=1, source_target_pairs={{0,4},{4,8},{8,12},{12,0},{1,5},{5,9},{9,13},{13,1},{2,6},{6,10},{... | collective-permute-start | bytes 589832 | tf_op jit(solution)/shard_map/ppermute | solution.py:280
  344.9 21.5 %collective-permute-start.32 = (bf16[384,512]{1,0:T(8,128)(2,1)S(1)}, bf16[384,512]{1,0:T(8,128)(2,1)S(1)}, u32[]{:S(2)}, u32[]{:S(2)}) collective-permute-start(bf16[384,512]{1,0:T(8,128)(2,1)S(1)} %get-tuple-element.75), channel_id=1, source_target_pairs={{0,80},{16,64},{32,112},{48,96},{64,16},{80,0},{96,48},{112,32},{1... | collective-permute-start | bytes 1179656 | tf_op jit(solution)/shard_map/ppermute | solution.py:296
  351.4 30.3 %collective-permute-start.31 = (bf16[384,512]{1,0:T(8,128)(2,1)S(1)}, bf16[384,512]{1,0:T(8,128)(2,1)S(1)}, u32[]{:S(2)}, u32[]{:S(2)}) collective-permute-start(bf16[384,512]{1,0:T(8,128)(2,1)S(1)} %get-tuple-element.76), channel_id=1, source_target_pairs={{0,64},{16,80},{32,96},{48,112},{64,0},{80,16},{96,32},{112,48},{1... | collective-permute-start | bytes 1179656 | tf_op jit(solution)/shard_map/ppermute | solution.py:296
  359.0 22.7 %collective-permute-start.30 = (bf16[384,512]{1,0:T(8,128)(2,1)S(1)}, bf16[384,512]{1,0:T(8,128)(2,1)S(1)}, u32[]{:S(2)}, u32[]{:S(2)}) collective-permute-start(bf16[384,512]{1,0:T(8,128)(2,1)S(1)} %get-tuple-element.77), channel_id=1, source_target_pairs={{0,48},{16,32},{32,80},{48,64},{64,112},{80,96},{96,16},{112,0},{1... | collective-permute-start | bytes 1179656 | tf_op jit(solution)/shard_map/ppermute | solution.py:296
  359.0 31.1 %collective-permute-start.29 = (bf16[384,512]{1,0:T(8,128)(2,1)S(1)}, bf16[384,512]{1,0:T(8,128)(2,1)S(1)}, u32[]{:S(2)}, u32[]{:S(2)}) collective-permute-start(bf16[384,512]{1,0:T(8,128)(2,1)S(1)} %get-tuple-element.78), channel_id=1, source_target_pairs={{0,32},{16,48},{32,64},{48,80},{64,96},{80,112},{96,0},{112,16},{1... | collective-permute-start | bytes 1179656 | tf_op jit(solution)/shard_map/ppermute | solution.py:296
  360.7 29.4 %collective-permute-start.28 = (bf16[384,512]{1,0:T(8,128)(2,1)S(1)}, bf16[384,512]{1,0:T(8,128)(2,1)S(1)}, u32[]{:S(2)}, u32[]{:S(2)}) collective-permute-start(bf16[384,512]{1,0:T(8,128)(2,1)S(1)} %get-tuple-element.72), channel_id=1, source_target_pairs={{0,16},{16,0},{32,48},{48,32},{64,80},{80,64},{96,112},{112,96},{1... | collective-permute-start | bytes 1179656 | tf_op jit(solution)/shard_map/ppermute | solution.py:296
  366.4 123.2 %collective-permute-start.40 = (bf16[32,49,768]{2,0,1:T(8,128)(2,1)}, bf16[32,49,768]{2,0,1:T(8,128)(2,1)}, u32[]{:S(2)}, u32[]{:S(2)}) collective-permute-start(bf16[32,49,768]{2,0,1:T(8,128)(2,1)} %copy.87), channel_id=1, source_target_pairs={{0,2},{2,0},{1,3},{3,1},{4,6},{6,4},{5,7},{7,5},{8,10},{10,8},{9,1... | collective-permute-start | bytes 7225352 | tf_op jit(solution)/shard_map/ppermute | solution.py:300
  397.3 20.8 %collective-permute-start.35 = (bf16[2,128,1536]{2,1,0:T(8,128)(2,1)}, bf16[2,128,1536]{2,1,0:T(8,128)(2,1)}, u32[]{:S(2)}, u32[]{:S(2)}) collective-permute-start(bf16[2,128,1536]{2,1,0:T(8,128)(2,1)} %bitcast.55), channel_id=1, source_target_pairs={{0,2},{2,0},{1,3},{3,1},{4,6},{6,4},{5,7},{7,5},{8,10},{10,8},{9,1... | collective-permute-start | bytes 2359304 | tf_op jit(solution)/shard_map/ppermute | solution.py:300
  404.5 35.1 %all-to-all-start.2 = ((bf16[32,25,768]{2,1,0:T(8,128)(2,1)}), bf16[32,25,768]{2,1,0:T(8,128)(2,1)}, u32[]{:S(2)}, u32[]{:S(2)}) async-start(bf16[32,25,768]{2,1,0:T(8,128)(2,1)} %fusion.4), calls=%async_computation.2 | async-start | bytes 3145728 | tf_op jit(solution)/shard_map/all_to_all | solution.py:484
  420.7 41.0 %collective-permute-start.36 = (bf16[128,1536]{1,0:T(8,128)(2,1)S(1)}, bf16[128,1536]{1,0:T(8,128)(2,1)}, u32[]{:S(2)}, u32[]{:S(2)}) collective-permute-start(bf16[128,1536]{1,0:T(8,128)(2,1)S(1)} %fusion.30), channel_id=1, source_target_pairs={{0,1},{1,0},{2,3},{3,2},{4,5},{5,4},{6,7},{7,6},{8,9},{9,8},{10,11... | collective-permute-start | bytes 1179656 | tf_op jit(solution)/shard_map/ppermute | solution.py:300
  448.0 34.2 %all-to-all-start.3 = ((bf16[32,25,768]{2,1,0:T(8,128)(2,1)}), bf16[32,25,768]{2,1,0:T(8,128)(2,1)}, u32[]{:S(2)}, u32[]{:S(2)}) async-start(bf16[32,25,768]{2,1,0:T(8,128)(2,1)} %broadcast_in_dim.172), calls=%async_computation.3 | async-start | bytes 3145728 | tf_op jit(solution)/shard_map/all_to_all | solution.py:310
  485.4 22.0 %collective-permute-start.39 = (bf16[32,25,768]{2,0,1:T(8,128)(2,1)}, bf16[32,25,768]{2,0,1:T(8,128)(2,1)}, u32[]{:S(2)}, u32[]{:S(2)}) collective-permute-start(bf16[32,25,768]{2,0,1:T(8,128)(2,1)} %copy.84), channel_id=1, source_target_pairs={{0,2},{2,0},{1,3},{3,1},{4,6},{6,4},{5,7},{7,5},{8,10},{10,8},{9,1... | collective-permute-start | bytes 3686408 | tf_op jit(solution)/shard_map/ppermute | solution.py:300
  (83 other events, 644.4 us)

commit v3 on v2

--- a/solution.py
+++ b/solution.py
@@ -25,14 +25,19 @@
 KEYS = ("z", "xh")
 GROUPS = ("z", "xh", "y")
 
-NH = 3
-HW = NH * HEAD
+NH = 1
+TH = 3
+HW = TH * HEAD
+KW = NH * HEAD
 TEAM_ROWS = 512
 NQ = 16
 NK = 32
 QT = 2
+FQT = 4
 CH = 4
-NT = NQ // QT
+PAIR = 2
+FPAIR = 2
+UNROLL = 4
 BF = jnp.bfloat16
 F32 = jnp.float32
 VMEM_LIMIT = 56 * 1024 * 1024
@@ -49,43 +54,43 @@
             kn[h, pl.ds(to, BLK), :] = blk[2 * HEAD * h : 2 * HEAD * (h + 1)].T
         return 0
 
-    lax.fori_loop(0, NK, step, 0)
-
-
-def _tile_columns(ref, qsrc, t, rows):
+    lax.fori_loop(0, NK, step, 0, unroll=UNROLL)
+
+
+def _tile_columns(ref, qsrc, t, rows, qt):
     parts = []
-    for i in range(QT):
-        src = qsrc[t * QT + i]
+    for i in range(qt):
+        src = qsrc[t * qt + i]
         at = pl.multiple_of((src % 4) * BLK, BLK)
         parts.append(ref[src // 4, rows, pl.ds(at, BLK)])
     return jnp.concatenate(parts, axis=1)
 
 
-def _allowed(kpos, qpos, t, c):
-    row = lax.broadcasted_iota(jnp.int32, (BLK, QT * BLK), 0)
+def _allowed(kpos, qpos, t, c, qt):
+    row = lax.broadcasted_iota(jnp.int32, (BLK, qt * BLK), 0)
     col = lax.broadcasted_iota(jnp.int32, (BLK, BLK), 1)
-    query = jnp.concatenate([qpos[t * QT + i] * BLK + col for i in range(QT)], axis=1)
+    query = jnp.concatenate([qpos[t * qt + i] * BLK + col for i in range(qt)], axis=1)
     return jnp.concatenate([kpos[c * CH + i] * BLK + row <= query for i in range(CH)], axis=0)
 
 
 def _forward(qsrc, qpos, ksrc, kpos, nfull, nall, qd_ref, kv_ref, o_ref, kvt, kn):
     _sort_keys(kv_ref, ksrc, kvt, kn)
-    width = QT * BLK
-    rows = CH * BLK
+    width = FQT * BLK
 
     def tile(t, _):
-        blk = _tile_columns(qd_ref, qsrc, t, slice(None))
+        blk = _tile_columns(qd_ref, qsrc, t, slice(None), FQT)
         half = lax.broadcasted_iota(jnp.int32, (2 * HEAD, width), 0) < HEAD
         zero = jnp.zeros((2 * HEAD, width), BF)
         queries = [
             jnp.where(half, blk[2 * HEAD * h : 2 * HEAD * (h + 1)], zero) for h in range(NH)
         ]
 
-        def chunk(masked, c, carry):
+        def chunk(masked, step, c, carry):
+            rows = step * CH * BLK
             at = pl.multiple_of(c * rows, rows)
             out = []
             if masked:
-                ok = _allowed(kpos, qpos, t, c)
+                ok = _allowed(kpos, qpos, t, c, FQT)
             for h in range(NH):
                 m, l, acc = carry[h]
                 s = jnp.dot(kn[h, pl.ds(at, rows), :], queries[h], preferred_element_type=F32)
@@ -108,8 +113,10 @@
             )
             for _ in range(NH)
         )
-        state = lax.fori_loop(0, nfull[t], partial(chunk, False), start)
-        state = lax.fori_loop(nfull[t], nall[t], partial(chunk, True), state)
+        wide = nfull[t] // FPAIR
+        state = lax.fori_loop(0, wide, partial(chunk, False, FPAIR), start)
+        state = lax.fori_loop(wide * FPAIR, nfull[t], partial(chunk, False, 1), state)
+        state = lax.fori_loop(nfull[t], nall[t], partial(chunk, True, 1), state)
         stats = []
         for h in range(NH):
             m, l, acc = state[h]
@@ -122,18 +129,18 @@
             mid = rest.astype(BF)
             low = (rest - mid.astype(F32)).astype(BF)
             stats += [hi.astype(F32), mid.astype(F32), low.astype(F32)]
-            for i in range(QT):
-                src = qsrc[t * QT + i]
+            for i in range(FQT):
+                src = qsrc[t * FQT + i]
                 at = pl.multiple_of((src % 4) * BLK, BLK)
                 o_ref[src // 4, HEAD * h : HEAD * (h + 1), pl.ds(at, BLK)] = o[:, i * BLK : (i + 1) * BLK]
         stats = jnp.concatenate(stats + [jnp.zeros((16 - 3 * NH, width), F32)], axis=0).astype(BF)
-        for i in range(QT):
-            src = qsrc[t * QT + i]
+        for i in range(FQT):
+            src = qsrc[t * FQT + i]
             at = pl.multiple_of((src % 4) * BLK, BLK)
-            o_ref[src // 4, HW : HW + 16, pl.ds(at, BLK)] = stats[:, i * BLK : (i + 1) * BLK]
+            o_ref[src // 4, KW : KW + 16, pl.ds(at, BLK)] = stats[:, i * BLK : (i + 1) * BLK]
         return 0
 
-    lax.fori_loop(0, NT, tile, 0)
+    lax.fori_loop(0, NQ // FQT, tile, 0)
 
 
 def _backward(
@@ -141,12 +148,11 @@
 ):
     _sort_keys(kv_ref, ksrc, kvt, kn)
     width = QT * BLK
-    rows = CH * BLK
     acc[...] = jnp.zeros_like(acc)
 
     def tile(t, _):
-        blk = _tile_columns(qd_ref, qsrc, t, slice(None))
-        stats = _tile_columns(ld_ref, qsrc, t, slice(None))
+        blk = _tile_columns(qd_ref, qsrc, t, slice(None), QT)
+        stats = _tile_columns(ld_ref, qsrc, t, slice(None), QT)
         top = lax.broadcasted_iota(jnp.int32, (2 * HEAD, width), 0) < HEAD
         left = lax.broadcasted_iota(jnp.int32, (width, 2 * HEAD), 1) < HEAD
         zero = jnp.zeros((2 * HEAD, width), BF)
@@ -160,10 +166,11 @@
             w2[h, width:, :] = jnp.where(left, zero_t, turned)
         dq[...] = jnp.zeros_like(dq)
 
-        def chunk(masked, c, _):
+        def chunk(masked, step, c, _):
+            rows = step * CH * BLK
             at = pl.multiple_of(c * rows, rows)
             if masked:
-                ok = _allowed(kpos, qpos, t, c)
+                ok = _allowed(kpos, qpos, t, c, QT)
             for h in range(NH):
                 sd = jnp.dot(kn[h, pl.ds(at, rows), :], w1[h], preferred_element_type=F32)
                 s = sd[:, :width]
@@ -177,8 +184,10 @@
                 dq[h] += jnp.dot(k, ds, preferred_element_type=F32)
             return 0
 
-        lax.fori_loop(0, nfull[t], partial(chunk, False), 0)
-        lax.fori_loop(nfull[t], nall[t], partial(chunk, True), 0)
+        wide = nfull[t] // PAIR
+        lax.fori_loop(0, wide, partial(chunk, False, PAIR), 0)
+        lax.fori_loop(wide * PAIR, nfull[t], partial(chunk, False, 1), 0)
+        lax.fori_loop(nfull[t], nall[t], partial(chunk, True, 1), 0)
         for h in range(NH):
             out = (dq[h] * 0.125).astype(BF)
             for i in range(QT):
@@ -187,7 +196,7 @@
                 dq_ref[src // 4, HEAD * h : HEAD * (h + 1), pl.ds(at, BLK)] = out[:, i * BLK : (i + 1) * BLK]
         return 0
 
-    lax.fori_loop(0, NT, tile, 0)
+    lax.fori_loop(0, NQ // QT, tile, 0)
 
     def back(r, _):
         src = ksrc[r]
@@ -197,7 +206,7 @@
             dkv_ref[src // 4, 2 * HEAD * h : 2 * HEAD * (h + 1), pl.ds(at, BLK)] = part
         return 0
 
-    lax.fori_loop(0, NK, back, 0)
+    lax.fori_loop(0, NK, back, 0, unroll=UNROLL)
 
 
 def _specs(n):
@@ -207,14 +216,15 @@
 def attend_forward(plan, qd, kv):
     return pl.pallas_call(
         _forward,
-        out_shape=jax.ShapeDtypeStruct((4, HW + 16, TEAM_ROWS), BF),
+        out_shape=jax.ShapeDtypeStruct((4, KW + 16, TEAM_ROWS), BF),
         in_specs=[pl.BlockSpec(memory_space=pltpu.SMEM)] * 6 + _specs(2),
         out_specs=pl.BlockSpec(memory_space=pltpu.VMEM),
         scratch_shapes=[
-            pltpu.VMEM((2 * HW, NK * BLK), BF),
+            pltpu.VMEM((2 * KW, NK * BLK), BF),
             pltpu.VMEM((NH, NK * BLK, 2 * HEAD), BF),
         ],
         compiler_params=pltpu.CompilerParams(vmem_limit_bytes=VMEM_LIMIT),
+        cost_estimate=pl.CostEstimate(flops=4 * NH * NQ * NK * BLK * BLK * HEAD, bytes_accessed=4 * NH * (NQ + NK) * BLK * BLK, transcendentals=NH * NQ * NK * BLK * BLK),
         name="attend_forward",
     )(*plan, qd, kv)
 
@@ -224,13 +234,13 @@
     return pl.pallas_call(
         _backward,
         out_shape=(
-            jax.ShapeDtypeStruct((4, HW, TEAM_ROWS), BF),
-            jax.ShapeDtypeStruct((8, 2 * HW, TEAM_ROWS), BF),
+            jax.ShapeDtypeStruct((4, KW, TEAM_ROWS), BF),
+            jax.ShapeDtypeStruct((8, 2 * KW, TEAM_ROWS), BF),
         ),
         in_specs=[pl.BlockSpec(memory_space=pltpu.SMEM)] * 6 + _specs(3),
         out_specs=tuple(_specs(2)),
         scratch_shapes=[
-            pltpu.VMEM((2 * HW, NK * BLK), BF),
+            pltpu.VMEM((2 * KW, NK * BLK), BF),
             pltpu.VMEM((NH, NK * BLK, 2 * HEAD), BF),
             pltpu.VMEM((NH, NK * BLK, 2 * HEAD), F32),
             pltpu.VMEM((NH, 2 * HEAD, 2 * width), BF),
@@ -238,6 +248,7 @@
             pltpu.VMEM((NH, HEAD, width), F32),
         ],
         compiler_params=pltpu.CompilerParams(vmem_limit_bytes=VMEM_LIMIT),
+        cost_estimate=pl.CostEstimate(flops=10 * NH * NQ * NK * BLK * BLK * HEAD, bytes_accessed=8 * NH * (NQ + NK) * BLK * BLK, transcendentals=NH * NQ * NK * BLK * BLK),
         name="attend_backward",
     )(*plan, qd, kv, ld)
 
@@ -261,15 +272,17 @@
     rows = jnp.arange(4, dtype=jnp.int32) ^ team
     other = (y + jnp.arange(4, dtype=jnp.int32)) % 4
     mine = ((z * 2 + xh) * 4 + other)[:, None] * 4 + rows[None, :]
-    step = jnp.arange(8, dtype=jnp.int32)
-    there = ((z + step // 2) % 4) * 2 + (xh ^ (step % 2))
-    theirs = (there * 4 + y)[:, None] * 4 + rows[None, :]
+    theirs = (jnp.arange(8, dtype=jnp.int32) * 4 + y)[:, None] * 4 + rows[None, :]
     qsrc, qpos = in_order(pick(block_order, mine.reshape(-1)))
     ksrc, kpos = in_order(pick(block_order, theirs.reshape(-1)))
-    ends = qpos.reshape(NT, QT)
-    below = jnp.sum((kpos[None, :] < ends[:, :1]).astype(jnp.int32), axis=1)
-    upto = jnp.sum((kpos[None, :] <= ends[:, -1:]).astype(jnp.int32), axis=1)
-    return (qsrc, qpos, ksrc, kpos, below // CH, (upto + CH - 1) // CH)
+
+    def plan(qt):
+        ends = qpos.reshape(NQ // qt, qt)
+        below = jnp.sum((kpos[None, :] < ends[:, :1]).astype(jnp.int32), axis=1)
+        upto = jnp.sum((kpos[None, :] <= ends[:, -1:]).astype(jnp.int32), axis=1)
+        return (qsrc, qpos, ksrc, kpos, below // CH, (upto + CH - 1) // CH)
+
+    return plan(FQT), plan(QT)
 
 
 def from_y(x, i):
@@ -280,20 +293,16 @@
     return lax.ppermute(x, "y", [(d, (d + i) % 4) for d in range(4)])
 
 
-def _key_pairs(i):
-    pairs = []
-    for d in range(8):
-        there = ((d // 2 + i // 2) % 4) * 2 + ((d % 2) ^ (i % 2))
-        pairs.append((d, there))
-    return pairs
-
-
-def from_keys(x, i):
-    return lax.ppermute(x, KEYS, [(b, a) for a, b in _key_pairs(i)])
-
-
-def to_keys(x, i):
-    return lax.ppermute(x, KEYS, _key_pairs(i))
+def from_keys(x):
+    return lax.all_to_all(jnp.broadcast_to(x[None], (8,) + x.shape), KEYS, 0, 0, tiled=True)
+
+
+def to_keys(parts):
+    return lax.all_to_all(parts, KEYS, 0, 0, tiled=True)
+
+
+def after(values, *done):
+    return lax.optimization_barrier((values, done))[0]
 
 
 def swapped(x, axis):
@@ -313,25 +322,15 @@
     return jnp.where(first, took, other), jnp.where(first, other, took)
 
 
-def _format_first(a_ref, b_ref, one_ref, two_ref):
-    def put(ref):
-        for i in range(16):
-            block = ref[0, i].astype(F32)
-            one_ref[24 * i : 24 * (i + 1), :] = block[:24]
-            two_ref[24 * i : 24 * (i + 1), :] = block[24:48]
-
-    @pl.when(pl.program_id(1) == 0)
-    def _():
-        put(a_ref)
-
-    @pl.when(pl.program_id(1) == 1)
-    def _():
-        put(b_ref)
-
-
-def format_first(a, b):
-    n = a.shape[1]
-    block = pl.BlockSpec((1, 16, n, D), lambda zh, c: (zh, 0, 0, 0))
+def _format_first(all_ref, one_ref, two_ref):
+    for i in range(16):
+        block = all_ref[0, i, 0].astype(F32)
+        one_ref[24 * i : 24 * (i + 1), :] = block[:24]
+        two_ref[24 * i : 24 * (i + 1), :] = block[24:48]
+
+
+def format_first(gathered):
+    n = gathered.shape[1]
     return pl.pallas_call(
         _format_first,
         grid=(2, 2),
@@ -339,14 +338,14 @@
             jax.ShapeDtypeStruct((384, FF), F32),
             jax.ShapeDtypeStruct((FF // 2, D), F32),
         ),
-        in_specs=[block, block],
+        in_specs=[pl.BlockSpec((1, 16, 1, n, D), lambda zh, c: (zh, 0, c, 0, 0))],
         out_specs=(
             pl.BlockSpec((384, D), lambda zh, c: (0, zh * 2 + c)),
             pl.BlockSpec((384, D), lambda zh, c: (c * 2 + zh, 0)),
         ),
         compiler_params=pltpu.CompilerParams(vmem_limit_bytes=VMEM_LIMIT),
         name="format_first",
-    )(a.reshape(2, 16, n, D), b.reshape(2, 16, n, D))
+    )(gathered.reshape(2, 16, 2, n, D))
 
 
 def _format_second(a_ref, b_ref, qkv_ref, out_ref):
@@ -442,7 +441,7 @@
     w_two = lax.dynamic_slice_in_dim(w_fc2, core * D, D, axis=0)
     b_one = lax.dynamic_slice_in_dim(b_fc1, core * D, D, axis=0).astype(F32)
 
-    plan = make_plan(block_order, team, z, xh, y)
+    fplan, bplan = make_plan(block_order, team, z, xh, y)
 
     x = x4.astype(F32)
     centred = x - jnp.mean(x, axis=1, keepdims=True)
@@ -452,19 +451,21 @@
     a_mlp = (n * g_mlp + c_mlp).astype(BF)
 
     qkv = dot(w_q, a_attn, ((0,), (1,))) + bias_qkv[:, None]
-    qkv = qkv.reshape(3, NH, HEAD, TEAM_ROWS)
+    qkv = qkv.reshape(3, TH, HEAD, TEAM_ROWS)
     anchors = pick(block_order, group * 4 + (jnp.arange(4, dtype=jnp.int32) ^ team))
     places = (anchors[:, None] * BLK + jnp.arange(BLK, dtype=jnp.int32)[None, :]).reshape(-1)
     frequency = jnp.exp(jnp.arange(ROT // 2, dtype=F32) * (-2.0 * math.log(10000.0) / ROT))
     angles = frequency[:, None] * places.astype(F32)[None, :]
     cosine, sine = jnp.cos(angles), jnp.sin(angles)
     turned = rotate(qkv[:2], cosine, sine).astype(BF)
-    kv = jnp.stack([turned[1], qkv[2].astype(BF)], axis=1).reshape(2 * HW, TEAM_ROWS)
-    kv_all = jnp.stack([kv] + [from_keys(kv, i) for i in range(1, 8)])
-    d_mixed = dot(w_o, dy4, ((1,), (1,))).astype(BF).reshape(NH, HEAD, TEAM_ROWS)
-    qd = jnp.stack([turned[0] * jnp.asarray(0.125, BF), d_mixed], axis=1)
-    qd = qd.reshape(2 * HW, TEAM_ROWS)
-    qd_all = jnp.stack([qd] + [from_y(qd, i) for i in range(1, 4)])
+    values = qkv[2].astype(BF)
+    d_mixed = dot(w_o, dy4, ((1,), (1,))).astype(BF).reshape(TH, HEAD, TEAM_ROWS)
+    kv_all, qd_all = [], []
+    for h in range(TH):
+        kv = jnp.concatenate([turned[1, h], values[h]], axis=0)
+        qd = jnp.concatenate([turned[0, h] * jnp.asarray(0.125, BF), d_mixed[h]], axis=0)
+        kv_all.append(from_keys(kv))
+        qd_all.append(jnp.stack([qd] + [from_y(qd, i) for i in range(1, 4)]))
 
     hidden_pre = dot(a_mlp, w_one, ((1,), (0,))) + b_one
     hidden_act, gelu_pull = jax.vjp(partial(jax.nn.gelu, approximate=False), hidden_pre)
@@ -501,8 +502,6 @@
         ],
         axis=1,
     )
-    first, qd_all, kv_all = lax.optimization_barrier((first, qd_all, kv_all))
-    first = lax.all_to_all(first, GROUPS, 0, 0, tiled=True)
 
     def to_owner(part):
         pairs = []
@@ -516,44 +515,59 @@
                 pairs.append((at, at))
         return lax.ppermute(part, ("z", "fsdp"), pairs)
 
-    partial_out = attend_forward(plan, qd_all, kv_all)
-    first, partial_out = lax.optimization_barrier((first, partial_out))
-    parts = [partial_out[0]] + [to_y(partial_out[i], i) for i in range(1, 4)]
-    parts = jnp.stack(parts).astype(F32)
-    o_parts = parts[:, :HW].reshape(4, NH, HEAD, TEAM_ROWS)
-    lse_parts = jnp.sum(parts[:, HW : HW + 3 * NH].reshape(4, NH, 3, TEAM_ROWS), axis=2)
-    peak = jnp.max(lse_parts, axis=0)
-    share = jnp.exp(lse_parts - peak[None])
-    total = jnp.sum(share, axis=0)
-    attended = jnp.sum(o_parts * (share / total[None])[:, :, None, :], axis=0)
-    lse = peak + jnp.log(total)
-    delta = jnp.sum(attended * d_mixed.astype(F32), axis=1)
-    mixed = attended.astype(BF).reshape(HW, TEAM_ROWS)
-    ld = jnp.concatenate([lse, delta, jnp.zeros((2, TEAM_ROWS), F32)], axis=0)
-    ld_all = jnp.stack([ld] + [from_y(ld, i) for i in range(1, 4)])
-
-    first = jnp.sum(first.astype(F32), axis=0)
+    def merged(out, h, *done):
+        parts = after([out[0]] + [to_y(out[i], i) for i in range(1, 4)], *done)
+        parts = jnp.stack(parts).astype(F32)
+        lse_parts = jnp.sum(parts[:, HEAD : HEAD + 3], axis=1)
+        peak = jnp.max(lse_parts, axis=0)
+        share = jnp.exp(lse_parts - peak[None])
+        total = jnp.sum(share, axis=0)
+        whole = jnp.sum(parts[:, :HEAD] * (share / total[None])[:, None, :], axis=0)
+        delta = jnp.sum(whole * d_mixed[h].astype(F32), axis=0)
+        return whole, jnp.stack([peak + jnp.log(total), delta] + [jnp.zeros_like(delta)] * 6)
+
+    def stats(ld, *done):
+        return jnp.stack(after([ld] + [from_y(ld, i) for i in range(1, 4)], *done))
+
+    def pulled(dq_parts, dkv_parts, *done):
+        dkv = to_keys(dkv_parts)
+        dq = [dq_parts[0]] + [to_y(dq_parts[i], i) for i in range(1, 4)]
+        dkv, dq = after((dkv, dq), *done)
+        return sum(part.astype(F32) for part in dq), jnp.sum(dkv.astype(F32), axis=0)
+
+    out_0 = attend_forward(fplan, qd_all[0], kv_all[0])
+    out_1 = attend_forward(after(fplan, out_0), qd_all[1], kv_all[1])
+    first = lax.all_to_all(after(first, out_1), GROUPS, 0, 0, tiled=True)
+    whole_0, ld_0 = merged(out_0, 0, out_1)
+    out_2 = attend_forward(after(fplan, out_1, ld_0), qd_all[2], kv_all[2])
+    ld_0 = stats(ld_0, out_2)
+    whole_1, ld_1 = merged(out_1, 1, out_2)
+    raw_0 = attend_backward(after(bplan, out_2, ld_1), qd_all[0], kv_all[0], ld_0)
+    ld_1 = stats(ld_1, raw_0)
+    whole_2, ld_2 = merged(out_2, 2, raw_0)
+    first = jnp.sum(after(first, raw_0).astype(F32), axis=0)
+    raw_1 = attend_backward(after(bplan, raw_0, ld_2, first), qd_all[1], kv_all[1], ld_1)
+    ld_2 = stats(ld_2, raw_1)
+    grads_0 = pulled(*raw_0, raw_1)
+    raw_2 = attend_backward(after(bplan, raw_1, grads_0), qd_all[2], kv_all[2], ld_2)
+    grads_1 = pulled(*raw_1, raw_2)
+    grads_2 = pulled(*raw_2)
+    mixed = jnp.concatenate([whole_0, whole_1, whole_2]).astype(BF)
+
     shares = first[48:]
     shares = shares + jnp.where(group < 24, swapped(shares, "fsdp"), 0.0)
     first = jnp.concatenate(
         [to_owner(first[:24].astype(BF)), first[24:48].astype(BF), shares.astype(BF)], axis=0
     )
-    first, ld_all = lax.optimization_barrier((first, ld_all))
-    sent = jnp.broadcast_to(first[None], (32,) + first.shape)
-    first = lax.all_to_all(sent, GROUPS, 0, 0, tiled=True)
-
-    dq_parts, dkv_parts = attend_backward(plan, qd_all, kv_all, ld_all)
-    first, dq_parts, dkv_parts = lax.optimization_barrier((first, dq_parts, dkv_parts))
-    dkv = [dkv_parts[0]] + [to_keys(dkv_parts[i], i) for i in range(1, 8)]
-    dq = [dq_parts[0]] + [to_y(dq_parts[i], i) for i in range(1, 4)]
-    other = swapped(first, "core")
-    first_a = jnp.where(core == 0, first, other)
-    first_b = jnp.where(core == 0, other, first)
-    dq = sum(part.astype(F32) for part in dq)
-    dkv = sum(part.astype(F32) for part in dkv)
-    dkv = dkv.reshape(NH, 2, HEAD, TEAM_ROWS)
-    back = rotate(jnp.stack([dq.reshape(NH, HEAD, TEAM_ROWS), dkv[:, 0]]), cosine, -sine)
-    d_qkv = jnp.concatenate([back, dkv[None, :, 1]], axis=0).astype(BF)
+    first_all = lax.all_gather(first, CTX, axis=0, tiled=False)
+
+    dqs, dks, dvs = [], [], []
+    for dq, dkv in (grads_0, grads_1, grads_2):
+        dqs.append(dq)
+        dks.append(dkv[:HEAD])
+        dvs.append(dkv[HEAD:])
+    back = rotate(jnp.stack([jnp.stack(dqs), jnp.stack(dks)]), cosine, -sine)
+    d_qkv = jnp.concatenate([back, jnp.stack(dvs)[None]], axis=0).astype(BF)
     d_qkv = d_qkv.reshape(3 * HW, TEAM_ROWS)
 
     grad_qkv = dot(a_attn, d_qkv, ((0,), (1,)))
@@ -605,9 +619,10 @@
         - n[:BLK] * jnp.mean(dn * n[:BLK], axis=1, keepdims=True)
     )
 
-    grad_w_one, grad_w_two = format_first(first_a, first_b)
+    grad_w_one, grad_w_two = format_first(first_all)
     grad_w_qkv, grad_w_out = format_second(second_a, second_b)
-    tail_a, tail_b = (t[:, 48, :96].astype(F32) for t in (first_a, first_b))
+    tails = first_all.reshape(32, 2, -1, D)[:, :, 48, :96].astype(F32)
+    tail_a, tail_b = tails[:, 0], tails[:, 1]
     early = (tail_a[:24] + tail_b[:24]).reshape(3, D)
     grad_b_one = jnp.concatenate([tail_a[24:].reshape(D), tail_b[24:].reshape(D)])
     late = second_a[:, 24, :120].astype(F32) + second_b[:, 24, :120].astype(F32)

time: 527 us -> 494 us (0.937)
  waiting for transfers between devices: 87 us -> 42.3 us
  local copies, waits for them, and re-layouts: 78.8 us -> 61.2 us
  Pallas kernels: 109 us -> 126 us
  between operations: 2.17 us -> 16.2 us
    ppermute x14 -> x0, starting transfers between devices: 44.5 us -> none  [the longest x7 24.7 us: from_keys(): return lax.ppermute(x, KEYS, [(b, a) for a, b in _key_pairs(i)])]
    ppermute x14 -> x0, waiting for transfers between devices: 38.8 us -> none  [the longest x7 22.2 us: from_keys(): return lax.ppermute(x, KEYS, [(b, a) for a, b in _key_pairs(i)])]
    all_to_all x2 -> x7, starting transfers between devices: 25.6 us -> 56.6 us  [the longest x3 28.1 us: to_keys(): return lax.all_to_all(parts, KEYS, 0, 0, tiled=True)]
    pallas_call x2 -> x6, Pallas kernels: 96.9 us -> 115 us  [the longest x3 65.5 us: attend_backward(): pl.pallas_call(_backward, out_shape=(jax.ShapeDtypeStruct((4, KW, TEAM_RO...]
    ppermute x6 -> x18, starting transfers between devices: 7.67 us -> 22.7 us  [from_y(): return lax.ppermute(x, 'y', [((d + i) % 4, d) for d in range(4)])]
    all_to_all x1, waiting for transfers between devices: 15.8 us -> 1.02 us  [summed(): lax.all_to_all(parts, GROUPS, 0, 0, tiled=True).astype(F32)]
    unnamed x154 -> x185, local copies, waits for them, and re-layouts: 29.1 us -> 16.6 us
    ppermute x6 -> x18, waiting for transfers between devices: 14.4 us -> 3.76 us  [to_y(): return lax.ppermute(x, 'y', [(d, (d + i) % 4) for d in range(4)])]
  transfers between devices with their start and end apart: 45 -> 60, of which waited for: 12 -> 8; matrix products, arithmetic and copies ran while one was open for 27% -> 25% of each run, Pallas kernels for 20% -> 20%
where the time goes in v3:
time: 494 us; the launch traced here: 486 us
  starting transfers between devices  154 us (31%)
  Pallas kernels  126 us (26%)
  local copies, waits for them, and re-layouts  61.2 us (12%)
  other arithmetic  59.6 us (12%)
  waiting for transfers between devices  42.3 us (9%)
  matrix products  26.4 us (5%)
  between operations  16.2 us (3%)
    pallas_call x3, Pallas kernels, attend_backward(): pl.pallas_call(_backward, out_shape=(jax.ShapeDtypeStruct((4, KW, TEAM_RO...  65.5 us
    pallas_call x3, Pallas kernels, attend_forward(): pl.pallas_call(_forward, out_shape=jax.ShapeDtypeStruct((4, KW + 16, TEAM...  49.6 us
    ppermute x12, starting transfers between devices, swapped(): return lax.ppermute(x, axis, [(0, 1), (1, 0)])  31.1 us
    all_to_all x3, starting transfers between devices, to_keys(): return lax.all_to_all(parts, KEYS, 0, 0, tiled=True)  28.1 us
    dot_general x12, matrix products, dot(): return lax.dot_general(a, b, (dims, ((), ())), preferred_element_type=F32)  26.4 us
    ppermute x18, starting transfers between devices, from_y(): return lax.ppermute(x, 'y', [((d + i) % 4, d) for d in range(4)])  22.7 us
    all_to_all x1, waiting for transfers between devices, to_all_groups(): took = lax.all_to_all(sent, GROUPS, 0, 0, tiled=True)  22.1 us
    all_to_all x3, starting transfers between devices, from_keys(): lax.all_to_all(jnp.broadcast_to(x[None], (8,) + x.shape), KEYS, 0, 0, til...  20 us
  transfers between devices with their start and end apart: 60, of which 8 were waited for; matrix products, arithmetic and copies ran while one was open for 25% of the time, Pallas kernels for 20%

profile of v3, /device:TPU:1, one launch (start us, length us, event | category | flops | bytes accessed | tf_op | source)
XLA Modules:
  0.0 485.8 jit_solution(14638884267830123408)
XLA Ops:
  48.6 4.0 collective-permute-done.4
  59.9 2.9 collective-permute-start.20
  67.5 7.3 %all-to-all-start = ((bf16[8,128,512]{2,1,0:T(8,128)(2,1)}), bf16[8,128,512]{2,1,0:T(8,128)(2,1)}, u32[]{:S(2)}, u32[]{:S(2)}) async-start(bf16[8,128,512]{2,1,0:T(8,128)(2,1)} %broadcast_in_dim.107), calls=%async_computation | async-start | bytes 2097152 | tf_op jit(solution)/shard_map/all_to_all | solution.py:297
  79.0 5.0 %multiply_convert_fusion = (bf16[512,768]{1,0:T(8,128)(2,1)}, f32[512,768]{1,0:T(8,128)S(1)}, f32[512,768]{1,0:T(8,128)S(1)}) fusion(f32[768]{0:T(1024)S(1)} %copy-done.81, bf16[384,768]{1,0:T(8,128)(2,1)S(1)} %get-tuple-element.207, bf16[384,768]{1,0:T(8,128)(2,1)S(1)} %get-tuple-element.206, f32[768]{0:T(1024)S(1)} %copy-done.79, f32[768]{0:T(1024)S(1)} %copy-done.76, ...), kind=kOutput, calls=%fused_computation.24 | convolution fusion | flops 636616704 | bytes 5911552 | tf_op jit(solution)/shard_map/dot_general | solution.py:387
  88.0 4.0 multiply_reduce_fusion.1
  101.0 6.8 %all-to-all-start.1 = ((bf16[8,128,512]{2,1,0:T(8,128)(2,1)}), bf16[8,128,512]{2,1,0:T(8,128)(2,1)}, u32[]{:S(2)}, u32[]{:S(2)}) async-start(bf16[8,128,512]{2,1,0:T(8,128)(2,1)} %broadcast_in_dim.108), calls=%async_computation.1 | async-start | bytes 2097152 | tf_op jit(solution)/shard_map/all_to_all | solution.py:297
  115.5 3.0 collective-permute-done.9
  119.4 16.5 %attend_forward.3 = bf16[4,80,512]{2,1,0:T(8,128)(2,1)} custom-call(s32[16]{0:T(128)} %get-tuple-element.150.qsrc, s32[16]{0:T(128)} %copy-done.71, s32[32]{0:T(128)} %get-tuple-element.152.ksrc, s32[32]{0:T(128)} %copy-done.72, s32[4]{0:T(128)} %get-tuple-element.109.nfull, s32[4]{0:T(128)} %get-tuple-element.110.nall, ...), custom_call_target="tpu_custom_call" | custom-call | flops 2147483648 | bytes 3145728 | tf_op jit(solution)/shard_map/attend_forward/pallas_call | solution.py:217
  140.2 5.9 %all-to-all-start.2 = ((bf16[8,128,512]{2,1,0:T(8,128)(2,1)}), bf16[8,128,512]{2,1,0:T(8,128)(2,1)}, u32[]{:S(2)}, u32[]{:S(2)}) async-start(bf16[8,128,512]{2,1,0:T(8,128)(2,1)} %broadcast_in_dim.109), calls=%async_computation.2 | async-start | bytes 2097152 | tf_op jit(solution)/shard_map/all_to_all | solution.py:297
  146.1 16.5 %attend_forward.4 = bf16[4,80,512]{2,1,0:T(8,128)(2,1)} custom-call(s32[16]{0:T(128)} %get-tuple-element.150.qsrc, s32[16]{0:T(128)} %copy-done.71, s32[32]{0:T(128)} %get-tuple-element.152.ksrc, s32[32]{0:T(128)} %copy-done.72, s32[4]{0:T(128)} %get-tuple-element.109.nfull, s32[4]{0:T(128)} %get-tuple-element.110.nall, ...), custom_call_target="tpu_custom_call" | custom-call | flops 2147483648 | bytes 3145728 | tf_op jit(solution)/shard_map/attend_forward/pallas_call | solution.py:217
  169.0 2.7 collective-permute-start.26
  171.7 8.5 %all-to-all-start.4 = ((bf16[32,49,768]{2,1,0:T(8,128)(2,1)}), bf16[32,49,768]{2,1,0:T(8,128)(2,1)}, u32[]{:S(2)}, u32[]{:S(2)}) async-start(bf16[32,49,768]{2,1,0:T(8,128)(2,1)} %fusion.2), calls=%async_computation.4 | async-start | bytes 5505024 | tf_op jit(solution)/shard_map/all_to_all | solution.py:540
  180.2 16.5 %attend_forward.5 = bf16[4,80,512]{2,1,0:T(8,128)(2,1)} custom-call(s32[16]{0:T(128)} %get-tuple-element.150.qsrc, s32[16]{0:T(128)} %copy-done.71, s32[32]{0:T(128)} %get-tuple-element.152.ksrc, s32[32]{0:T(128)} %copy-done.72, s32[4]{0:T(128)} %get-tuple-element.109.nfull, s32[4]{0:T(128)} %get-tuple-element.110.nall, ...), custom_call_target="tpu_custom_call" | custom-call | flops 2147483648 | bytes 3145728 | tf_op jit(solution)/shard_map/attend_forward/pallas_call | solution.py:217
  202.7 5.1 %collective-permute-done.25 = f32[8,512]{1,0:T(8,128)S(1)} collective-permute-done((f32[8,512]{1,0:T(8,128)S(1)}, f32[8,512]{1,0:T(8,128)S(1)}, u32[]{:S(2)}, u32[]{:S(2)}) %collective-permute-start.25) | collective-permute-done | bytes 16416 | tf_op jit(solution)/shard_map/ppermute | solution.py:289
  208.6 21.8 %attend_backward.3 = (bf16[4,64,512]{2,1,0:T(8,128)(2,1)}, bf16[8,128,512]{2,1,0:T(8,128)(2,1)}) custom-call(s32[16]{0:T(128)} %get-tuple-element.150.qsrc, s32[16]{0:T(128)} %copy-done.71, s32[32]{0:T(128)} %get-tuple-element.152.ksrc, s32[32]{0:T(128)} %copy-done.72, s32[8]{0:T(128)} %get-tuple-element.154.nfull, s32[8]{0:T(128)} %get-tuple-element.155.nall, ...), custom_call_target="tpu_custom_call" | custom-call | flops 5368709120 | bytes 6291456 | tf_op jit(solution)/shard_map/attend_backward/pallas_call | solution.py:234
  236.9 14.1 %all-to-all-start.3 = ((bf16[8,128,512]{2,1,0:T(8,128)(2,1)}), bf16[8,128,512]{2,1,0:T(8,128)(2,1)S(1)}, u32[]{:S(2)}, u32[]{:S(2)}) async-start(bf16[8,128,512]{2,1,0:T(8,128)(2,1)} %get-tuple-element.126), calls=%async_computation.3 | async-start | bytes 2097152 | tf_op jit(solution)/shard_map/all_to_all | solution.py:301
  255.0 2.9 convert_reduce_fusion
  257.9 21.8 %attend_backward.4 = (bf16[4,64,512]{2,1,0:T(8,128)(2,1)}, bf16[8,128,512]{2,1,0:T(8,128)(2,1)}) custom-call(s32[16]{0:T(128)} %get-tuple-element.150.qsrc, s32[16]{0:T(128)} %copy-done.71, s32[32]{0:T(128)} %get-tuple-element.152.ksrc, s32[32]{0:T(128)} %copy-done.72, s32[8]{0:T(128)} %get-tuple-element.154.nfull, s32[8]{0:T(128)} %get-tuple-element.155.nall, ...), custom_call_target="tpu_custom_call" | custom-call | flops 5368709120 | bytes 6291456 | tf_op jit(solution)/shard_map/attend_backward/pallas_call | solution.py:234
  283.6 21.8 %attend_backward.5 = (bf16[4,64,512]{2,1,0:T(8,128)(2,1)}, bf16[8,128,512]{2,1,0:T(8,128)(2,1)}) custom-call(s32[16]{0:T(128)} %get-tuple-element.150.qsrc, s32[16]{0:T(128)} %copy-done.71, s32[32]{0:T(128)} %get-tuple-element.152.ksrc, s32[32]{0:T(128)} %copy-done.72, s32[8]{0:T(128)} %get-tuple-element.154.nfull, s32[8]{0:T(128)} %get-tuple-element.155.nall, ...), custom_call_target="tpu_custom_call" | custom-call | flops 5368709120 | bytes 6291456 | tf_op jit(solution)/shard_map/attend_backward/pallas_call | solution.py:234
  305.4 9.7 %all-to-all-start.6 = ((bf16[8,128,512]{2,1,0:T(8,128)(2,1)}), bf16[8,128,512]{2,1,0:T(8,128)(2,1)S(1)}, u32[]{:S(2)}, u32[]{:S(2)}) async-start(bf16[8,128,512]{2,1,0:T(8,128)(2,1)} %get-tuple-element.161), calls=%async_computation.6 | async-start | bytes 2097152 | tf_op jit(solution)/shard_map/all_to_all | solution.py:301
  323.8 3.1 all-to-all-done.6
  326.9 4.2 all-to-all-start.5
  343.6 3.0 collective-permute-done.35
  355.9 4.9 %multiply_reduce_fusion = (bf16[768]{0:T(1024)(128)(2,1)S(1)}, bf16[768]{0:T(1024)(128)(2,1)S(1)}, f32[512,768]{1,0:T(8,128)}, f32[512,768]{1,0:T(8,128)}) fusion(f32[512]{0:T(512)} %copy-done.82, f32[512]{0:T(512)S(1)} %copy-done.61, bf16[256,768]{1,0:T(8,128)(2,1)} %copy-done.7, bf16[128,768]{1,0:T(8,128)(2,1)} %copy-done.13, ...), kind=kOutput, calls=%fused_computation.18 | convolution fusion | flops 460257792 | bytes 6992896 | tf_op jit(solution)/shard_map/dot_general | solution.py:387
  363.6 12.0 %all-to-all-start.7 = ((bf16[32,25,768]{2,1,0:T(8,128)(2,1)}), bf16[32,25,768]{2,1,0:T(8,128)(2,1)}, u32[]{:S(2)}, u32[]{:S(2)}) async-start(bf16[32,25,768]{2,1,0:T(8,128)(2,1)} %fusion.4), calls=%async_computation.7 | async-start | bytes 3145728 | tf_op jit(solution)/shard_map/all_to_all | solution.py:485
  379.2 10.8 %collective-permute-start.43 = (bf16[2,128,1536]{2,1,0:T(8,128)(2,1)}, bf16[2,128,1536]{2,1,0:T(8,128)(2,1)S(1)}, u32[]{:S(2)}, u32[]{:S(2)}) collective-permute-start(bf16[2,128,1536]{2,1,0:T(8,128)(2,1)} %bitcast.91), channel_id=1, source_target_pairs={{0,2},{2,0},{1,3},{3,1},{4,6},{6,4},{5,7},{7,5},{8,10},{10,8},{9,1... | collective-permute-start | bytes 2359304 | tf_op jit(solution)/shard_map/ppermute | solution.py:309
  397.6 14.9 %all-to-all-start.8 = ((bf16[32,25,768]{2,1,0:T(8,128)(2,1)}), bf16[32,25,768]{2,1,0:T(8,128)(2,1)}, u32[]{:S(2)}, u32[]{:S(2)}) async-start(bf16[32,25,768]{2,1,0:T(8,128)(2,1)} %broadcast_in_dim.122), calls=%async_computation.8 | async-start | bytes 3145728 | tf_op jit(solution)/shard_map/all_to_all | solution.py:319
  417.9 22.1 %all-to-all-done.8 = bf16[32,25,768]{2,1,0:T(8,128)(2,1)} async-done(((bf16[32,25,768]{2,1,0:T(8,128)(2,1)}), bf16[32,25,768]{2,1,0:T(8,128)(2,1)}, u32[]{:S(2)}, u32[]{:S(2)}) %all-to-all-start.8) | async-done | bytes 1228832 | tf_op jit(solution)/shard_map/all_to_all | solution.py:319
  442.3 11.0 %collective-permute-start.47 = (bf16[32,25,768]{2,0,1:T(8,128)(2,1)S(1)}, bf16[32,25,768]{2,0,1:T(8,128)(2,1)S(1)}, u32[]{:S(2)}, u32[]{:S(2)}) collective-permute-start(bf16[32,25,768]{2,0,1:T(8,128)(2,1)S(1)} %copy.41), channel_id=1, source_target_pairs={{0,2},{2,0},{1,3},{3,1},{4,6},{6,4},{5,7},{7,5},{8,10},{10,8},{9,1... | collective-permute-start | bytes 3686408 | tf_op jit(solution)/shard_map/ppermute | solution.py:309
  456.5 3.9 broadcast_select_fusion.1
  460.4 4.5 format_second.1
  470.7 6.6 %format_first.1 = (f32[384,3072]{1,0:T(8,128)}, f32[1536,768]{1,0:T(8,128)}) custom-call(bf16[2,16,2,49,768]{4,3,2,1,0:T(8,128)(2,1)} %bitcast.173), custom_call_target="tpu_custom_call" | custom-call | tf_op jit(solution)/shard_map/format_first/pallas_call | solution.py:334
  (493 shorter events, 171.4 us)
Async XLA Ops:
  22.8 52.1 %collective-permute-start.3 = (bf16[384,768]{1,0:T(8,128)(2,1)}, bf16[384,768]{1,0:T(8,128)(2,1)}, u32[]{:S(2)}, u32[]{:S(2)}) collective-permute-start(bf16[384,768]{1,0:T(8,128)(2,1)} %constant_dynamic-slice_fusion.6), channel_id=1, source_target_pairs={{0,1},{1,0},{2,3},{3,2},{4,5},{5,4},{6,7},{7,6},{8,9},{9,8},{10,11... | collective-permute-start | bytes 1769480 | tf_op jit(solution)/shard_map/ppermute | solution.py:309
  59.9 39.9 %collective-permute-start.20 = (bf16[128,512]{1,0:T(8,128)(2,1)}, bf16[128,512]{1,0:T(8,128)(2,1)}, u32[]{:S(2)}, u32[]{:S(2)}) collective-permute-start(bf16[128,512]{1,0:T(8,128)(2,1)} %get-tuple-element.272), channel_id=1, source_target_pairs={{8,0},{12,4},{0,8},{4,12},{9,1},{13,5},{1,9},{5,13},{10,2},{14,6},... | collective-permute-start | bytes 393224 | tf_op jit(solution)/shard_map/ppermute | solution.py:289
  62.9 44.9 %collective-permute-start.19 = (bf16[128,512]{1,0:T(8,128)(2,1)}, bf16[128,512]{1,0:T(8,128)(2,1)}, u32[]{:S(2)}, u32[]{:S(2)}) collective-permute-start(bf16[128,512]{1,0:T(8,128)(2,1)} %get-tuple-element.272), channel_id=1, source_target_pairs={{4,0},{8,4},{12,8},{0,12},{5,1},{9,5},{13,9},{1,13},{6,2},{10,6},{... | collective-permute-start | bytes 393224 | tf_op jit(solution)/shard_map/ppermute | solution.py:289
  63.7 45.9 %collective-permute-start.21 = (bf16[128,512]{1,0:T(8,128)(2,1)}, bf16[128,512]{1,0:T(8,128)(2,1)}, u32[]{:S(2)}, u32[]{:S(2)}) collective-permute-start(bf16[128,512]{1,0:T(8,128)(2,1)} %get-tuple-element.272), channel_id=1, source_target_pairs={{12,0},{0,4},{4,8},{8,12},{13,1},{1,5},{5,9},{9,13},{14,2},{2,6},{... | collective-permute-start | bytes 393224 | tf_op jit(solution)/shard_map/ppermute | solution.py:289
  65.1 46.5 %collective-permute-start.14 = (bf16[128,512]{1,0:T(8,128)(2,1)}, bf16[128,512]{1,0:T(8,128)(2,1)}, u32[]{:S(2)}, u32[]{:S(2)}) collective-permute-start(bf16[128,512]{1,0:T(8,128)(2,1)} %get-tuple-element.274), channel_id=1, source_target_pairs={{8,0},{12,4},{0,8},{4,12},{9,1},{13,5},{1,9},{5,13},{10,2},{14,6},... | collective-permute-start | bytes 393224 | tf_op jit(solution)/shard_map/ppermute | solution.py:289
  67.5 32.4 %all-to-all-start = ((bf16[8,128,512]{2,1,0:T(8,128)(2,1)}), bf16[8,128,512]{2,1,0:T(8,128)(2,1)}, u32[]{:S(2)}, u32[]{:S(2)}) async-start(bf16[8,128,512]{2,1,0:T(8,128)(2,1)} %broadcast_in_dim.107), calls=%async_computation | async-start | bytes 2097152 | tf_op jit(solution)/shard_map/all_to_all | solution.py:297
  74.9 38.7 %collective-permute-start.13 = (bf16[128,512]{1,0:T(8,128)(2,1)}, bf16[128,512]{1,0:T(8,128)(2,1)}, u32[]{:S(2)}, u32[]{:S(2)}) collective-permute-start(bf16[128,512]{1,0:T(8,128)(2,1)} %get-tuple-element.274), channel_id=1, source_target_pairs={{4,0},{8,4},{12,8},{0,12},{5,1},{9,5},{13,9},{1,13},{6,2},{10,6},{... | collective-permute-start | bytes 393224 | tf_op jit(solution)/shard_map/ppermute | solution.py:289
  101.0 38.1 %all-to-all-start.1 = ((bf16[8,128,512]{2,1,0:T(8,128)(2,1)}), bf16[8,128,512]{2,1,0:T(8,128)(2,1)}, u32[]{:S(2)}, u32[]{:S(2)}) async-start(bf16[8,128,512]{2,1,0:T(8,128)(2,1)} %broadcast_in_dim.108), calls=%async_computation.1 | async-start | bytes 2097152 | tf_op jit(solution)/shard_map/all_to_all | solution.py:297
  137.7 29.2 %collective-permute-start.12 = (bf16[80,512]{1,0:T(8,128)(2,1)S(1)}, bf16[80,512]{1,0:T(8,128)(2,1)S(1)}, u32[]{:S(2)}, u32[]{:S(2)}) collective-permute-start(bf16[80,512]{1,0:T(8,128)(2,1)S(1)} %get-tuple-element.244), channel_id=1, source_target_pairs={{0,12},{4,0},{8,4},{12,8},{1,13},{5,1},{9,5},{13,9},{2,14},{6,2},{... | collective-permute-start | bytes 245768 | tf_op jit(solution)/shard_map/ppermute | solution.py:293
  137.7 30.1 %collective-permute-start.11 = (bf16[80,512]{1,0:T(8,128)(2,1)}, bf16[80,512]{1,0:T(8,128)(2,1)S(1)}, u32[]{:S(2)}, u32[]{:S(2)}) collective-permute-start(bf16[80,512]{1,0:T(8,128)(2,1)} %get-tuple-element.245), channel_id=1, source_target_pairs={{0,8},{4,12},{8,0},{12,4},{1,9},{5,13},{9,1},{13,5},{2,10},{6,14},... | collective-permute-start | bytes 245768 | tf_op jit(solution)/shard_map/ppermute | solution.py:293
  137.7 30.1 %collective-permute-start.10 = (bf16[80,512]{1,0:T(8,128)(2,1)}, bf16[80,512]{1,0:T(8,128)(2,1)S(1)}, u32[]{:S(2)}, u32[]{:S(2)}) collective-permute-start(bf16[80,512]{1,0:T(8,128)(2,1)} %get-tuple-element.246), channel_id=1, source_target_pairs={{0,4},{4,8},{8,12},{12,0},{1,5},{5,9},{9,13},{13,1},{2,6},{6,10},{... | collective-permute-start | bytes 245768 | tf_op jit(solution)/shard_map/ppermute | solution.py:293
  140.2 31.5 %all-to-all-start.2 = ((bf16[8,128,512]{2,1,0:T(8,128)(2,1)}), bf16[8,128,512]{2,1,0:T(8,128)(2,1)}, u32[]{:S(2)}, u32[]{:S(2)}) async-start(bf16[8,128,512]{2,1,0:T(8,128)(2,1)} %broadcast_in_dim.109), calls=%async_computation.2 | async-start | bytes 2097152 | tf_op jit(solution)/shard_map/all_to_all | solution.py:297
  164.4 32.4 %collective-permute-start.18 = (bf16[80,512]{1,0:T(8,128)(2,1)}, bf16[80,512]{1,0:T(8,128)(2,1)S(1)}, u32[]{:S(2)}, u32[]{:S(2)}) collective-permute-start(bf16[80,512]{1,0:T(8,128)(2,1)} %get-tuple-element.236), channel_id=1, source_target_pairs={{0,12},{4,0},{8,4},{12,8},{1,13},{5,1},{9,5},{13,9},{2,14},{6,2},{... | collective-permute-start | bytes 245768 | tf_op jit(solution)/shard_map/ppermute | solution.py:293
  165.4 32.5 %collective-permute-start.17 = (bf16[80,512]{1,0:T(8,128)(2,1)}, bf16[80,512]{1,0:T(8,128)(2,1)S(1)}, u32[]{:S(2)}, u32[]{:S(2)}) collective-permute-start(bf16[80,512]{1,0:T(8,128)(2,1)} %get-tuple-element.237), channel_id=1, source_target_pairs={{0,8},{4,12},{8,0},{12,4},{1,9},{5,13},{9,1},{13,5},{2,10},{6,14},... | collective-permute-start | bytes 245768 | tf_op jit(solution)/shard_map/ppermute | solution.py:293
  166.9 31.0 %collective-permute-start.16 = (bf16[80,512]{1,0:T(8,128)(2,1)S(1)}, bf16[80,512]{1,0:T(8,128)(2,1)S(1)}, u32[]{:S(2)}, u32[]{:S(2)}) collective-permute-start(bf16[80,512]{1,0:T(8,128)(2,1)S(1)} %get-tuple-element.238), channel_id=1, source_target_pairs={{0,4},{4,8},{8,12},{12,0},{1,5},{5,9},{9,13},{13,1},{2,6},{6,10},{... | collective-permute-start | bytes 245768 | tf_op jit(solution)/shard_map/ppermute | solution.py:293
  168.7 32.3 %collective-permute-start.27 = (f32[8,512]{1,0:T(8,128)S(1)}, f32[8,512]{1,0:T(8,128)S(1)}, u32[]{:S(2)}, u32[]{:S(2)}) collective-permute-start(f32[8,512]{1,0:T(8,128)S(1)} %maximum_maximum_fusion), channel_id=1, source_target_pairs={{12,0},{0,4},{4,8},{8,12},{13,1},{1,5},{5,9},{9,13},{14,2},{2,6},{... | collective-permute-start | bytes 49160 | tf_op jit(solution)/shard_map/ppermute | solution.py:289
  169.0 32.9 %collective-permute-start.26 = (f32[8,512]{1,0:T(8,128)S(1)}, f32[8,512]{1,0:T(8,128)S(1)}, u32[]{:S(2)}, u32[]{:S(2)}) collective-permute-start(f32[8,512]{1,0:T(8,128)S(1)} %maximum_maximum_fusion), channel_id=1, source_target_pairs={{8,0},{12,4},{0,8},{4,12},{9,1},{13,5},{1,9},{5,13},{10,2},{14,6},... | collective-permute-start | bytes 49160 | tf_op jit(solution)/shard_map/ppermute | solution.py:289
  171.7 65.2 %all-to-all-start.4 = ((bf16[32,49,768]{2,1,0:T(8,128)(2,1)}), bf16[32,49,768]{2,1,0:T(8,128)(2,1)}, u32[]{:S(2)}, u32[]{:S(2)}) async-start(bf16[32,49,768]{2,1,0:T(8,128)(2,1)} %fusion.2), calls=%async_computation.4 | async-start | bytes 5505024 | tf_op jit(solution)/shard_map/all_to_all | solution.py:540
  198.8 31.6 %collective-permute-start.33 = (f32[8,512]{1,0:T(8,128)S(1)}, f32[8,512]{1,0:T(8,128)S(1)}, u32[]{:S(2)}, u32[]{:S(2)}) collective-permute-start(f32[8,512]{1,0:T(8,128)S(1)} %maximum_maximum_fusion.1), channel_id=1, source_target_pairs={{12,0},{0,4},{4,8},{8,12},{13,1},{1,5},{5,9},{9,13},{14,2},{2,6},{... | collective-permute-start | bytes 49160 | tf_op jit(solution)/shard_map/ppermute | solution.py:289
  199.3 31.1 %collective-permute-start.32 = (f32[8,512]{1,0:T(8,128)S(1)}, f32[8,512]{1,0:T(8,128)S(1)}, u32[]{:S(2)}, u32[]{:S(2)}) collective-permute-start(f32[8,512]{1,0:T(8,128)S(1)} %maximum_maximum_fusion.1), channel_id=1, source_target_pairs={{8,0},{12,4},{0,8},{4,12},{9,1},{13,5},{1,9},{5,13},{10,2},{14,6},... | collective-permute-start | bytes 49160 | tf_op jit(solution)/shard_map/ppermute | solution.py:289
  201.0 29.5 %collective-permute-start.31 = (f32[8,512]{1,0:T(8,128)S(1)}, f32[8,512]{1,0:T(8,128)S(1)}, u32[]{:S(2)}, u32[]{:S(2)}) collective-permute-start(f32[8,512]{1,0:T(8,128)S(1)} %maximum_maximum_fusion.1), channel_id=1, source_target_pairs={{4,0},{8,4},{12,8},{0,12},{5,1},{9,5},{13,9},{1,13},{6,2},{10,6},{... | collective-permute-start | bytes 49160 | tf_op jit(solution)/shard_map/ppermute | solution.py:289
  201.9 33.7 %collective-permute-start.24 = (bf16[80,512]{1,0:T(8,128)(2,1)S(1)}, bf16[80,512]{1,0:T(8,128)(2,1)S(1)}, u32[]{:S(2)}, u32[]{:S(2)}) collective-permute-start(bf16[80,512]{1,0:T(8,128)(2,1)S(1)} %get-tuple-element.240), channel_id=1, source_target_pairs={{0,12},{4,0},{8,4},{12,8},{1,13},{5,1},{9,5},{13,9},{2,14},{6,2},{... | collective-permute-start | bytes 245768 | tf_op jit(solution)/shard_map/ppermute | solution.py:293
  207.8 28.3 %collective-permute-start.23 = (bf16[80,512]{1,0:T(8,128)(2,1)S(1)}, bf16[80,512]{1,0:T(8,128)(2,1)S(1)}, u32[]{:S(2)}, u32[]{:S(2)}) collective-permute-start(bf16[80,512]{1,0:T(8,128)(2,1)S(1)} %get-tuple-element.241), channel_id=1, source_target_pairs={{0,8},{4,12},{8,0},{12,4},{1,9},{5,13},{9,1},{13,5},{2,10},{6,14},... | collective-permute-start | bytes 245768 | tf_op jit(solution)/shard_map/ppermute | solution.py:293
  232.1 47.7 %collective-permute-start.30 = (bf16[64,512]{1,0:T(8,128)(2,1)}, bf16[64,512]{1,0:T(8,128)(2,1)}, u32[]{:S(2)}, u32[]{:S(2)}) collective-permute-start(bf16[64,512]{1,0:T(8,128)(2,1)} %get-tuple-element.256), channel_id=1, source_target_pairs={{0,12},{4,0},{8,4},{12,8},{1,13},{5,1},{9,5},{13,9},{2,14},{6,2},{... | collective-permute-start | bytes 196616 | tf_op jit(solution)/shard_map/ppermute | solution.py:293
  234.8 45.0 %collective-permute-start.29 = (bf16[64,512]{1,0:T(8,128)(2,1)}, bf16[64,512]{1,0:T(8,128)(2,1)}, u32[]{:S(2)}, u32[]{:S(2)}) collective-permute-start(bf16[64,512]{1,0:T(8,128)(2,1)} %get-tuple-element.257), channel_id=1, source_target_pairs={{0,8},{4,12},{8,0},{12,4},{1,9},{5,13},{9,1},{13,5},{2,10},{6,14},... | collective-permute-start | bytes 196616 | tf_op jit(solution)/shard_map/ppermute | solution.py:293
  235.6 44.2 %collective-permute-start.28 = (bf16[64,512]{1,0:T(8,128)(2,1)}, bf16[64,512]{1,0:T(8,128)(2,1)}, u32[]{:S(2)}, u32[]{:S(2)}) collective-permute-start(bf16[64,512]{1,0:T(8,128)(2,1)} %get-tuple-element.258), channel_id=1, source_target_pairs={{0,4},{4,8},{8,12},{12,0},{1,5},{5,9},{9,13},{13,1},{2,6},{6,10},{... | collective-permute-start | bytes 196616 | tf_op jit(solution)/shard_map/ppermute | solution.py:293
  236.9 42.9 %all-to-all-start.3 = ((bf16[8,128,512]{2,1,0:T(8,128)(2,1)}), bf16[8,128,512]{2,1,0:T(8,128)(2,1)S(1)}, u32[]{:S(2)}, u32[]{:S(2)}) async-start(bf16[8,128,512]{2,1,0:T(8,128)(2,1)} %get-tuple-element.126), calls=%async_computation.3 | async-start | bytes 2097152 | tf_op jit(solution)/shard_map/all_to_all | solution.py:301
  331.2 136.8 %all-gather.4.cloned.1.call-start = ((), (), s32[]{:S(2)}) async-start(), calls=%async_computation.9 | async-start | bytes 5591040 | tf_op jit(solution)/shard_map/all_gather | solution.py:562
  363.6 27.3 %all-to-all-start.7 = ((bf16[32,25,768]{2,1,0:T(8,128)(2,1)}), bf16[32,25,768]{2,1,0:T(8,128)(2,1)}, u32[]{:S(2)}, u32[]{:S(2)}) async-start(bf16[32,25,768]{2,1,0:T(8,128)(2,1)} %fusion.4), calls=%async_computation.7 | async-start | bytes 3145728 | tf_op jit(solution)/shard_map/all_to_all | solution.py:485
  379.2 33.3 %collective-permute-start.43 = (bf16[2,128,1536]{2,1,0:T(8,128)(2,1)}, bf16[2,128,1536]{2,1,0:T(8,128)(2,1)S(1)}, u32[]{:S(2)}, u32[]{:S(2)}) collective-permute-start(bf16[2,128,1536]{2,1,0:T(8,128)(2,1)} %bitcast.91), channel_id=1, source_target_pairs={{0,2},{2,0},{1,3},{3,1},{4,6},{6,4},{5,7},{7,5},{8,10},{10,8},{9,1... | collective-permute-start | bytes 2359304 | tf_op jit(solution)/shard_map/ppermute | solution.py:309
  397.6 42.5 %all-to-all-start.8 = ((bf16[32,25,768]{2,1,0:T(8,128)(2,1)}), bf16[32,25,768]{2,1,0:T(8,128)(2,1)}, u32[]{:S(2)}, u32[]{:S(2)}) async-start(bf16[32,25,768]{2,1,0:T(8,128)(2,1)} %broadcast_in_dim.122), calls=%async_computation.8 | async-start | bytes 3145728 | tf_op jit(solution)/shard_map/all_to_all | solution.py:319
  416.5 36.8 %collective-permute-start.44 = (bf16[128,1536]{1,0:T(8,128)(2,1)S(1)}, bf16[128,1536]{1,0:T(8,128)(2,1)}, u32[]{:S(2)}, u32[]{:S(2)}) collective-permute-start(bf16[128,1536]{1,0:T(8,128)(2,1)S(1)} %fusion.26), channel_id=1, source_target_pairs={{0,1},{1,0},{2,3},{3,2},{4,5},{5,4},{6,7},{7,6},{8,9},{9,8},{10,11... | collective-permute-start | bytes 1179656 | tf_op jit(solution)/shard_map/ppermute | solution.py:309
  (117 other events, 931.1 us)
Sparse Core Ops, SparseCore 0:
  343.7 103.9 all-gather.3

commit v4 on v3

--- a/solution.py
+++ b/solution.py
@@ -314,14 +314,6 @@
     return jnp.concatenate([pair, swapped(pair, "core")])
 
 
-def to_all_groups(x):
-    sent = jnp.broadcast_to(x[None], (32,) + x.shape)
-    took = lax.all_to_all(sent, GROUPS, 0, 0, tiled=True)
-    other = swapped(took, "core")
-    first = lax.axis_index("core") == 0
-    return jnp.where(first, took, other), jnp.where(first, other, took)
-
-
 def _format_first(all_ref, one_ref, two_ref):
     for i in range(16):
         block = all_ref[0, i, 0].astype(F32)
@@ -348,39 +340,167 @@
     )(gathered.reshape(2, 16, 2, n, D))
 
 
-def _format_second(a_ref, b_ref, qkv_ref, out_ref):
-    for c, ref in enumerate((a_ref, b_ref)):
-        turned = []
-        for zh in range(2):
-            h = zh * 2 + c
-            for i in range(16):
-                block = ref[zh * 16 + i].astype(F32)[:24]
+def _ordered(first, own, other):
+    return jnp.where(first, own, other), jnp.where(first, other, own)
+
+
+def _turn(x, cosine, sine):
+    a, b = x[: ROT // 2], x[ROT // 2 : ROT]
+    return jnp.concatenate([a * cosine - b * sine, b * cosine + a * sine, x[ROT:]], axis=0)
+
+
+def _project(
+    me, x_ref, dy_ref, wk_ref, wo_ref, wout_ref, own_ref, other_ref, cos_ref, sin_ref,
+    n_ref, scale_ref, a_ref, m_ref, vec_ref, *heads,
+):
+    first = me[0] == 0
+    lo, hi = _ordered(first, own_ref[...].astype(F32), other_ref[...].astype(F32))
+    vec = jnp.concatenate([lo, hi], axis=1)
+    vec_ref[...] = vec
+    x = x_ref[...].astype(F32)
+    centred = x - jnp.mean(x, axis=1, keepdims=True)
+    scale = lax.rsqrt(jnp.mean(centred * centred, axis=1, keepdims=True) + EPS)
+    n = centred * scale
+    n_ref[...] = n
+    scale_ref[...] = jnp.broadcast_to(scale, scale_ref.shape)
+    a = n * vec[0:1] + vec[1:2]
+    a_ref[...] = a.astype(BF)
+    m_ref[...] = (n * vec[2:3] + vec[3:4]).astype(BF)
+    keep, rest = _ordered(first, a[:, : D // 2], a[:, D // 2 :])
+    qkv = jnp.dot(keep.astype(BF), wk_ref[...], preferred_element_type=F32)
+    qkv = qkv + jnp.dot(rest.astype(BF), wo_ref[...], preferred_element_type=F32)
+    bias = []
+    for p in range(3):
+        part = jnp.zeros((1, HW), F32)
+        for j in range(4):
+            b = p * 4 + j
+            src = (lo, hi)[b // 6]
+            row = 6 + (b % 6) // 2
+            at = (b % 2) * HW
+            part = part + jnp.where(me[1] == j, src[row : row + 1, at : at + HW], 0.0)
+        bias.append(part)
+    qkv = (qkv + jnp.concatenate(bias, axis=1)).T
+    d_mixed = lax.dot_general(
+        wout_ref[...], dy_ref[...], (((1,), (1,)), ((), ())), preferred_element_type=F32
+    ).astype(BF)
+    cosine, sine = cos_ref[...], sin_ref[...]
+    for h in range(TH):
+        kv_ref, qd_ref = heads[h], heads[TH + h]
+        rows = [slice(p * HW + h * HEAD, p * HW + (h + 1) * HEAD) for p in range(3)]
+        qd_ref[:HEAD] = _turn(qkv[rows[0]], cosine, sine).astype(BF) * jnp.asarray(0.125, BF)
+        qd_ref[HEAD:] = d_mixed[h * HEAD : (h + 1) * HEAD]
+        kv_ref[:HEAD] = _turn(qkv[rows[1]], cosine, sine).astype(BF)
+        kv_ref[HEAD:] = qkv[rows[2]].astype(BF)
+
+
+def project(me, *args):
+    return pl.pallas_call(
+        _project,
+        out_shape=(
+            jax.ShapeDtypeStruct((TEAM_ROWS, D), F32),
+            jax.ShapeDtypeStruct((TEAM_ROWS, 128), F32),
+            jax.ShapeDtypeStruct((TEAM_ROWS, D), BF),
+            jax.ShapeDtypeStruct((TEAM_ROWS, D), BF),
+            jax.ShapeDtypeStruct((9, D), F32),
+        )
+        + (jax.ShapeDtypeStruct((2 * HEAD, TEAM_ROWS), BF),) * (2 * TH),
+        in_specs=[pl.BlockSpec(memory_space=pltpu.SMEM)] + _specs(9),
+        out_specs=tuple(_specs(5 + 2 * TH)),
+        compiler_params=pltpu.CompilerParams(vmem_limit_bytes=VMEM_LIMIT),
+        name="project",
+    )(me, *args)
+
+
+SLOT = 128
+
+
+def _tail(
+    me, dq0, dq1, dq2, dkv0, dkv1, dkv2, cos_ref, sin_ref, a_ref, n_ref, dy_ref, mixed_ref,
+    w_ref, early_ref, second_ref, dh_ref, small,
+):
+    cosine, sine = cos_ref[...], -sin_ref[...]
+    parts = [_turn(r[...], cosine, sine) for r in (dq0, dq1, dq2)]
+    parts += [_turn(r[:HEAD], cosine, sine) for r in (dkv0, dkv1, dkv2)]
+    parts += [r[HEAD:] for r in (dkv0, dkv1, dkv2)]
+    turned = jnp.concatenate(parts, axis=0).astype(BF)
+    grads = jnp.concatenate(
+        [
+            jnp.dot(turned, a_ref[...], preferred_element_type=F32),
+            jnp.dot(mixed_ref[...], dy_ref[...], preferred_element_type=F32),
+        ],
+        axis=0,
+    ).T
+    rows = turned.astype(F32).T
+    dh = lax.dot_general(
+        rows.astype(BF), w_ref[...], (((1,), (1,)), ((), ())), preferred_element_type=F32
+    )
+    dh_ref[...] = dh
+    vectors = [early_ref[i : i + 1] for i in range(4)]
+    vectors.append(jnp.sum(dh * n_ref[...], axis=0, keepdims=True))
+    vectors.append(jnp.sum(dh, axis=0, keepdims=True))
+    bias = jnp.sum(rows, axis=0, keepdims=True)
+    for p in range(3):
+        part = bias[:, p * HW : (p + 1) * HW]
+        vectors.append(
+            jnp.concatenate([jnp.where(me[1] == j, part, 0.0) for j in range(4)], axis=1)
+        )
+    small[...] = jnp.zeros_like(small)
+    for v, vector in enumerate(vectors):
+        for i in range(6):
+            at = v * 6 + i
+            small[at % 32, at // 32 : at // 32 + 1, :] = vector[:, i * SLOT : (i + 1) * SLOT]
+    for g in range(32):
+        second_ref[g, :, :D] = grads[24 * g : 24 * (g + 1)].astype(BF)
+        second_ref[g, :, D:] = small[g].astype(BF)
+
+
+def tail(me, *args):
+    return pl.pallas_call(
+        _tail,
+        out_shape=(
+            jax.ShapeDtypeStruct((32, 24, D + SLOT), BF),
+            jax.ShapeDtypeStruct((TEAM_ROWS, D), F32),
+        ),
+        in_specs=[pl.BlockSpec(memory_space=pltpu.SMEM)] + _specs(14),
+        out_specs=tuple(_specs(2)),
+        scratch_shapes=[pltpu.VMEM((32, 24, SLOT), F32)],
+        compiler_params=pltpu.CompilerParams(vmem_limit_bytes=VMEM_LIMIT),
+        name="tail",
+    )(me, *args)
+
+
+def _format_second(me, own_ref, other_ref, qkv_ref, out_ref, small_ref):
+    first = me[2] == 0
+    turned = [[], []]
+    for zh in range(2):
+        for i in range(16):
+            g = zh * 16 + i
+            pair = _ordered(first, own_ref[g].astype(F32), other_ref[g].astype(F32))
+            for c, block in enumerate(pair):
+                h = zh * 2 + c
                 for p in range(3):
                     at = p * D + h * HW
                     qkv_ref[24 * i : 24 * (i + 1), at : at + HW] = block[:, p * HW : (p + 1) * HW]
-                turned.append(block[:, 3 * HW :])
-        out_ref[c * HW : (c + 1) * HW, :] = jnp.concatenate(turned, axis=0).T
-
-
-def format_second(a, b):
+                turned[c].append(block[:, 3 * HW : D])
+                for slot in range(2):
+                    small_ref[c, slot * 32 + g : slot * 32 + g + 1, :] = block[slot : slot + 1, D:]
+    for c in range(2):
+        out_ref[c * HW : (c + 1) * HW, :] = jnp.concatenate(turned[c], axis=0).T
+
+
+def format_second(me, own, other):
     return pl.pallas_call(
         _format_second,
         out_shape=(
             jax.ShapeDtypeStruct((384, 3 * D), F32),
             jax.ShapeDtypeStruct((384, D), F32),
+            jax.ShapeDtypeStruct((2, 64, SLOT), F32),
         ),
-        in_specs=_specs(2),
-        out_specs=tuple(_specs(2)),
+        in_specs=[pl.BlockSpec(memory_space=pltpu.SMEM)] + _specs(2),
+        out_specs=tuple(_specs(3)),
         compiler_params=pltpu.CompilerParams(vmem_limit_bytes=VMEM_LIMIT),
         name="format_second",
-    )(a, b)
-
-
-def rotate(x, cosine, sine):
-    a, b = x[:, :, : ROT // 2], x[:, :, ROT // 2 : ROT]
-    return jnp.concatenate(
-        [a * cosine - b * sine, b * cosine + a * sine, x[:, :, ROT:]], axis=2
-    )
+    )(me, own, other)
 
 
 def dot(a, b, dims):
@@ -424,48 +544,39 @@
     def whole_rows(keep, send):
         return jnp.concatenate(ordered(keep, swapped(send, "fsdp")))
 
+    me = jnp.stack([fsdp, mine, core]).astype(jnp.int32)
+
     x4 = team_rows(tokens)
-    w_q = whole_rows(qkv_columns(w_qkv, mine), qkv_columns(w_qkv, theirs))
+    w_keep = qkv_columns(w_qkv, mine)
+    w_rest = swapped(qkv_columns(w_qkv, theirs), "fsdp")
     dy4 = team_rows(cotangent)
     vectors = jnp.concatenate(
-        [ln_gain_attn, ln_bias_attn, ln_gain_mlp, ln_bias_mlp, b_out, b_fc2, b_qkv]
-    ).reshape(27, 128)
-    vectors = jnp.stack(ordered(vectors, swapped(vectors, "fsdp"))).astype(F32).reshape(2, -1)
-    g_attn, c_attn, g_mlp, c_mlp, bias_out, bias_two = (
-        vectors[:, i * 384 : (i + 1) * 384].reshape(D) for i in range(6)
-    )
-    bias_qkv = vectors[:, 6 * 384 :].reshape(3, 4, HW)
-    bias_qkv = lax.dynamic_index_in_dim(bias_qkv, mine, 1, keepdims=False).reshape(3 * HW)
+        [
+            v.reshape(-1, 384)
+            for v in (ln_gain_attn, ln_bias_attn, ln_gain_mlp, ln_bias_mlp, b_out, b_fc2, b_qkv)
+        ]
+    )
+    w_o = lax.dynamic_slice_in_dim(w_out, core * HW, HW, axis=0)
     w_one = whole_rows(columns(w_fc1, mine, D), columns(w_fc1, theirs, D))
-    w_o = lax.dynamic_slice_in_dim(w_out, core * HW, HW, axis=0)
     w_two = lax.dynamic_slice_in_dim(w_fc2, core * D, D, axis=0)
     b_one = lax.dynamic_slice_in_dim(b_fc1, core * D, D, axis=0).astype(F32)
 
     fplan, bplan = make_plan(block_order, team, z, xh, y)
 
-    x = x4.astype(F32)
-    centred = x - jnp.mean(x, axis=1, keepdims=True)
-    scale = lax.rsqrt(jnp.mean(centred * centred, axis=1, keepdims=True) + EPS)
-    n = centred * scale
-    a_attn = (n * g_attn + c_attn).astype(BF)
-    a_mlp = (n * g_mlp + c_mlp).astype(BF)
-
-    qkv = dot(w_q, a_attn, ((0,), (1,))) + bias_qkv[:, None]
-    qkv = qkv.reshape(3, TH, HEAD, TEAM_ROWS)
     anchors = pick(block_order, group * 4 + (jnp.arange(4, dtype=jnp.int32) ^ team))
     places = (anchors[:, None] * BLK + jnp.arange(BLK, dtype=jnp.int32)[None, :]).reshape(-1)
     frequency = jnp.exp(jnp.arange(ROT // 2, dtype=F32) * (-2.0 * math.log(10000.0) / ROT))
     angles = frequency[:, None] * places.astype(F32)[None, :]
     cosine, sine = jnp.cos(angles), jnp.sin(angles)
-    turned = rotate(qkv[:2], cosine, sine).astype(BF)
-    values = qkv[2].astype(BF)
-    d_mixed = dot(w_o, dy4, ((1,), (1,))).astype(BF).reshape(TH, HEAD, TEAM_ROWS)
-    kv_all, qd_all = [], []
-    for h in range(TH):
-        kv = jnp.concatenate([turned[1, h], values[h]], axis=0)
-        qd = jnp.concatenate([turned[0, h] * jnp.asarray(0.125, BF), d_mixed[h]], axis=0)
-        kv_all.append(from_keys(kv))
-        qd_all.append(jnp.stack([qd] + [from_y(qd, i) for i in range(1, 4)]))
+
+    n, scale, a_attn, a_mlp, vec, *heads = project(
+        me, x4, dy4, w_keep, w_rest, w_o, vectors, swapped(vectors, "fsdp"), cosine, sine
+    )
+    kv_all = [from_keys(kv) for kv in heads[:TH]]
+    qd_all = [
+        jnp.stack([qd] + [from_y(qd, i) for i in range(1, 4)]) for qd in heads[TH:]
+    ]
+    d_mixed = [qd[HEAD:] for qd in heads[TH:]]
 
     hidden_pre = dot(a_mlp, w_one, ((1,), (0,))) + b_one
     hidden_act, gelu_pull = jax.vjp(partial(jax.nn.gelu, approximate=False), hidden_pre)
@@ -478,29 +589,16 @@
     grad_b_one = jnp.sum(d_hidden.astype(F32), axis=0)
     dh_mlp = dot(d_hidden, w_one, ((1,), (1,)))
 
-    def row(vectors, width):
-        return jnp.pad(vectors.reshape(32, 1, width).astype(BF), ((0, 0), (0, 0), (0, D - width)))
-
-    def summed(parts):
-        return jnp.sum(lax.all_to_all(parts, GROUPS, 0, 0, tiled=True).astype(F32), axis=0)
-
+    early = jnp.stack(
+        [
+            jnp.sum(dh_mlp * n, axis=0),
+            jnp.sum(dh_mlp, axis=0),
+            jnp.sum(cotangent.astype(F32), axis=0),
+            grad_b_one,
+        ]
+    )
     first = jnp.concatenate(
-        [
-            grad_one.astype(BF).reshape(32, 24, D),
-            grad_two.astype(BF).reshape(32, 24, D),
-            row(
-                jnp.concatenate(
-                    [
-                        jnp.sum(dh_mlp * n, axis=0),
-                        jnp.sum(dh_mlp, axis=0),
-                        jnp.sum(cotangent.astype(F32), axis=0),
-                        grad_b_one,
-                    ]
-                ),
-                96,
-            ),
-        ],
-        axis=1,
+        [grad_one.astype(BF).reshape(32, 24, D), grad_two.astype(BF).reshape(32, 24, D)], axis=1
     )
 
     def to_owner(part):
@@ -554,98 +652,69 @@
     grads_2 = pulled(*raw_2)
     mixed = jnp.concatenate([whole_0, whole_1, whole_2]).astype(BF)
 
-    shares = first[48:]
-    shares = shares + jnp.where(group < 24, swapped(shares, "fsdp"), 0.0)
-    first = jnp.concatenate(
-        [to_owner(first[:24].astype(BF)), first[24:48].astype(BF), shares.astype(BF)], axis=0
-    )
+    first = jnp.concatenate([to_owner(first[:24].astype(BF)), first[24:].astype(BF)], axis=0)
     first_all = lax.all_gather(first, CTX, axis=0, tiled=False)
 
-    dqs, dks, dvs = [], [], []
-    for dq, dkv in (grads_0, grads_1, grads_2):
-        dqs.append(dq)
-        dks.append(dkv[:HEAD])
-        dvs.append(dkv[HEAD:])
-    back = rotate(jnp.stack([jnp.stack(dqs), jnp.stack(dks)]), cosine, -sine)
-    d_qkv = jnp.concatenate([back, jnp.stack(dvs)[None]], axis=0).astype(BF)
-    d_qkv = d_qkv.reshape(3 * HW, TEAM_ROWS)
-
-    grad_qkv = dot(a_attn, d_qkv, ((0,), (1,)))
-    grad_out_t = dot(dy4, mixed, ((0,), (1,)))
-    dh_attn = dot(d_qkv, w_q, ((0,), (1,)))
-    grad_b_qkv = jnp.sum(d_qkv.astype(F32), axis=1).reshape(3, 1, HW)
-    grad_b_qkv = jnp.where(jnp.arange(4, dtype=jnp.int32)[:, None] == mine, grad_b_qkv, 0.0)
+    w_q = jnp.concatenate(ordered(w_keep, w_rest))
+    second, dh_attn = tail(
+        me,
+        *(dq for dq, _ in (grads_0, grads_1, grads_2)),
+        *(dkv for _, dkv in (grads_0, grads_1, grads_2)),
+        cosine,
+        sine,
+        a_attn,
+        n,
+        dy4,
+        mixed,
+        w_q,
+        early,
+    )
+    second = jnp.sum(lax.all_to_all(second, GROUPS, 0, 0, tiled=True).astype(F32), axis=0)
+    shares = second[:, D:]
+    whole = (jnp.arange(24, dtype=jnp.int32)[:, None] == 0) & (group >= 18) & (group < 24)
+    shares = shares + jnp.where(whole, 0.0, swapped(shares, "fsdp"))
+    second = second.astype(BF)
     second = jnp.concatenate(
-        [
-            jnp.concatenate([grad_qkv.astype(BF), grad_out_t.astype(BF)], axis=1).reshape(32, 24, D),
-            row(
-                jnp.concatenate(
-                    [
-                        jnp.sum(dh_attn * n, axis=0),
-                        jnp.sum(dh_attn, axis=0),
-                        grad_b_qkv.reshape(-1),
-                    ]
-                ),
-                120,
-            ),
-        ],
-        axis=1,
-    )
-    second = summed(second)
-    shares = second[24:]
-    shares = shares + swapped(shares, "fsdp")
-    second = jnp.concatenate(
-        [
-            jnp.concatenate(
-                [to_owner(second[:24, : 3 * HW].astype(BF)), second[:24, 3 * HW :].astype(BF)], axis=1
-            ),
-            shares.astype(BF),
-        ],
-        axis=0,
-    )
-    second_a, second_b = to_all_groups(second)
+        [to_owner(second[:, : 3 * HW]), second[:, 3 * HW : D], shares.astype(BF)], axis=1
+    )
+    sent = jnp.broadcast_to(second[None], (32,) + second.shape)
+    second = lax.all_to_all(sent, GROUPS, 0, 0, tiled=True)
+    second_other = swapped(second, "core")
 
     out_part = out_part + dot(mixed, w_o, ((0,), (0,)))
-    dn_part = dh_attn * g_attn + dh_mlp * g_mlp
+    dn_part = dh_attn * vec[0:1] + dh_mlp * vec[2:3]
     both = jnp.concatenate([out_part, dn_part], axis=1).reshape(4, BLK, 2 * D)
     both = both[:2] + swapped(both[2:].astype(BF), "core").astype(F32)
     both = both[0] + swapped(both[1].astype(BF), "fsdp").astype(F32)
-    own = x[:BLK]
-    layer_out = (own + both[:, :D] + bias_out + bias_two).astype(BF)
+    layer_out = (tokens.astype(F32) + both[:, :D] + vec[4:5] + vec[5:6]).astype(BF)
     dn = both[:, D:]
-    grad_tokens = cotangent.astype(F32) + scale[:BLK] * (
+    grad_tokens = cotangent.astype(F32) + scale[:BLK, :1] * (
         dn
         - jnp.mean(dn, axis=1, keepdims=True)
         - n[:BLK] * jnp.mean(dn * n[:BLK], axis=1, keepdims=True)
     )
 
     grad_w_one, grad_w_two = format_first(first_all)
-    grad_w_qkv, grad_w_out = format_second(second_a, second_b)
-    tails = first_all.reshape(32, 2, -1, D)[:, :, 48, :96].astype(F32)
-    tail_a, tail_b = tails[:, 0], tails[:, 1]
-    early = (tail_a[:24] + tail_b[:24]).reshape(3, D)
-    grad_b_one = jnp.concatenate([tail_a[24:].reshape(D), tail_b[24:].reshape(D)])
-    late = second_a[:, 24, :120].astype(F32) + second_b[:, 24, :120].astype(F32)
-    late = late.reshape(-1)
-
-    def half(vector):
-        width = vector.shape[0] // 2
-        return lax.dynamic_slice_in_dim(vector, fsdp * width, width)
-
-    grad_b_out = half(early[2])
+    grad_w_qkv, grad_w_out, small = format_second(me, second, second_other)
+    summed = small[0] + small[1]
+
+    def half(at, rows):
+        return lax.dynamic_slice_in_dim(summed[at : at + rows], fsdp * (rows // 2), rows // 2).reshape(-1)
+
+    grad_b_out = half(12, 6)
     return (
         layer_out,
         grad_tokens,
-        half(late[:D]),
-        half(late[D : 2 * D]),
-        half(early[0]),
-        half(early[1]),
+        half(24, 6),
+        half(30, 6),
+        half(0, 6),
+        half(6, 6),
         grad_w_qkv,
-        half(late[2 * D :]),
+        half(36, 18),
         grad_w_out,
         grad_b_out,
         grad_w_one,
-        grad_b_one,
+        small[:, 18:24].reshape(-1),
         grad_w_two,
         grad_b_out,
     )

time: 494 us -> 487 us (0.986)
  starting transfers between devices: 154 us -> 177 us
  local copies, waits for them, and re-layouts: 61.2 us -> 46.6 us
  Pallas kernels: 126 us -> 136 us
  waiting for transfers between devices: 42.3 us -> 32.6 us
  other arithmetic: 59.6 us -> 51.3 us
  matrix products: 26.4 us -> 19.3 us
    ppermute x12 -> x11, starting transfers between devices: 31.1 us -> 52.7 us  [swapped(): return lax.ppermute(x, axis, [(0, 1), (1, 0)])]
    all_to_all x2, waiting for transfers between devices: 23.2 us -> 11.7 us  [the longest x1 11.7 us: local(): second = lax.all_to_all(sent, GROUPS, 0, 0, tiled=True)]
    pallas_call x0 -> x2, Pallas kernels: none -> 10.2 us  [the longest x1 5.68 us: tail(): pl.pallas_call(_tail, out_shape=(jax.ShapeDtypeStruct((32, 24, D + SLOT),...]
    all_to_all x3, starting transfers between devices: 28.1 us -> 19.1 us  [to_keys(): return lax.all_to_all(parts, KEYS, 0, 0, tiled=True)]
    ppermute x18, starting transfers between devices: 15.3 us -> 23.6 us  [to_y(): return lax.ppermute(x, 'y', [(d, (d + i) % 4) for d in range(4)])]
    reshape x3 -> x14, local copies, waits for them, and re-layouts: 0.23 us -> 8.49 us  [the longest x7 4.94 us: local(): v.reshape(-1, 384)]
    ppermute x18, waiting for transfers between devices: 8.16 us -> 0.39 us  [from_y(): return lax.ppermute(x, 'y', [((d + i) % 4, d) for d in range(4)])]
    concatenate x6 -> x1, local copies, waits for them, and re-layouts: 7.52 us -> 0.13 us  [local(): jnp.concatenate([v.reshape(-1, 384) for v in (ln_gain_attn, ln_bias_attn,...]
  transfers between devices with their start and end apart: 60 -> 59, of which waited for: 8 -> 7; matrix products, arithmetic and copies ran while one was open for 25% -> 21% of each run, Pallas kernels for 20% -> 27%
where the time goes in v4:
time: 487 us; the launch traced here: 479 us
  starting transfers between devices  177 us (36%)
  Pallas kernels  136 us (28%)
  other arithmetic  51.3 us (11%)
  local copies, waits for them, and re-layouts  46.6 us (10%)
  waiting for transfers between devices  32.6 us (7%)
  matrix products  19.3 us (4%)
  between operations  15.5 us (3%)
    pallas_call x3, Pallas kernels, attend_backward(): pl.pallas_call(_backward, out_shape=(jax.ShapeDtypeStruct((4, KW, TEAM_RO...  65.6 us
    ppermute x11, starting transfers between devices, swapped(): return lax.ppermute(x, axis, [(0, 1), (1, 0)])  52.7 us
    pallas_call x3, Pallas kernels, attend_forward(): pl.pallas_call(_forward, out_shape=jax.ShapeDtypeStruct((4, KW + 16, TEAM...  49.6 us
    ppermute x18, starting transfers between devices, from_y(): return lax.ppermute(x, 'y', [((d + i) % 4, d) for d in range(4)])  26.8 us
    ppermute x18, starting transfers between devices, to_y(): return lax.ppermute(x, 'y', [(d, (d + i) % 4) for d in range(4)])  23.6 us
    all_to_all x3, starting transfers between devices, from_keys(): lax.all_to_all(jnp.broadcast_to(x[None], (8,) + x.shape), KEYS, 0, 0, til...  20.7 us
    dot_general x7, matrix products, dot(): return lax.dot_general(a, b, (dims, ((), ())), preferred_element_type=F32)  19.3 us
    all_to_all x3, starting transfers between devices, to_keys(): return lax.all_to_all(parts, KEYS, 0, 0, tiled=True)  19.1 us
  transfers between devices with their start and end apart: 59, of which 7 were waited for; matrix products, arithmetic and copies ran while one was open for 21% of the time, Pallas kernels for 27%

profile of v4, /device:TPU:1, one launch (start us, length us, event | category | flops | bytes accessed | tf_op | source)
XLA Modules:
  0.0 479.1 jit_solution(14769589274100284741)
XLA Ops:
  40.1 7.3 %collective-permute-done.4.wo_ref = bf16[384,576]{1,0:T(8,128)(2,1)S(1)} collective-permute-done((bf16[384,576]{1,0:T(8,128)(2,1)}, bf16[384,576]{1,0:T(8,128)(2,1)S(1)}, u32[]{:S(2)}, u32[]{:S(2)}) %collective-permute-start.4) | collective-permute-done | bytes 442400 | tf_op jit(solution)/shard_map/ppermute | solution.py:309
  50.6 4.5 project.1
  62.5 7.4 %all-to-all-start = ((bf16[8,128,512]{2,1,0:T(8,128)(2,1)}), bf16[8,128,512]{2,1,0:T(8,128)(2,1)}, u32[]{:S(2)}, u32[]{:S(2)}) async-start(bf16[8,128,512]{2,1,0:T(8,128)(2,1)} %broadcast_in_dim.94), calls=%async_computation | async-start | bytes 2097152 | tf_op jit(solution)/shard_map/all_to_all | solution.py:297
  72.8 10.2 %multiply_convert_fusion = (bf16[512,768]{1,0:T(8,128)(2,1)S(1)}, f32[512,768]{1,0:T(8,128)S(1)}, f32[512,768]{1,0:T(8,128)S(1)}) fusion(f32[768]{0:T(1024)S(1)} %dynamic-slice_convert_fusion, bf16[512,768]{1,0:T(8,128)(2,1)S(1)} %copy-done.62, bf16[384,768]{1,0:T(8,128)(2,1)S(1)} %get-tuple-element.229, bf16[384,768]{1,0:T(8,128)(2,1)S(1)} %get-tuple-element.228), kind=kOutput, calls=%fused_computation.18 | convolution fusion | flops 632291328 | bytes 5901312 | tf_op jit(solution)/shard_map/dot_general | solution.py:507
  90.6 6.6 %all-to-all-start.1 = ((bf16[8,128,512]{2,1,0:T(8,128)(2,1)}), bf16[8,128,512]{2,1,0:T(8,128)(2,1)}, u32[]{:S(2)}, u32[]{:S(2)}) async-start(bf16[8,128,512]{2,1,0:T(8,128)(2,1)} %broadcast_in_dim.95), calls=%async_computation.1 | async-start | bytes 2097152 | tf_op jit(solution)/shard_map/all_to_all | solution.py:297
  97.2 2.9 pad_maximum_fusion
  109.2 16.5 %attend_forward.3 = bf16[4,80,512]{2,1,0:T(8,128)(2,1)} custom-call(s32[16]{0:T(128)} %get-tuple-element.171.qsrc, s32[16]{0:T(128)} %copy-done.59, s32[32]{0:T(128)} %get-tuple-element.173.ksrc, s32[32]{0:T(128)} %copy-done.60, s32[4]{0:T(128)} %get-tuple-element.128.nfull, s32[4]{0:T(128)} %get-tuple-element.129.nall, ...), custom_call_target="tpu_custom_call" | custom-call | flops 2147483648 | bytes 3145728 | tf_op jit(solution)/shard_map/attend_forward/pallas_call | solution.py:217
  131.7 6.6 %all-to-all-start.2 = ((bf16[8,128,512]{2,1,0:T(8,128)(2,1)}), bf16[8,128,512]{2,1,0:T(8,128)(2,1)S(1)}, u32[]{:S(2)}, u32[]{:S(2)}) async-start(bf16[8,128,512]{2,1,0:T(8,128)(2,1)} %broadcast_in_dim.96), calls=%async_computation.2 | async-start | bytes 2097152 | tf_op jit(solution)/shard_map/all_to_all | solution.py:297
  138.4 16.5 %attend_forward.4 = bf16[4,80,512]{2,1,0:T(8,128)(2,1)} custom-call(s32[16]{0:T(128)} %get-tuple-element.171.qsrc, s32[16]{0:T(128)} %copy-done.59, s32[32]{0:T(128)} %get-tuple-element.173.ksrc, s32[32]{0:T(128)} %copy-done.60, s32[4]{0:T(128)} %get-tuple-element.128.nfull, s32[4]{0:T(128)} %get-tuple-element.129.nall, ...), custom_call_target="tpu_custom_call" | custom-call | flops 2147483648 | bytes 3145728 | tf_op jit(solution)/shard_map/attend_forward/pallas_call | solution.py:217
  156.6 2.9 collective-permute-start.18
  167.1 7.7 %all-to-all-start.4 = ((bf16[32,48,768]{2,1,0:T(8,128)(2,1)}), bf16[32,48,768]{2,1,0:T(8,128)(2,1)}, u32[]{:S(2)}, u32[]{:S(2)}) async-start(bf16[32,48,768]{2,1,0:T(8,128)(2,1)} %pad_maximum_fusion), calls=%async_computation.4 | async-start | bytes 4718592 | tf_op jit(solution)/shard_map/all_to_all | solution.py:638
  174.8 16.5 %attend_forward.5 = bf16[4,80,512]{2,1,0:T(8,128)(2,1)} custom-call(s32[16]{0:T(128)} %get-tuple-element.171.qsrc, s32[16]{0:T(128)} %copy-done.59, s32[32]{0:T(128)} %get-tuple-element.173.ksrc, s32[32]{0:T(128)} %copy-done.60, s32[4]{0:T(128)} %get-tuple-element.128.nfull, s32[4]{0:T(128)} %get-tuple-element.129.nall, ...), custom_call_target="tpu_custom_call" | custom-call | flops 2147483648 | bytes 3145728 | tf_op jit(solution)/shard_map/attend_forward/pallas_call | solution.py:217
  191.3 3.5 collective-permute-start.25
  204.1 21.9 %attend_backward.3 = (bf16[4,64,512]{2,1,0:T(8,128)(2,1)}, bf16[8,128,512]{2,1,0:T(8,128)(2,1)}) custom-call(s32[16]{0:T(128)} %get-tuple-element.171.qsrc, s32[16]{0:T(128)} %copy-done.59, s32[32]{0:T(128)} %get-tuple-element.173.ksrc, s32[32]{0:T(128)} %copy-done.60, s32[8]{0:T(128)} %get-tuple-element.175.nfull, s32[8]{0:T(128)} %get-tuple-element.176.nall, ...), custom_call_target="tpu_custom_call" | custom-call | flops 5368709120 | bytes 6291456 | tf_op jit(solution)/shard_map/attend_backward/pallas_call | solution.py:234
  227.8 2.9 collective-permute-start.30
  237.5 6.7 %all-to-all-start.3 = ((bf16[8,128,512]{2,1,0:T(8,128)(2,1)}), bf16[8,128,512]{2,1,0:T(8,128)(2,1)S(1)}, u32[]{:S(2)}, u32[]{:S(2)}) async-start(bf16[8,128,512]{2,1,0:T(8,128)(2,1)} %get-tuple-element.147), calls=%async_computation.3 | async-start | bytes 2097152 | tf_op jit(solution)/shard_map/all_to_all | solution.py:301
  246.2 21.9 %attend_backward.4 = (bf16[4,64,512]{2,1,0:T(8,128)(2,1)}, bf16[8,128,512]{2,1,0:T(8,128)(2,1)}) custom-call(s32[16]{0:T(128)} %get-tuple-element.171.qsrc, s32[16]{0:T(128)} %copy-done.59, s32[32]{0:T(128)} %get-tuple-element.173.ksrc, s32[32]{0:T(128)} %copy-done.60, s32[8]{0:T(128)} %get-tuple-element.175.nfull, s32[8]{0:T(128)} %get-tuple-element.176.nall, ...), custom_call_target="tpu_custom_call" | custom-call | flops 5368709120 | bytes 6291456 | tf_op jit(solution)/shard_map/attend_backward/pallas_call | solution.py:234
  277.3 21.9 %attend_backward.5 = (bf16[4,64,512]{2,1,0:T(8,128)(2,1)}, bf16[8,128,512]{2,1,0:T(8,128)(2,1)}) custom-call(s32[16]{0:T(128)} %get-tuple-element.171.qsrc, s32[16]{0:T(128)} %copy-done.59, s32[32]{0:T(128)} %get-tuple-element.173.ksrc, s32[32]{0:T(128)} %copy-done.60, s32[8]{0:T(128)} %get-tuple-element.175.nfull, s32[8]{0:T(128)} %get-tuple-element.176.nall, ...), custom_call_target="tpu_custom_call" | custom-call | flops 5368709120 | bytes 6291456 | tf_op jit(solution)/shard_map/attend_backward/pallas_call | solution.py:234
  299.2 8.8 %all-to-all-start.6 = ((bf16[8,128,512]{2,1,0:T(8,128)(2,1)}), bf16[8,128,512]{2,1,0:T(8,128)(2,1)}, u32[]{:S(2)}, u32[]{:S(2)}) async-start(bf16[8,128,512]{2,1,0:T(8,128)(2,1)} %get-tuple-element.182), calls=%async_computation.6 | async-start | bytes 2097152 | tf_op jit(solution)/shard_map/all_to_all | solution.py:301
  310.1 9.9 %all-to-all-done.6 = bf16[8,128,512]{2,1,0:T(8,128)(2,1)} async-done(((bf16[8,128,512]{2,1,0:T(8,128)(2,1)}), bf16[8,128,512]{2,1,0:T(8,128)(2,1)}, u32[]{:S(2)}, u32[]{:S(2)}) %all-to-all-start.6) | async-done | bytes 1048608 | tf_op jit(solution)/shard_map/all_to_all | solution.py:301
  320.0 3.6 all-to-all-start.5
  323.6 4.0 multiply_reduce_fusion
  328.9 4.9 %collective-permute-start.42 = (bf16[64,512]{1,0:T(8,128)(2,1)S(1)}, bf16[64,512]{1,0:T(8,128)(2,1)S(1)}, u32[]{:S(2)}, u32[]{:S(2)}) collective-permute-start(bf16[64,512]{1,0:T(8,128)(2,1)S(1)} %get-tuple-element.253), channel_id=1, source_target_pairs={{0,12},{4,0},{8,4},{12,8},{1,13},{5,1},{9,5},{13,9},{2,14},{6,2},{... | collective-permute-start | bytes 196616 | tf_op jit(solution)/shard_map/ppermute | solution.py:293
  348.8 5.7 %tail.1 = (bf16[32,24,896]{2,1,0:T(8,128)(2,1)}, f32[512,768]{1,0:T(8,128)}) custom-call(s32[3]{0:T(128)} %pad_add_fusion.me, f32[64,512]{1,0:T(8,128)} %convert_add_fusion.4.dq0, f32[64,512]{1,0:T(8,128)} %convert_add_fusion.3.dq1, f32[64,512]{1,0:T(8,128)} %convert_add_fusion.2.dq2, f32[128,512]{1,0:T(8,128)} %convert_reduce_fusion.4.dkv0, ...), custom_call_target="tpu_custom_call" | custom-call | tf_op jit(solution)/shard_map/tail/pallas_call | solution.py:458
  354.5 8.0 %all-to-all-start.7 = ((bf16[32,24,896]{2,1,0:T(8,128)(2,1)}), bf16[32,24,896]{2,1,0:T(8,128)(2,1)}, u32[]{:S(2)}, u32[]{:S(2)}) async-start(bf16[32,24,896]{2,1,0:T(8,128)(2,1)} %get-tuple-element.198), calls=%async_computation.7 | async-start | bytes 2752512 | tf_op jit(solution)/shard_map/all_to_all | solution.py:672
  368.0 30.3 %collective-permute-start.43 = (bf16[2,128,1536]{2,1,0:T(8,128)(2,1)}, bf16[2,128,1536]{2,1,0:T(8,128)(2,1)S(1)}, u32[]{:S(2)}, u32[]{:S(2)}) collective-permute-start(bf16[2,128,1536]{2,1,0:T(8,128)(2,1)} %bitcast.73), channel_id=1, source_target_pairs={{0,2},{2,0},{1,3},{3,1},{4,6},{6,4},{5,7},{7,5},{8,10},{10,8},{9,1... | collective-permute-start | bytes 2359304 | tf_op jit(solution)/shard_map/ppermute | solution.py:309
  399.8 3.1 collective-permute-start.46
  407.7 16.6 %all-to-all-start.8 = ((bf16[32,24,896]{2,1,0:T(8,128)(2,1)}), bf16[32,24,896]{2,1,0:T(8,128)(2,1)}, u32[]{:S(2)}, u32[]{:S(2)}) async-start(bf16[32,24,896]{2,1,0:T(8,128)(2,1)} %broadcast_in_dim.103), calls=%async_computation.8 | async-start | bytes 2752512 | tf_op jit(solution)/shard_map/all_to_all | solution.py:681
  427.3 11.7 %all-to-all-done.8.own_ref = bf16[32,24,896]{2,1,0:T(8,128)(2,1)} async-done(((bf16[32,24,896]{2,1,0:T(8,128)(2,1)}), bf16[32,24,896]{2,1,0:T(8,128)(2,1)}, u32[]{:S(2)}, u32[]{:S(2)}) %all-to-all-start.8) | async-done | bytes 1376288 | tf_op jit(solution)/shard_map/all_to_all | solution.py:681
  439.0 11.9 %collective-permute-start.47 = (bf16[32,24,896]{2,1,0:T(8,128)(2,1)}, bf16[32,24,896]{2,1,0:T(8,128)(2,1)S(1)}, u32[]{:S(2)}, u32[]{:S(2)}) collective-permute-start(bf16[32,24,896]{2,1,0:T(8,128)(2,1)} %all-to-all-done.8.own_ref), channel_id=1, source_target_pairs={{0,2},{2,0},{1,3},{3,1},{4,6},{6,4},{5,7},{7,5},{8,10},{10,8},{9,1... | collective-permute-start | bytes 4128776 | tf_op jit(solution)/shard_map/ppermute | solution.py:309
  455.3 4.5 format_second.1
  464.8 6.5 %format_first.1 = (f32[384,3072]{1,0:T(8,128)}, f32[1536,768]{1,0:T(8,128)}) custom-call(bf16[2,16,2,48,768]{4,3,2,1,0:T(8,128)(2,1)} %bitcast.128), custom_call_target="tpu_custom_call" | custom-call | tf_op jit(solution)/shard_map/format_first/pallas_call | solution.py:326
  (383 shorter events, 149.7 us)
Async XLA Ops:
  12.3 37.4 %collective-permute-start.5 = (bf16[9,384]{1,0:T(8,128)(2,1)S(1)}, bf16[9,384]{1,0:T(8,128)(2,1)S(1)}, u32[]{:S(2)}, u32[]{:S(2)}) collective-permute-start(bf16[9,384]{1,0:T(8,128)(2,1)S(1)} %concatenate.51.own_ref), channel_id=1, source_target_pairs={{0,1},{1,0},{2,3},{3,2},{4,5},{5,4},{6,7},{7,6},{8,9},{9,8},{10,11... | collective-permute-start | bytes 20744 | tf_op jit(solution)/shard_map/ppermute | solution.py:309
  17.8 52.1 %collective-permute-start.6 = (bf16[384,768]{1,0:T(8,128)(2,1)}, bf16[384,768]{1,0:T(8,128)(2,1)}, u32[]{:S(2)}, u32[]{:S(2)}) collective-permute-start(bf16[384,768]{1,0:T(8,128)(2,1)} %constant_dynamic-slice_fusion.5), channel_id=1, source_target_pairs={{0,1},{1,0},{2,3},{3,2},{4,5},{5,4},{6,7},{7,6},{8,9},{9,8},{10,11... | collective-permute-start | bytes 1769480 | tf_op jit(solution)/shard_map/ppermute | solution.py:309
  55.2 31.8 %collective-permute-start.9 = (bf16[128,512]{1,0:T(8,128)(2,1)}, bf16[128,512]{1,0:T(8,128)(2,1)}, u32[]{:S(2)}, u32[]{:S(2)}) collective-permute-start(bf16[128,512]{1,0:T(8,128)(2,1)} %get-tuple-element.110), channel_id=1, source_target_pairs={{12,0},{0,4},{4,8},{8,12},{13,1},{1,5},{5,9},{9,13},{14,2},{2,6},{... | collective-permute-start | bytes 393224 | tf_op jit(solution)/shard_map/ppermute | solution.py:289
  56.5 43.6 %collective-permute-start.8 = (bf16[128,512]{1,0:T(8,128)(2,1)}, bf16[128,512]{1,0:T(8,128)(2,1)}, u32[]{:S(2)}, u32[]{:S(2)}) collective-permute-start(bf16[128,512]{1,0:T(8,128)(2,1)} %get-tuple-element.110), channel_id=1, source_target_pairs={{8,0},{12,4},{0,8},{4,12},{9,1},{13,5},{1,9},{5,13},{10,2},{14,6},... | collective-permute-start | bytes 393224 | tf_op jit(solution)/shard_map/ppermute | solution.py:289
  59.1 41.5 %collective-permute-start.7 = (bf16[128,512]{1,0:T(8,128)(2,1)}, bf16[128,512]{1,0:T(8,128)(2,1)}, u32[]{:S(2)}, u32[]{:S(2)}) collective-permute-start(bf16[128,512]{1,0:T(8,128)(2,1)} %get-tuple-element.110), channel_id=1, source_target_pairs={{4,0},{8,4},{12,8},{0,12},{5,1},{9,5},{13,9},{1,13},{6,2},{10,6},{... | collective-permute-start | bytes 393224 | tf_op jit(solution)/shard_map/ppermute | solution.py:289
  60.2 42.3 %collective-permute-start.15 = (bf16[128,512]{1,0:T(8,128)(2,1)}, bf16[128,512]{1,0:T(8,128)(2,1)}, u32[]{:S(2)}, u32[]{:S(2)}) collective-permute-start(bf16[128,512]{1,0:T(8,128)(2,1)} %get-tuple-element.118), channel_id=1, source_target_pairs={{12,0},{0,4},{4,8},{8,12},{13,1},{1,5},{5,9},{9,13},{14,2},{2,6},{... | collective-permute-start | bytes 393224 | tf_op jit(solution)/shard_map/ppermute | solution.py:289
  70.0 36.4 %collective-permute-start.14 = (bf16[128,512]{1,0:T(8,128)(2,1)}, bf16[128,512]{1,0:T(8,128)(2,1)}, u32[]{:S(2)}, u32[]{:S(2)}) collective-permute-start(bf16[128,512]{1,0:T(8,128)(2,1)} %get-tuple-element.118), channel_id=1, source_target_pairs={{8,0},{12,4},{0,8},{4,12},{9,1},{13,5},{1,9},{5,13},{10,2},{14,6},... | collective-permute-start | bytes 393224 | tf_op jit(solution)/shard_map/ppermute | solution.py:289
  90.6 40.1 %all-to-all-start.1 = ((bf16[8,128,512]{2,1,0:T(8,128)(2,1)}), bf16[8,128,512]{2,1,0:T(8,128)(2,1)}, u32[]{:S(2)}, u32[]{:S(2)}) async-start(bf16[8,128,512]{2,1,0:T(8,128)(2,1)} %broadcast_in_dim.95), calls=%async_computation.1 | async-start | bytes 2097152 | tf_op jit(solution)/shard_map/all_to_all | solution.py:297
  127.5 32.0 %collective-permute-start.12 = (bf16[80,512]{1,0:T(8,128)(2,1)}, bf16[80,512]{1,0:T(8,128)(2,1)}, u32[]{:S(2)}, u32[]{:S(2)}) collective-permute-start(bf16[80,512]{1,0:T(8,128)(2,1)} %get-tuple-element.249), channel_id=1, source_target_pairs={{0,12},{4,0},{8,4},{12,8},{1,13},{5,1},{9,5},{13,9},{2,14},{6,2},{... | collective-permute-start | bytes 245768 | tf_op jit(solution)/shard_map/ppermute | solution.py:293
  130.1 30.0 %collective-permute-start.11 = (bf16[80,512]{1,0:T(8,128)(2,1)}, bf16[80,512]{1,0:T(8,128)(2,1)}, u32[]{:S(2)}, u32[]{:S(2)}) collective-permute-start(bf16[80,512]{1,0:T(8,128)(2,1)} %get-tuple-element.250), channel_id=1, source_target_pairs={{0,8},{4,12},{8,0},{12,4},{1,9},{5,13},{9,1},{13,5},{2,10},{6,14},... | collective-permute-start | bytes 245768 | tf_op jit(solution)/shard_map/ppermute | solution.py:293
  130.1 30.0 %collective-permute-start.10 = (bf16[80,512]{1,0:T(8,128)(2,1)}, bf16[80,512]{1,0:T(8,128)(2,1)}, u32[]{:S(2)}, u32[]{:S(2)}) collective-permute-start(bf16[80,512]{1,0:T(8,128)(2,1)} %get-tuple-element.251), channel_id=1, source_target_pairs={{0,4},{4,8},{8,12},{12,0},{1,5},{5,9},{9,13},{13,1},{2,6},{6,10},{... | collective-permute-start | bytes 245768 | tf_op jit(solution)/shard_map/ppermute | solution.py:293
  131.7 34.3 %all-to-all-start.2 = ((bf16[8,128,512]{2,1,0:T(8,128)(2,1)}), bf16[8,128,512]{2,1,0:T(8,128)(2,1)S(1)}, u32[]{:S(2)}, u32[]{:S(2)}) async-start(bf16[8,128,512]{2,1,0:T(8,128)(2,1)} %broadcast_in_dim.96), calls=%async_computation.2 | async-start | bytes 2097152 | tf_op jit(solution)/shard_map/all_to_all | solution.py:297
  156.6 34.7 %collective-permute-start.18 = (bf16[80,512]{1,0:T(8,128)(2,1)}, bf16[80,512]{1,0:T(8,128)(2,1)}, u32[]{:S(2)}, u32[]{:S(2)}) collective-permute-start(bf16[80,512]{1,0:T(8,128)(2,1)} %get-tuple-element.241), channel_id=1, source_target_pairs={{0,12},{4,0},{8,4},{12,8},{1,13},{5,1},{9,5},{13,9},{2,14},{6,2},{... | collective-permute-start | bytes 245768 | tf_op jit(solution)/shard_map/ppermute | solution.py:293
  159.5 35.3 %collective-permute-start.17 = (bf16[80,512]{1,0:T(8,128)(2,1)}, bf16[80,512]{1,0:T(8,128)(2,1)}, u32[]{:S(2)}, u32[]{:S(2)}) collective-permute-start(bf16[80,512]{1,0:T(8,128)(2,1)} %get-tuple-element.242), channel_id=1, source_target_pairs={{0,8},{4,12},{8,0},{12,4},{1,9},{5,13},{9,1},{13,5},{2,10},{6,14},... | collective-permute-start | bytes 245768 | tf_op jit(solution)/shard_map/ppermute | solution.py:293
  159.5 35.3 %collective-permute-start.16 = (bf16[80,512]{1,0:T(8,128)(2,1)}, bf16[80,512]{1,0:T(8,128)(2,1)}, u32[]{:S(2)}, u32[]{:S(2)}) collective-permute-start(bf16[80,512]{1,0:T(8,128)(2,1)} %get-tuple-element.243), channel_id=1, source_target_pairs={{0,4},{4,8},{8,12},{12,0},{1,5},{5,9},{9,13},{13,1},{2,6},{6,10},{... | collective-permute-start | bytes 245768 | tf_op jit(solution)/shard_map/ppermute | solution.py:293
  162.8 36.7 %collective-permute-start.27 = (f32[8,512]{1,0:T(8,128)S(1)}, f32[8,512]{1,0:T(8,128)S(1)}, u32[]{:S(2)}, u32[]{:S(2)}) collective-permute-start(f32[8,512]{1,0:T(8,128)S(1)} %maximum_maximum_fusion), channel_id=1, source_target_pairs={{12,0},{0,4},{4,8},{8,12},{13,1},{1,5},{5,9},{9,13},{14,2},{2,6},{... | collective-permute-start | bytes 49160 | tf_op jit(solution)/shard_map/ppermute | solution.py:289
  164.9 36.2 %collective-permute-start.26 = (f32[8,512]{1,0:T(8,128)S(1)}, f32[8,512]{1,0:T(8,128)S(1)}, u32[]{:S(2)}, u32[]{:S(2)}) collective-permute-start(f32[8,512]{1,0:T(8,128)S(1)} %maximum_maximum_fusion), channel_id=1, source_target_pairs={{8,0},{12,4},{0,8},{4,12},{9,1},{13,5},{1,9},{5,13},{10,2},{14,6},... | collective-permute-start | bytes 49160 | tf_op jit(solution)/shard_map/ppermute | solution.py:289
  167.1 70.4 %all-to-all-start.4 = ((bf16[32,48,768]{2,1,0:T(8,128)(2,1)}), bf16[32,48,768]{2,1,0:T(8,128)(2,1)}, u32[]{:S(2)}, u32[]{:S(2)}) async-start(bf16[32,48,768]{2,1,0:T(8,128)(2,1)} %pad_maximum_fusion), calls=%async_computation.4 | async-start | bytes 4718592 | tf_op jit(solution)/shard_map/all_to_all | solution.py:638
  198.3 27.7 %collective-permute-start.33 = (f32[8,512]{1,0:T(8,128)S(1)}, f32[8,512]{1,0:T(8,128)S(1)}, u32[]{:S(2)}, u32[]{:S(2)}) collective-permute-start(f32[8,512]{1,0:T(8,128)S(1)} %maximum_maximum_fusion.1), channel_id=1, source_target_pairs={{12,0},{0,4},{4,8},{8,12},{13,1},{1,5},{5,9},{9,13},{14,2},{2,6},{... | collective-permute-start | bytes 49160 | tf_op jit(solution)/shard_map/ppermute | solution.py:289
  198.3 27.8 %collective-permute-start.32 = (f32[8,512]{1,0:T(8,128)S(1)}, f32[8,512]{1,0:T(8,128)S(1)}, u32[]{:S(2)}, u32[]{:S(2)}) collective-permute-start(f32[8,512]{1,0:T(8,128)S(1)} %maximum_maximum_fusion.1), channel_id=1, source_target_pairs={{8,0},{12,4},{0,8},{4,12},{9,1},{13,5},{1,9},{5,13},{10,2},{14,6},... | collective-permute-start | bytes 49160 | tf_op jit(solution)/shard_map/ppermute | solution.py:289
  201.1 31.4 %collective-permute-start.24 = (bf16[80,512]{1,0:T(8,128)(2,1)S(1)}, bf16[80,512]{1,0:T(8,128)(2,1)S(1)}, u32[]{:S(2)}, u32[]{:S(2)}) collective-permute-start(bf16[80,512]{1,0:T(8,128)(2,1)S(1)} %get-tuple-element.245), channel_id=1, source_target_pairs={{0,12},{4,0},{8,4},{12,8},{1,13},{5,1},{9,5},{13,9},{2,14},{6,2},{... | collective-permute-start | bytes 245768 | tf_op jit(solution)/shard_map/ppermute | solution.py:293
  201.7 31.8 %collective-permute-start.23 = (bf16[80,512]{1,0:T(8,128)(2,1)S(1)}, bf16[80,512]{1,0:T(8,128)(2,1)S(1)}, u32[]{:S(2)}, u32[]{:S(2)}) collective-permute-start(bf16[80,512]{1,0:T(8,128)(2,1)S(1)} %get-tuple-element.246), channel_id=1, source_target_pairs={{0,8},{4,12},{8,0},{12,4},{1,9},{5,13},{9,1},{13,5},{2,10},{6,14},... | collective-permute-start | bytes 245768 | tf_op jit(solution)/shard_map/ppermute | solution.py:293
  227.8 42.9 %collective-permute-start.30 = (bf16[64,512]{1,0:T(8,128)(2,1)}, bf16[64,512]{1,0:T(8,128)(2,1)}, u32[]{:S(2)}, u32[]{:S(2)}) collective-permute-start(bf16[64,512]{1,0:T(8,128)(2,1)} %get-tuple-element.261), channel_id=1, source_target_pairs={{0,12},{4,0},{8,4},{12,8},{1,13},{5,1},{9,5},{13,9},{2,14},{6,2},{... | collective-permute-start | bytes 196616 | tf_op jit(solution)/shard_map/ppermute | solution.py:293
  230.7 40.0 %collective-permute-start.29 = (bf16[64,512]{1,0:T(8,128)(2,1)}, bf16[64,512]{1,0:T(8,128)(2,1)}, u32[]{:S(2)}, u32[]{:S(2)}) collective-permute-start(bf16[64,512]{1,0:T(8,128)(2,1)} %get-tuple-element.262), channel_id=1, source_target_pairs={{0,8},{4,12},{8,0},{12,4},{1,9},{5,13},{9,1},{13,5},{2,10},{6,14},... | collective-permute-start | bytes 196616 | tf_op jit(solution)/shard_map/ppermute | solution.py:293
  232.5 38.8 %collective-permute-start.28 = (bf16[64,512]{1,0:T(8,128)(2,1)}, bf16[64,512]{1,0:T(8,128)(2,1)}, u32[]{:S(2)}, u32[]{:S(2)}) collective-permute-start(bf16[64,512]{1,0:T(8,128)(2,1)} %get-tuple-element.263), channel_id=1, source_target_pairs={{0,4},{4,8},{8,12},{12,0},{1,5},{5,9},{9,13},{13,1},{2,6},{6,10},{... | collective-permute-start | bytes 196616 | tf_op jit(solution)/shard_map/ppermute | solution.py:293
  234.5 33.6 %collective-permute-start.39 = (f32[8,512]{1,0:T(8,128)S(1)}, f32[8,512]{1,0:T(8,128)S(1)}, u32[]{:S(2)}, u32[]{:S(2)}) collective-permute-start(f32[8,512]{1,0:T(8,128)S(1)} %maximum_maximum_fusion.2), channel_id=1, source_target_pairs={{12,0},{0,4},{4,8},{8,12},{13,1},{1,5},{5,9},{9,13},{14,2},{2,6},{... | collective-permute-start | bytes 49160 | tf_op jit(solution)/shard_map/ppermute | solution.py:289
  235.1 35.2 %collective-permute-start.38 = (f32[8,512]{1,0:T(8,128)S(1)}, f32[8,512]{1,0:T(8,128)}, u32[]{:S(2)}, u32[]{:S(2)}) collective-permute-start(f32[8,512]{1,0:T(8,128)S(1)} %maximum_maximum_fusion.2), channel_id=1, source_target_pairs={{8,0},{12,4},{0,8},{4,12},{9,1},{13,5},{1,9},{5,13},{10,2},{14,6},... | collective-permute-start | bytes 49160 | tf_op jit(solution)/shard_map/ppermute | solution.py:289
  237.5 33.8 %all-to-all-start.3 = ((bf16[8,128,512]{2,1,0:T(8,128)(2,1)}), bf16[8,128,512]{2,1,0:T(8,128)(2,1)S(1)}, u32[]{:S(2)}, u32[]{:S(2)}) async-start(bf16[8,128,512]{2,1,0:T(8,128)(2,1)} %get-tuple-element.147), calls=%async_computation.3 | async-start | bytes 2097152 | tf_op jit(solution)/shard_map/all_to_all | solution.py:301
  244.2 220.6 %all-gather.3.cloned.1.call-start = ((), (), s32[]{:S(2)}) async-start(), calls=%async_computation.9 | async-start | bytes 4792320 | tf_op jit(solution)/shard_map/all_gather | solution.py:656
  354.5 43.7 %all-to-all-start.7 = ((bf16[32,24,896]{2,1,0:T(8,128)(2,1)}), bf16[32,24,896]{2,1,0:T(8,128)(2,1)}, u32[]{:S(2)}, u32[]{:S(2)}) async-start(bf16[32,24,896]{2,1,0:T(8,128)(2,1)} %get-tuple-element.198), calls=%async_computation.7 | async-start | bytes 2752512 | tf_op jit(solution)/shard_map/all_to_all | solution.py:672
  368.0 56.4 %collective-permute-start.43 = (bf16[2,128,1536]{2,1,0:T(8,128)(2,1)}, bf16[2,128,1536]{2,1,0:T(8,128)(2,1)S(1)}, u32[]{:S(2)}, u32[]{:S(2)}) collective-permute-start(bf16[2,128,1536]{2,1,0:T(8,128)(2,1)} %bitcast.73), channel_id=1, source_target_pairs={{0,2},{2,0},{1,3},{3,1},{4,6},{6,4},{5,7},{7,5},{8,10},{10,8},{9,1... | collective-permute-start | bytes 2359304 | tf_op jit(solution)/shard_map/ppermute | solution.py:309
  407.7 31.2 %all-to-all-start.8 = ((bf16[32,24,896]{2,1,0:T(8,128)(2,1)}), bf16[32,24,896]{2,1,0:T(8,128)(2,1)}, u32[]{:S(2)}, u32[]{:S(2)}) async-start(bf16[32,24,896]{2,1,0:T(8,128)(2,1)} %broadcast_in_dim.103), calls=%async_computation.8 | async-start | bytes 2752512 | tf_op jit(solution)/shard_map/all_to_all | solution.py:681
  (92 other events, 900.8 us)
Sparse Core Ops, SparseCore 0:
  277.4 102.2 all-gather.2
